TPU v7x, 32 devices: a whole 2x2x4 slice. The times are simulated.
32 devices in a mesh: dp: 4 (over y, x), expert: 8 (over z, core).
Axes of the slice: x: 2, y: 2, z: 4, core: 2. Of those that a mesh axis runs over, the one named last changes fastest.
Arguments:
- cotangent: bfloat16 [4096, 4096], P(('dp', 'expert')), may hold values from -0.59765625 to 0.59765625
- expert_ids: int32 [4096, 8], P(('dp', 'expert')), may hold values from 0 to 15, all different within a row; in each aligned block of 128 rows (0 to 127, 128 to 255, ...) at most 80 rows name the same one
- gates: bfloat16 [4096, 8], P(('dp', 'expert')), may hold values from 0.019897461 to 0.5
- hidden: bfloat16 [16, 4, 640, 1536], P('expert', 'dp'), may hold values from -6 to 6
- q_prev: bfloat16 [16, 4096, 64], P('expert', 'dp'), may hold values from -0.09375 to 0.09375
Outputs:
- p_merged: float32 [16, 1536, 64], P('expert', 'dp')
- q_next: float32 [16, 4096, 64], P('expert', 'dp')
Inputs may be any that keep to these rules, and one draw needn't show every extreme that they name: `expert_ids`: each row names 8 different experts. Within the 128 rows of one device no expert is named by more than 80 rows, a bound that some block reaches.
All inputs are finite; a program needn't handle non-finite values.
Results may differ from a plain program's by a relative error of at most 0.0056.
Values may be sent and summed in bfloat16 or wider, within the bound.
No kernel may reach another device: no remote copies, remote signals or barrier semaphores. Data moves between devices by JAX's collectives and lax.ppermute only.
A program may use at most 128 MiB of HBM per device.

v0:
```python
import jax
import jax.numpy as jnp
from jax import lax
from jax.sharding import PartitionSpec as P


def slot_positions(expert_ids, experts_all):
    flat_ids = expert_ids.reshape(-1)
    labels = jnp.arange(experts_all, dtype=jnp.int32)
    onehot = (labels[:, None] == flat_ids[None, :]).astype(jnp.bfloat16)
    positions = jnp.arange(flat_ids.shape[0], dtype=jnp.int32)
    upper_mask = (positions[:, None] < positions[None, :]).astype(jnp.bfloat16)
    earlier = jnp.dot(onehot, upper_mask, preferred_element_type=jnp.float32)
    slot_index = jnp.sum(earlier * onehot.astype(jnp.float32), axis=0)
    return slot_index.astype(jnp.int32).reshape(expert_ids.shape)


def selection(target, gate_values, row_total):
    row_labels = jnp.arange(row_total, dtype=jnp.int32)[:, None]
    chooser = jnp.zeros((row_total, target.shape[0]), jnp.bfloat16)
    for column in range(target.shape[1]):
        hit = row_labels == target[:, column][None, :]
        chooser = chooser + jnp.where(
            hit, gate_values[:, column][None, :], jnp.zeros((), jnp.bfloat16)
        )
    return chooser


def whiten(gram_matrix, factor):
    lower_factor = jnp.linalg.cholesky(gram_matrix)

    def solve_one(lower_one, block_rhs):
        return jax.scipy.linalg.solve_triangular(lower_one, block_rhs, lower=True)

    solved = jax.vmap(solve_one)(lower_factor, jnp.swapaxes(factor, 1, 2))
    return jnp.swapaxes(solved, 1, 2).astype(jnp.bfloat16)


def local(cotangent, expert_ids, gates, hidden, q_prev):
    groups = lax.axis_size("expert")
    held_experts = hidden.shape[0]
    capacity = hidden.shape[2] // groups
    experts_all = held_experts * groups
    slot_count = groups * capacity
    model_width = cotangent.shape[1]
    token_count = cotangent.shape[0]
    row_total = held_experts * slot_count
    slot_index = slot_positions(expert_ids, experts_all)
    my_index = lax.axis_index("expert")
    piece_rows = lax.all_gather(cotangent, "expert", axis=0, tiled=True)
    piece_ids = lax.all_gather(expert_ids, "expert", axis=0, tiled=True)
    piece_gates = lax.all_gather(gates, "expert", axis=0, tiled=True)
    piece_slots = lax.all_gather(slot_index, "expert", axis=0, tiled=True)
    row_count = piece_rows.shape[0]
    source = jnp.arange(row_count, dtype=jnp.int32) // token_count
    is_owned = piece_ids // held_experts == my_index
    target = jnp.where(
        is_owned,
        piece_ids % held_experts * slot_count + source[:, None] * capacity + piece_slots,
        row_total,
    )
    chooser = selection(target, piece_gates, row_total)
    row_values = jnp.dot(chooser, piece_rows, preferred_element_type=jnp.float32)
    dispatched = row_values.astype(jnp.bfloat16).reshape(held_experts, slot_count, model_width)
    whole_factor = lax.all_gather(q_prev, "dp", axis=1, tiled=True)
    projected = jnp.einsum(
        "esd,edr->esr", dispatched, whole_factor, preferred_element_type=jnp.float32
    ).astype(jnp.bfloat16)
    own_hidden = hidden[:, 0]
    partial_value = jnp.einsum(
        "esf,esr->efr", own_hidden, projected, preferred_element_type=jnp.float32
    )
    members = lax.axis_size("dp")
    dp_index = lax.axis_index("dp")
    hidden_width = own_hidden.shape[2]
    share_rows = hidden_width // members
    merged = lax.psum(partial_value, "dp")
    gram_matrix = jnp.einsum("efr,efs->ers", merged, merged, precision=lax.Precision.HIGHEST)
    basis_rows = whiten(gram_matrix, merged)
    p_share = lax.dynamic_slice_in_dim(merged, dp_index * share_rows, share_rows, 1)
    mapped = jnp.einsum(
        "esf,efr->esr", own_hidden, basis_rows, preferred_element_type=jnp.float32
    ).astype(jnp.bfloat16)
    width_rows = model_width // members
    q_part = jnp.einsum("esd,esr->edr", dispatched, mapped, preferred_element_type=jnp.float32)
    q_summed = lax.psum(q_part, "dp")
    q_share = lax.dynamic_slice_in_dim(q_summed, dp_index * width_rows, width_rows, 1)
    return (p_share, q_share)


def solution(mesh):
    placed = (
        P(("dp", "expert"), None),
        P(("dp", "expert"), None),
        P(("dp", "expert"), None),
        P("expert", "dp", None, None),
        P("expert", "dp", None),
    )
    return jax.shard_map(
        local,
        mesh=mesh,
        in_specs=placed,
        out_specs=(P("expert", "dp", None), P("expert", "dp", None)),
        check_vma=False,
    )
```

profile of v0, /device:TPU:0, one launch (start us, length us, event | category | flops | bytes accessed | tf_op | source)
XLA Modules:
  0.0 299.4 jit_solution(17109533313557334668)
XLA Ops:
  7.2 0.0 all-gather.3.cloned.1.call-start
  7.2 0.7 all-gather.3.cloned.1.call-update
  7.9 0.0 all-gather.5.cloned.1.call-start
  8.0 0.7 all-gather.5.cloned.1.call-update
  8.7 0.0 all-reduce.3.cloned.1.call-start
  8.7 0.8 copy.15
  9.5 0.1 eq.147
  9.6 16.7 %all_gather.15 = s32[1024,8]{1,0:T(8,128)S(1)} all-gather(s32[128,8]{1,0:T(8,128)S(1)} %copy.15), channel_id=1, replica_groups=mesh['dp'=4,'expert'=8] {'expert'}, dimensions={0}, use_global_device_ids=true | all-gather | bytes 36864 | tf_op jit(solution)/shard_map/all_gather | solution.py:51
  26.3 0.3 fusion.52
  26.7 0.1 convert_element_type.30
  26.8 18.7 %all_gather.16 = s32[1024,8]{1,0:T(8,128)S(1)} all-gather(s32[128,8]{1,0:T(8,128)S(1)} %convert_element_type.30), channel_id=1, replica_groups=mesh['dp'=4,'expert'=8] {'expert'}, dimensions={0}, use_global_device_ids=true | all-gather | bytes 36864 | tf_op jit(solution)/shard_map/all_gather | solution.py:53
  45.5 0.5 fusion.60
  46.0 2.1 slice_reduce_fusion.7
  48.1 13.0 %all_gather.17 = bf16[1024,8]{0,1:T(8,128)(2,1)S(1)} all-gather(bf16[128,8]{0,1:T(8,128)(2,1)S(1)} %copy-done), channel_id=1, replica_groups=mesh['dp'=4,'expert'=8] {'expert'}, dimensions={0}, use_global_device_ids=true | all-gather | bytes 18432 | tf_op jit(solution)/shard_map/all_gather | solution.py:52
  61.1 0.1 slice_reduce_fusion.15
  61.2 37.9 %all-gather.3.cloned.1.call-done = bf16[1024,4096]{1,0:T(8,128)(2,1)} async-done(((bf16[128,4096]{1,0:T(8,128)(2,1)}), bf16[1024,4096]{1,0:T(8,128)(2,1)}) %all-gather.3.cloned.1.call-update) | async-done | bytes 8388624 | tf_op jit(solution)/shard_map/all_gather | solution.py:50
  99.1 20.5 %convolution_convert_fusion = bf16[1280,4096]{1,0:T(8,128)(2,1)} fusion(bf16[1024,4096]{1,0:T(8,128)(2,1)} %all-gather.3.cloned.1.call-done, s32[1024]{0:T(1024)S(1)} %get-tuple-element.3, s32[1024]{0:T(1024)S(1)} %get-tuple-element.4, s32[1024]{0:T(1024)S(1)} %get-tuple-element.5, s32[1024]{0:T(1024)S(1)} %get-tuple-element.6, ...), kind=kOutput, calls=%fused_computation | convolution fusion | flops 10784604160 | bytes 18923520 | tf_op jit(solution)/shard_map/dot_general | solution.py:63
  119.7 6.5 %all-gather.5.cloned.1.call-done = bf16[2,4096,64]{1,2,0:T(8,128)(2,1)} async-done(((bf16[2,1024,64]{1,2,0:T(8,128)(2,1)}), bf16[2,4096,64]{1,2,0:T(8,128)(2,1)}) %all-gather.5.cloned.1.call-update) | async-done | bytes 1048592 | tf_op jit(solution)/shard_map/all_gather | solution.py:65
  126.2 10.3 %fusion.36 = f32[2,1536,64]{1,2,0:T(8,128)} fusion(bf16[2,1,640,1536]{3,2,1,0:T(8,128)(2,1)} %param.8, bf16[2,640,4096]{2,1,0:T(8,128)(2,1)} %bitcast.31, bf16[2,4096,64]{1,2,0:T(8,128)(2,1)} %all-gather.5.cloned.1.call-done), kind=kOutput, calls=%fused_computation.38 | convolution fusion | flops 922828800 | bytes 16252928 | tf_op jit(solution)/shard_map/esf,esr->efr/dot_general | solution.py:70
  136.5 0.2 all-reduce.5.cloned.1.call-start
  136.8 48.6 %all-reduce.3.cloned.1.call-done = f32[2,1536,64]{1,2,0:T(8,128)} async-done(((f32[2,1536,64]{1,2,0:T(8,128)}), f32[2,1536,64]{1,2,0:T(8,128)}) %all-reduce.3.cloned.1.call-update) | async-done | bytes 786448 | tf_op jit(solution)/shard_map/psum | solution.py:77
  185.4 2.2 fusion.72
  187.6 0.1 copy.17
  187.7 11.7 %custom-call.8 = f32[2,64,64]{2,1,0:T(8,128)S(1)} custom-call(f32[2,64,64]{2,1,0:T(8,128)S(1)} %fusion.64), custom_call_target="Cholesky" | custom-call | tf_op jit(solution)/shard_map/jit(cholesky)/cholesky | solution.py:30
  199.5 0.1 compare_reduce_fusion
  199.6 0.1 select_bitcast_fusion
  199.7 9.8 %custom-call.9 = f32[2,1,64,64]{2,3,1,0:T(8,128)S(1)} custom-call(f32[2,1,64,64]{3,2,1,0:T(8,128)S(1)} %select_bitcast_fusion), custom_call_target="InvertDiagBlocksLowerTriangular" | custom-call | tf_op jit(solution)/shard_map/vmap(jit(_solve_triangular))/triangular_solve | solution.py:33
  209.5 2.0 convolution_convert_fusion.1
  211.5 9.6 %fusion.54 = f32[2,4096,64]{1,2,0:T(8,128)} fusion(bf16[2,640,4096]{2,1,0:T(8,128)(2,1)} %bitcast.32, bf16[2,1536,64]{1,2,0:T(8,128)(2,1)S(1)} %convolution_convert_fusion.1, bf16[2,1,640,1536]{3,2,1,0:T(8,128)(2,1)} %param.8), kind=kOutput, calls=%fused_computation.53 | convolution fusion | flops 922828800 | bytes 16908288 | tf_op jit(solution)/shard_map/esd,esr->edr/dot_general | solution.py:85
  221.2 1.6 constant_dynamic-slice_fusion.1
  222.8 68.2 %all-reduce.5.cloned.1.call-done = f32[2,4096,64]{1,2,0:T(8,128)} async-done(((f32[2,4096,64]{1,2,0:T(8,128)}), f32[2,4096,64]{1,2,0:T(8,128)}) %all-reduce.5.cloned.1.call-update) | async-done | bytes 2097168 | tf_op jit(solution)/shard_map/psum | solution.py:86
  291.0 1.9 constant_dynamic-slice_fusion
  (10 shorter events, 0.1 us)
Async XLA Ops:
  7.2 41.0 %copy-start = (bf16[128,8]{0,1:T(8,128)(2,1)S(1)}, bf16[128,8]{0,1:T(8,128)(2,1)}, u32[]{:S(2)}) copy-start(bf16[128,8]{0,1:T(8,128)(2,1)} %param.7) | copy-start | bytes 6148
  7.2 92.0 %all-gather.3.cloned.1.call-start = ((), (), s32[]{:S(2)}) async-start(), calls=%async_computation | async-start | bytes 9437184 | tf_op jit(solution)/shard_map/all_gather | solution.py:50
  7.9 118.2 %all-gather.5.cloned.1.call-start = ((), (), s32[]{:S(2)}) async-start(), calls=%async_computation.1 | async-start | bytes 1310720 | tf_op jit(solution)/shard_map/all_gather | solution.py:65
  8.7 176.7 %all-reduce.3.cloned.1.call-start = ((), (), s32[]{:S(2)}) async-start(), calls=%async_computation.2 | async-start | bytes 1572864 | tf_op jit(solution)/shard_map/psum | solution.py:77
  136.5 154.5 %all-reduce.5.cloned.1.call-start = ((), (), s32[]{:S(2)}) async-start(), calls=%async_computation.3 | async-start | bytes 4194304 | tf_op jit(solution)/shard_map/psum | solution.py:86
Sparse Core Ops, SparseCore 0:
  9.6 89.4 all-gather.2
  101.0 25.1 all-gather.4
  136.6 48.7 all-reduce.2
  221.3 69.6 all-reduce.4
where the time goes:
time: 300 us; the launch traced here: 299 us
  waiting for transfers between devices  163 us (54%)
  blocking collectives  48.4 us (16%)
  matrix products  45 us (15%)
  other arithmetic  22.4 us (7%)
  between operations  13.9 us (5%)
  local copies, waits for them, and re-layouts  6.76 us (2%)
    psum x1, waiting for transfers between devices, local(): q_summed = lax.psum(q_part, 'dp')  68.2 us
    psum x1, waiting for transfers between devices, local(): merged = lax.psum(partial_value, 'dp')  48.6 us
    all_gather x1, waiting for transfers between devices, local(): piece_rows = lax.all_gather(cotangent, 'expert', axis=0, tiled=True)  37.9 us
    dot_general x1, matrix products, local(): jnp.dot(chooser, piece_rows, preferred_element_type=jnp.float32)  20.5 us
    all_gather x1, blocking collectives, local(): piece_slots = lax.all_gather(slot_index, 'expert', axis=0, tiled=True)  18.7 us
    all_gather x1, blocking collectives, local(): piece_ids = lax.all_gather(expert_ids, 'expert', axis=0, tiled=True)  16.7 us
    all_gather x1, blocking collectives, local(): piece_gates = lax.all_gather(gates, 'expert', axis=0, tiled=True)  13 us
    another operation x4, other arithmetic, whiten(): lower_factor = jnp.linalg.cholesky(gram_matrix)  11.9 us
  transfers between devices with their start and end apart: 4, of which 4 were waited for; matrix products, arithmetic and copies ran while one was open for 9% of the time, Pallas kernels for 0%

commit v1 on v0

v1 whole, which is shorter than its diff:
```python
import jax
import jax.numpy as jnp
from jax import lax
from jax.sharding import PartitionSpec as P

CORES = 2


def exchange(value, axis, distance):
    size = lax.axis_size(axis)
    return lax.ppermute(value, axis, [(i, i ^ distance) for i in range(size)])


def dense_gates(expert_ids, gates, experts_all):
    labels = jnp.arange(experts_all, dtype=jnp.int32)[:, None]
    dense = jnp.zeros((experts_all, expert_ids.shape[0]), jnp.bfloat16)
    for column in range(expert_ids.shape[1]):
        hit = labels == expert_ids[:, column][None, :]
        dense = dense + jnp.where(hit, gates[:, column][None, :], jnp.zeros((), jnp.bfloat16))
    return dense


def slot_choice(dense, capacity):
    tokens = dense.shape[-1]
    named = (dense > 0).astype(jnp.bfloat16)
    position = jnp.arange(tokens, dtype=jnp.int32)
    before = (position[:, None] < position[None, :]).astype(jnp.bfloat16)
    slot = jnp.einsum("...t,tu->...u", named, before, preferred_element_type=jnp.float32)
    slot = jnp.where(dense > 0, slot, -1.0).astype(jnp.int32)
    return slot[..., None, :] == jnp.arange(capacity, dtype=jnp.int32)[:, None]


def sum_over_dp(value):
    half = value.shape[-1] // 2
    distances = []
    step = 1
    while step < lax.axis_size("dp"):
        distances.append(step)
        step *= 2
    parts = [value[..., :half], value[..., half:]]
    for index in range(len(distances)):
        sent = []
        for part, order in zip(parts, (distances, distances[::-1])):
            rounded = part.astype(jnp.bfloat16)
            got = exchange(rounded, "dp", order[index])
            sent.append(rounded.astype(jnp.float32) + got.astype(jnp.float32))
        parts = sent
    return jnp.concatenate(parts, axis=-1)


def local(cotangent, expert_ids, gates, hidden, q_prev):
    members = lax.axis_size("dp")
    places = lax.axis_size("expert")
    chips = places // CORES
    held, _, slots, width = hidden.shape
    rank = q_prev.shape[2]
    tokens, model_width = cotangent.shape
    experts_all = held * places
    capacity = slots // places
    part = model_width // members
    my_dp = lax.axis_index("dp")
    my_place = lax.axis_index("expert")
    my_chip, my_core = my_place // CORES, my_place % CORES
    own_hidden = hidden[:, 0]

    dense = dense_gates(expert_ids, gates, experts_all)
    dense_pair = jnp.stack([dense, exchange(dense, "expert", 1)])

    factor = jnp.swapaxes(q_prev, 1, 2).reshape(held * rank, part)
    factors = [factor] + [exchange(factor, "expert", CORES * k) for k in range(1, chips)]

    columns = []
    for k in range(members):
        piece = lax.dynamic_slice_in_dim(cotangent, (my_dp ^ k) * part, part, 1)
        columns.append(exchange(piece, "dp", k) if k else piece)
    columns = jnp.stack(columns)
    columns_pair = jnp.stack([columns, exchange(columns, "expert", 1)])

    dense_groups = jnp.stack([dense] + [exchange(dense, "dp", k) for k in range(1, members)])
    gathered_gates = lax.all_gather(dense_groups, "expert", axis=1)
    gathered = lax.all_gather(columns, "expert", axis=1)

    flat_pair = columns_pair.reshape(-1, part)
    arrived = []
    for k in range(chips):
        y = lax.dot_general(
            flat_pair, factors[k], (((1,), (1,)), ((), ())), preferred_element_type=jnp.float32
        )
        y = y.astype(jnp.bfloat16).reshape(CORES, members, tokens, held * rank)
        total = y[:, 0].astype(jnp.float32)
        for d in range(1, members):
            total = total + exchange(y[:, d], "dp", d).astype(jnp.float32)
        owner = (my_chip ^ k) * CORES + my_core
        mine = lax.dynamic_slice_in_dim(dense_pair, owner * held, held, 1)
        weighted = total.reshape(CORES, tokens, held, rank) * jnp.swapaxes(mine, 1, 2).astype(
            jnp.float32
        )[..., None]
        choice = slot_choice(mine, capacity).astype(jnp.bfloat16)
        packed = jnp.einsum(
            "phct,pthr->pchr",
            choice,
            weighted.astype(jnp.bfloat16),
            preferred_element_type=jnp.float32,
        ).astype(jnp.bfloat16)
        packed = packed.reshape(CORES, capacity, held * rank)
        arrived.append(exchange(packed, "expert", CORES * k) if k else packed)
    arrived = jnp.stack(arrived)
    arrived = jnp.take(arrived, jnp.arange(chips) ^ my_chip, axis=0)
    arrived = jnp.take(arrived, jnp.arange(CORES) ^ my_core, axis=1)
    projected = arrived.reshape(slots, held, rank)

    partial_value = jnp.einsum(
        "shr,hsf->hrf", projected, own_hidden, preferred_element_type=jnp.float32
    )
    merged = sum_over_dp(partial_value)
    gram = jnp.einsum("hrf,hsf->hrs", merged, merged, precision=lax.Precision.HIGHEST)
    lower = jnp.linalg.cholesky(gram)
    basis = jax.vmap(
        lambda one, rhs: jax.scipy.linalg.solve_triangular(one, rhs, lower=True)
    )(lower, merged).astype(jnp.bfloat16)
    mapped = jnp.einsum(
        "hsf,hrf->shr", own_hidden, basis, preferred_element_type=jnp.float32
    ).astype(jnp.bfloat16)
    mapped = mapped.reshape(slots, held * rank)
    mapped_groups = jnp.stack([mapped] + [exchange(mapped, "dp", k) for k in range(1, members)])

    own_gates = lax.dynamic_slice_in_dim(gathered_gates, my_place * held, held, 2)
    choice = jnp.where(
        slot_choice(own_gates, capacity), own_gates[..., None, :], jnp.zeros((), jnp.bfloat16)
    )
    dispatched = jnp.einsum(
        "gphct,gptd->hgpcd", choice, gathered, preferred_element_type=jnp.float32
    ).astype(jnp.bfloat16)
    q_next = jnp.einsum(
        "gshr,hgsd->hrd",
        mapped_groups.reshape(members, slots, held, rank),
        dispatched.reshape(held, members, slots, part),
        preferred_element_type=jnp.float32,
    )
    share = width // members
    p_share = lax.dynamic_slice_in_dim(merged, my_dp * share, share, 2)
    return (jnp.swapaxes(p_share, 1, 2), jnp.swapaxes(q_next, 1, 2))


def solution(mesh):
    placed = (
        P(("dp", "expert"), None),
        P(("dp", "expert"), None),
        P(("dp", "expert"), None),
        P("expert", "dp", None, None),
        P("expert", "dp", None),
    )
    return jax.shard_map(
        local,
        mesh=mesh,
        in_specs=placed,
        out_specs=(P("expert", "dp", None), P("expert", "dp", None)),
        check_vma=False,
    )
```

time: 300 us -> 208 us (0.69)
  waiting for transfers between devices: 163 us -> 79.5 us
  blocking collectives: 48.4 us -> 14.3 us
  starting transfers between devices: 0.34 us -> 33 us
  matrix products: 45 us -> 27.9 us
  local copies, waits for them, and re-layouts: 6.76 us -> 14.2 us
    psum x2 -> x0, waiting for transfers between devices: 117 us -> none  [the longest x1 68.2 us: local(): q_summed = lax.psum(q_part, 'dp')]
    ppermute x0 -> x33, waiting for transfers between devices: none -> 79.5 us  [exchange(): return lax.ppermute(value, axis, [(i, i ^ distance) for i in range(size)])]
    all_gather x2 -> x1, waiting for transfers between devices: 44.4 us -> 0.01 us  [local(): gathered = lax.all_gather(columns, 'expert', axis=1)]
    all_gather x3 -> x1, blocking collectives: 48.4 us -> 14.3 us  [local(): gathered_gates = lax.all_gather(dense_groups, 'expert', axis=1)]
    ppermute x0 -> x33, starting transfers between devices: none -> 33 us  [exchange(): return lax.ppermute(value, axis, [(i, i ^ distance) for i in range(size)])]
    dot_general x5 -> x18, matrix products: 43.1 us -> 27 us  [the longest x1 8.91 us: local(): jnp.einsum('gphct,gptd->hgpcd', choice, gathered, preferred_element_type=...]
    convert_element_type x1 -> x2, local copies, waits for them, and re-layouts: 0.08 us -> 10.1 us  [the longest x1 10.1 us: local(): dispatched = jnp.einsum('gphct,gptd->hgpcd', choice, gathered, preferred_...]
    dynamic_slice x2 -> x1, local copies, waits for them, and re-layouts: 3.51 us -> 0.02 us  [local(): lax.dynamic_slice_in_dim(gathered_gates, my_place * held, held, 2)]
  transfers between devices with their start and end apart: 4 -> 34, of which waited for: 4 -> 17; matrix products, arithmetic and copies ran while one was open for 9% -> 28% of each run, Pallas kernels for 0% -> 0%
where the time goes in v1:
time: 208 us
  waiting for transfers between devices  79.5 us (38%)
  starting transfers between devices  33 us (16%)
  matrix products  27.9 us (13%)
  other arithmetic  24.4 us (12%)
  between operations  14.5 us (7%)
  blocking collectives  14.3 us (7%)
  local copies, waits for them, and re-layouts  14.2 us (7%)
    ppermute x33, waiting for transfers between devices, exchange(): return lax.ppermute(value, axis, [(i, i ^ distance) for i in range(size)])  79.5 us
    ppermute x33, starting transfers between devices, exchange(): return lax.ppermute(value, axis, [(i, i ^ distance) for i in range(size)])  33 us
    all_gather x1, blocking collectives, local(): gathered_gates = lax.all_gather(dense_groups, 'expert', axis=1)  14.3 us
    another operation x4, other arithmetic, local(): lower = jnp.linalg.cholesky(gram)  11.9 us
    convert_element_type x1, local copies, waits for them, and re-layouts, local(): dispatched = jnp.einsum('gphct,gptd->hgpcd', choice, gathered, preferred_...  10.1 us
    another operation x3, other arithmetic, local(): jax.scipy.linalg.solve_triangular(one, rhs, lower=True)  9.92 us
    dot_general x1, matrix products, local(): jnp.einsum('gphct,gptd->hgpcd', choice, gathered, preferred_element_type=...  8.91 us
    dot_general x1, matrix products, local(): jnp.einsum('gshr,hgsd->hrd', mapped_groups.reshape(members, slots, held,...  6.71 us
  transfers between devices with their start and end apart: 34, of which 17 were waited for; matrix products, arithmetic and copies ran while one was open for 28% of the time, Pallas kernels for 0%

profile of v1, /device:TPU:0, one launch (start us, length us, event | category | flops | bytes accessed | tf_op | source)
XLA Modules:
  0.0 207.9 jit_solution(623754268837195455)
XLA Ops:
  7.2 1.3 dynamic-slice_bitcast_fusion
  8.6 3.0 %collective-permute-start = (bf16[128,1024]{1,0:T(8,128)(2,1)S(1)}, bf16[128,1024]{1,0:T(8,128)(2,1)S(1)}, u32[]{:S(2)}, u32[]{:S(2)}) collective-permute-start(bf16[128,1024]{1,0:T(8,128)(2,1)S(1)} %get-tuple-element.13), channel_id=1, source_target_pairs={{0,8},{8,0},{16,24},{24,16},{1,9},{9,1},{17,25},{25,17},{2,10},{10... | collective-permute-start | bytes 786440 | tf_op jit(solution)/shard_map/ppermute | solution.py:11
  11.6 1.5 collective-permute-start.2
  13.1 5.6 %collective-permute-done = bf16[128,1024]{1,0:T(8,128)(2,1)S(1)} collective-permute-done((bf16[128,1024]{1,0:T(8,128)(2,1)S(1)}, bf16[128,1024]{1,0:T(8,128)(2,1)S(1)}, u32[]{:S(2)}, u32[]{:S(2)}) %collective-permute-start) | collective-permute-done | bytes 262176 | tf_op jit(solution)/shard_map/ppermute | solution.py:11
  18.7 6.1 %collective-permute-done.2 = bf16[128,1024]{1,0:T(8,128)(2,1)S(1)} collective-permute-done((bf16[128,1024]{1,0:T(8,128)(2,1)S(1)}, bf16[128,1024]{1,0:T(8,128)(2,1)S(1)}, u32[]{:S(2)}, u32[]{:S(2)}) %collective-permute-start.2) | collective-permute-done | bytes 262176 | tf_op jit(solution)/shard_map/ppermute | solution.py:11
  24.8 1.4 collective-permute-done.1
  27.4 1.5 collective-permute-start.29
  28.9 1.5 collective-permute-start.28
  30.4 3.6 %collective-permute-start.18 = (bf16[128,1024]{1,0:T(8,128)(2,1)S(1)}, bf16[128,1024]{1,0:T(8,128)(2,1)S(1)}, u32[]{:S(2)}, u32[]{:S(2)}) collective-permute-start(bf16[128,1024]{1,0:T(8,128)(2,1)S(1)} %bitcast.236), channel_id=1, source_target_pairs={{0,6},{1,7},{2,4},{3,5},{4,2},{5,3},{6,0},{7,1},{8,14},{9,15},{10,... | collective-permute-start | bytes 786440 | tf_op jit(solution)/shard_map/ppermute | solution.py:11
  35.3 1.8 collective-permute-done.3
  37.3 19.2 %collective-permute-done.8 = bf16[128,1024]{1,0:T(8,128)(2,1)S(1)} collective-permute-done((bf16[128,1024]{1,0:T(8,128)(2,1)S(1)}, bf16[128,1024]{1,0:T(8,128)(2,1)S(1)}, u32[]{:S(2)}, u32[]{:S(2)}) %collective-permute-start.8) | collective-permute-done | bytes 262176 | tf_op jit(solution)/shard_map/ppermute | solution.py:11
  58.5 26.3 %collective-permute-done.13 = bf16[128,1024]{1,0:T(8,128)(2,1)S(1)} collective-permute-done((bf16[128,1024]{1,0:T(8,128)(2,1)S(1)}, bf16[128,1024]{1,0:T(8,128)(2,1)S(1)}, u32[]{:S(2)}, u32[]{:S(2)}) %collective-permute-start.13) | collective-permute-done | bytes 262176 | tf_op jit(solution)/shard_map/ppermute | solution.py:11
  85.5 1.8 collective-permute-start.10
  88.0 1.9 collective-permute-start.14
  92.4 1.9 collective-permute-start.4
  94.3 1.5 collective-permute-done.16
  97.3 2.3 %collective-permute-start.19 = (bf16[2,128,128]{2,1,0:T(8,128)(2,1)S(1)}, bf16[2,128,128]{2,1,0:T(8,128)(2,1)S(1)}, u32[]{:S(2)}, u32[]{:S(2)}) collective-permute-start(bf16[2,128,128]{2,1,0:T(8,128)(2,1)S(1)} %get-tuple-element.29), channel_id=1, source_target_pairs={{0,8},{8,0},{16,24},{24,16},{1,9},{9,1},{17,25},{25,17},{2,10},{10... | collective-permute-start | bytes 196616 | tf_op jit(solution)/shard_map/ppermute | solution.py:11
  99.6 1.4 collective-permute-done.6
  103.4 2.8 %collective-permute-done.21 = bf16[2,128,128]{2,1,0:T(8,128)(2,1)S(1)} collective-permute-done((bf16[2,128,128]{2,1,0:T(8,128)(2,1)S(1)}, bf16[2,128,128]{2,1,0:T(8,128)(2,1)S(1)}, u32[]{:S(2)}, u32[]{:S(2)}) %collective-permute-start.21) | collective-permute-done | bytes 65568 | tf_op jit(solution)/shard_map/ppermute | solution.py:11
  108.6 2.3 %collective-permute-done.12 = bf16[2,80,128]{2,1,0:T(8,128)(2,1)S(1)} collective-permute-done((bf16[2,80,128]{2,1,0:T(8,128)(2,1)S(1)}, bf16[2,80,128]{2,1,0:T(8,128)(2,1)S(1)}, u32[]{:S(2)}, u32[]{:S(2)}) %collective-permute-start.12) | collective-permute-done | bytes 40992 | tf_op jit(solution)/shard_map/ppermute | solution.py:11
  111.7 3.5 %collective-permute-done.17 = bf16[2,80,128]{2,1,0:T(8,128)(2,1)S(1)} collective-permute-done((bf16[2,80,128]{2,1,0:T(8,128)(2,1)S(1)}, bf16[2,80,128]{2,1,0:T(8,128)(2,1)S(1)}, u32[]{:S(2)}, u32[]{:S(2)}) %collective-permute-start.17) | collective-permute-done | bytes 40992 | tf_op jit(solution)/shard_map/ppermute | solution.py:11
  116.9 3.0 %fusion.5 = bf16[2,64,1536]{2,1,0:T(8,128)(2,1)S(1)} fusion(bf16[2,1,640,1536]{3,2,1,0:T(8,128)(2,1)} %param.8, bf16[640,2,64]{0,2,1:T(8,128)(2,1)S(1)} %gather.12, pred[640]{0:T(1024)(128)(4,1)S(1)} %broadcast_in_dim.161), kind=kOutput, calls=%fused_computation.9 | convolution fusion | flops 251936768 | bytes 4489856 | tf_op jit(solution)/shard_map/shr,hsf->hrf/dot_general | solution.py:112
  121.2 14.3 %all-gather.1 = bf16[4,128,128]{2,1,0:T(8,128)(2,1)S(1)} all-gather(bf16[4,16,128]{2,1,0:T(8,128)(2,1)S(1)} %pad_maximum_fusion.7), channel_id=3, replica_groups=mesh['dp'=4,'expert'=8] {'expert'}, dimensions={1}, use_global_device_ids=true | all-gather | bytes 147456 | tf_op jit(solution)/shard_map/all_gather | solution.py:80
  137.0 1.7 collective-permute-start.24
  138.7 4.2 %collective-permute-done.26 = bf16[2,64,768]{2,1,0:T(8,128)(2,1)S(1)} collective-permute-done((bf16[2,64,768]{2,1,0:T(8,128)(2,1)S(1)}, bf16[2,64,768]{2,1,0:T(8,128)(2,1)S(1)}, u32[]{:S(2)}, u32[]{:S(2)}) %collective-permute-start.26) | collective-permute-done | bytes 196640 | tf_op jit(solution)/shard_map/ppermute | solution.py:11
  144.9 11.7 %custom-call.8 = f32[2,64,64]{2,1,0:T(8,128)S(1)} custom-call(f32[2,64,64]{2,1,0:T(8,128)S(1)} %fusion.40), custom_call_target="Cholesky" | custom-call | tf_op jit(solution)/shard_map/jit(cholesky)/cholesky | solution.py:117
  156.9 9.8 %custom-call.9 = f32[2,1,64,64]{2,3,1,0:T(8,128)S(1)} custom-call(f32[2,1,64,64]{3,2,1,0:T(8,128)S(1)} %select_bitcast_fusion), custom_call_target="InvertDiagBlocksLowerTriangular" | custom-call | tf_op jit(solution)/shard_map/vmap(jit(_solve_triangular))/triangular_solve | solution.py:119
  167.6 3.4 %fusion.10 = bf16[2,64,640]{2,1,0:T(8,128)(2,1)S(1)} fusion(bf16[2,64,1536]{2,1,0:T(8,128)(2,1)S(1)} %convolution_convert_fusion, bf16[2,1,640,1536]{3,2,1,0:T(8,128)(2,1)} %param.8), kind=kOutput, calls=%fused_computation.18 | convolution fusion | flops 251740160 | bytes 4489216 | tf_op jit(solution)/shard_map/hsf,hrf->shr/dot_general | solution.py:121
  171.0 1.4 collective-permute-start.32
  175.3 8.9 %convert_bitcast_fusion = bf16[2,4,8,80,1024]{4,3,0,2,1:T(8,128)(2,1)} fusion(bf16[4,8,128,1024,1]{3,2,4,1,0:T(8,128)(2,1)} %bitcast.221, s32[4,8,2,128]{3,2,1,0:T(2,128)S(1)} %copy.119, bf16[4,8,2,128]{3,2,1,0:T(2,128)(2,1)S(1)} %constant_dynamic-slice_fusion), kind=kOutput, calls=%fused_computation.2 | convolution fusion | flops 1348730880 | bytes 18923520 | tf_op jit(solution)/shard_map/gphct,gptd->hgpcd/dot_general | solution.py:131
  184.2 10.1 %copy.121 = bf16[2,4,8,80,1024]{4,3,2,1,0:T(8,128)(2,1)} copy(bf16[2,4,8,80,1024]{4,3,0,2,1:T(8,128)(2,1)} %convert_bitcast_fusion) | data formatting | bytes 20971520 | tf_op jit(solution)/shard_map/convert_element_type | solution.py:133
  194.3 6.7 %convolution_bitcast_fusion = f32[2,1024,64]{1,2,0:T(8,128)} fusion(bf16[2,4,640,1024]{3,2,1,0:T(8,128)(2,1)} %bitcast.220, bf16[1,640,2,64]{1,3,2,0:T(8,128)(2,1)S(1)} %bitcast.259, bf16[1,640,2,64]{1,3,2,0:T(8,128)(2,1)S(1)} %bitcast.260, bf16[1,640,2,64]{1,3,2,0:T(8,128)(2,1)S(1)} %bitcast.261, bf16[1,640,2,64]{1,3,2,0:T(8,128)(2,1)S(1)} %bitcast.251), kind=kOutput, calls=%fused_computation.13 | convolution fusion | flops 672071680 | bytes 11665408 | tf_op jit(solution)/shard_map/gshr,hgsd->hrd/dot_general | solution.py:134
  (119 shorter events, 26.1 us)
Async XLA Ops:
  7.2 168.1 %all-gather.4.cloned.1.call-start = ((), (), s32[]{:S(2)}) async-start(), calls=%async_computation | async-start | bytes 9437184 | tf_op jit(solution)/shard_map/all_gather | solution.py:81
  8.6 10.1 %collective-permute-start = (bf16[128,1024]{1,0:T(8,128)(2,1)S(1)}, bf16[128,1024]{1,0:T(8,128)(2,1)S(1)}, u32[]{:S(2)}, u32[]{:S(2)}) collective-permute-start(bf16[128,1024]{1,0:T(8,128)(2,1)S(1)} %get-tuple-element.13), channel_id=1, source_target_pairs={{0,8},{8,0},{16,24},{24,16},{1,9},{9,1},{17,25},{25,17},{2,10},{10... | collective-permute-start | bytes 786440 | tf_op jit(solution)/shard_map/ppermute | solution.py:11
  11.6 13.2 %collective-permute-start.2 = (bf16[128,1024]{1,0:T(8,128)(2,1)S(1)}, bf16[128,1024]{1,0:T(8,128)(2,1)S(1)}, u32[]{:S(2)}, u32[]{:S(2)}) collective-permute-start(bf16[128,1024]{1,0:T(8,128)(2,1)S(1)} %get-tuple-element.14), channel_id=1, source_target_pairs={{0,24},{8,16},{16,8},{24,0},{1,25},{9,17},{17,9},{25,1},{2,26},{10... | collective-permute-start | bytes 786440 | tf_op jit(solution)/shard_map/ppermute | solution.py:11
  13.0 13.1 %collective-permute-start.1 = (bf16[128,1024]{1,0:T(8,128)(2,1)S(1)}, bf16[128,1024]{1,0:T(8,128)(2,1)S(1)}, u32[]{:S(2)}, u32[]{:S(2)}) collective-permute-start(bf16[128,1024]{1,0:T(8,128)(2,1)S(1)} %get-tuple-element.15), channel_id=1, source_target_pairs={{0,16},{8,24},{16,0},{24,8},{1,17},{9,25},{17,1},{25,9},{2,18},{10... | collective-permute-start | bytes 786440 | tf_op jit(solution)/shard_map/ppermute | solution.py:11
  27.4 93.7 %collective-permute-start.29 = (bf16[16,128]{1,0:T(8,128)(2,1)S(1)}, bf16[16,128]{1,0:T(8,128)(2,1)S(1)}, u32[]{:S(2)}, u32[]{:S(2)}) collective-permute-start(bf16[16,128]{1,0:T(8,128)(2,1)S(1)} %fusion.71), channel_id=1, source_target_pairs={{0,24},{8,16},{16,8},{24,0},{1,25},{9,17},{17,9},{25,1},{2,26},{10... | collective-permute-start | bytes 12296 | tf_op jit(solution)/shard_map/ppermute | solution.py:11
  28.9 92.2 %collective-permute-start.28 = (bf16[16,128]{1,0:T(8,128)(2,1)S(1)}, bf16[16,128]{1,0:T(8,128)(2,1)S(1)}, u32[]{:S(2)}, u32[]{:S(2)}) collective-permute-start(bf16[16,128]{1,0:T(8,128)(2,1)S(1)} %fusion.71), channel_id=1, source_target_pairs={{0,16},{8,24},{16,0},{24,8},{1,17},{9,25},{17,1},{25,9},{2,18},{10... | collective-permute-start | bytes 12296 | tf_op jit(solution)/shard_map/ppermute | solution.py:11
  30.4 55.1 %collective-permute-start.18 = (bf16[128,1024]{1,0:T(8,128)(2,1)S(1)}, bf16[128,1024]{1,0:T(8,128)(2,1)S(1)}, u32[]{:S(2)}, u32[]{:S(2)}) collective-permute-start(bf16[128,1024]{1,0:T(8,128)(2,1)S(1)} %bitcast.236), channel_id=1, source_target_pairs={{0,6},{1,7},{2,4},{3,5},{4,2},{5,3},{6,0},{7,1},{8,14},{9,15},{10,... | collective-permute-start | bytes 786440 | tf_op jit(solution)/shard_map/ppermute | solution.py:11
  34.6 21.9 %collective-permute-start.8 = (bf16[128,1024]{1,0:T(8,128)(2,1)S(1)}, bf16[128,1024]{1,0:T(8,128)(2,1)S(1)}, u32[]{:S(2)}, u32[]{:S(2)}) collective-permute-start(bf16[128,1024]{1,0:T(8,128)(2,1)S(1)} %bitcast.237), channel_id=1, source_target_pairs={{0,2},{1,3},{2,0},{3,1},{4,6},{5,7},{6,4},{7,5},{8,10},{9,11},{10,... | collective-permute-start | bytes 786440 | tf_op jit(solution)/shard_map/ppermute | solution.py:11
  37.1 47.6 %collective-permute-start.13 = (bf16[128,1024]{1,0:T(8,128)(2,1)S(1)}, bf16[128,1024]{1,0:T(8,128)(2,1)S(1)}, u32[]{:S(2)}, u32[]{:S(2)}) collective-permute-start(bf16[128,1024]{1,0:T(8,128)(2,1)S(1)} %bitcast.238), channel_id=1, source_target_pairs={{0,4},{1,5},{2,6},{3,7},{4,0},{5,1},{6,2},{7,3},{8,12},{9,13},{10,... | collective-permute-start | bytes 786440 | tf_op jit(solution)/shard_map/ppermute | solution.py:11
  57.3 30.8 %collective-permute-start.9 = (bf16[2,128,128]{2,1,0:T(8,128)(2,1)S(1)}, bf16[2,128,128]{2,1,0:T(8,128)(2,1)S(1)}, u32[]{:S(2)}, u32[]{:S(2)}) collective-permute-start(bf16[2,128,128]{2,1,0:T(8,128)(2,1)S(1)} %get-tuple-element.23), channel_id=1, source_target_pairs={{0,8},{8,0},{16,24},{24,16},{1,9},{9,1},{17,25},{25,17},{2,10},{10... | collective-permute-start | bytes 196616 | tf_op jit(solution)/shard_map/ppermute | solution.py:11
  84.7 5.8 %collective-permute-start.11 = (bf16[2,128,128]{2,1,0:T(8,128)(2,1)S(1)}, bf16[2,128,128]{2,1,0:T(8,128)(2,1)S(1)}, u32[]{:S(2)}, u32[]{:S(2)}) collective-permute-start(bf16[2,128,128]{2,1,0:T(8,128)(2,1)S(1)} %get-tuple-element.24), channel_id=1, source_target_pairs={{0,24},{8,16},{16,8},{24,0},{1,25},{9,17},{17,9},{25,1},{2,26},{10... | collective-permute-start | bytes 196616 | tf_op jit(solution)/shard_map/ppermute | solution.py:11
  85.5 5.0 %collective-permute-start.10 = (bf16[2,128,128]{2,1,0:T(8,128)(2,1)S(1)}, bf16[2,128,128]{2,1,0:T(8,128)(2,1)S(1)}, u32[]{:S(2)}, u32[]{:S(2)}) collective-permute-start(bf16[2,128,128]{2,1,0:T(8,128)(2,1)S(1)} %get-tuple-element.25), channel_id=1, source_target_pairs={{0,16},{8,24},{16,0},{24,8},{1,17},{9,25},{17,1},{25,9},{2,18},{10... | collective-permute-start | bytes 196616 | tf_op jit(solution)/shard_map/ppermute | solution.py:11
  88.0 4.3 %collective-permute-start.14 = (bf16[2,128,128]{2,1,0:T(8,128)(2,1)S(1)}, bf16[2,128,128]{2,1,0:T(8,128)(2,1)S(1)}, u32[]{:S(2)}, u32[]{:S(2)}) collective-permute-start(bf16[2,128,128]{2,1,0:T(8,128)(2,1)S(1)} %get-tuple-element.26), channel_id=1, source_target_pairs={{0,8},{8,0},{16,24},{24,16},{1,9},{9,1},{17,25},{25,17},{2,10},{10... | collective-permute-start | bytes 196616 | tf_op jit(solution)/shard_map/ppermute | solution.py:11
  90.6 5.2 %collective-permute-start.16 = (bf16[2,128,128]{2,1,0:T(8,128)(2,1)S(1)}, bf16[2,128,128]{2,1,0:T(8,128)(2,1)S(1)}, u32[]{:S(2)}, u32[]{:S(2)}) collective-permute-start(bf16[2,128,128]{2,1,0:T(8,128)(2,1)S(1)} %get-tuple-element.27), channel_id=1, source_target_pairs={{0,24},{8,16},{16,8},{24,0},{1,25},{9,17},{17,9},{25,1},{2,26},{10... | collective-permute-start | bytes 196616 | tf_op jit(solution)/shard_map/ppermute | solution.py:11
  90.6 5.7 %collective-permute-start.15 = (bf16[2,128,128]{2,1,0:T(8,128)(2,1)S(1)}, bf16[2,128,128]{2,1,0:T(8,128)(2,1)S(1)}, u32[]{:S(2)}, u32[]{:S(2)}) collective-permute-start(bf16[2,128,128]{2,1,0:T(8,128)(2,1)S(1)} %get-tuple-element.28), channel_id=1, source_target_pairs={{0,16},{8,24},{16,0},{24,8},{1,17},{9,25},{17,1},{25,9},{2,18},{10... | collective-permute-start | bytes 196616 | tf_op jit(solution)/shard_map/ppermute | solution.py:11
  92.4 5.0 %collective-permute-start.4 = (bf16[2,128,128]{2,1,0:T(8,128)(2,1)S(1)}, bf16[2,128,128]{2,1,0:T(8,128)(2,1)S(1)}, u32[]{:S(2)}, u32[]{:S(2)}) collective-permute-start(bf16[2,128,128]{2,1,0:T(8,128)(2,1)S(1)} %get-tuple-element.20), channel_id=1, source_target_pairs={{0,8},{8,0},{16,24},{24,16},{1,9},{9,1},{17,25},{25,17},{2,10},{10... | collective-permute-start | bytes 196616 | tf_op jit(solution)/shard_map/ppermute | solution.py:11
  95.7 5.3 %collective-permute-start.6 = (bf16[2,128,128]{2,1,0:T(8,128)(2,1)S(1)}, bf16[2,128,128]{2,1,0:T(8,128)(2,1)S(1)}, u32[]{:S(2)}, u32[]{:S(2)}) collective-permute-start(bf16[2,128,128]{2,1,0:T(8,128)(2,1)S(1)} %get-tuple-element.21), channel_id=1, source_target_pairs={{0,24},{8,16},{16,8},{24,0},{1,25},{9,17},{17,9},{25,1},{2,26},{10... | collective-permute-start | bytes 196616 | tf_op jit(solution)/shard_map/ppermute | solution.py:11
  96.2 5.7 %collective-permute-start.5 = (bf16[2,128,128]{2,1,0:T(8,128)(2,1)S(1)}, bf16[2,128,128]{2,1,0:T(8,128)(2,1)S(1)}, u32[]{:S(2)}, u32[]{:S(2)}) collective-permute-start(bf16[2,128,128]{2,1,0:T(8,128)(2,1)S(1)} %get-tuple-element.22), channel_id=1, source_target_pairs={{0,16},{8,24},{16,0},{24,8},{1,17},{9,25},{17,1},{25,9},{2,18},{10... | collective-permute-start | bytes 196616 | tf_op jit(solution)/shard_map/ppermute | solution.py:11
  97.3 6.0 %collective-permute-start.19 = (bf16[2,128,128]{2,1,0:T(8,128)(2,1)S(1)}, bf16[2,128,128]{2,1,0:T(8,128)(2,1)S(1)}, u32[]{:S(2)}, u32[]{:S(2)}) collective-permute-start(bf16[2,128,128]{2,1,0:T(8,128)(2,1)S(1)} %get-tuple-element.29), channel_id=1, source_target_pairs={{0,8},{8,0},{16,24},{24,16},{1,9},{9,1},{17,25},{25,17},{2,10},{10... | collective-permute-start | bytes 196616 | tf_op jit(solution)/shard_map/ppermute | solution.py:11
  101.0 5.2 %collective-permute-start.21 = (bf16[2,128,128]{2,1,0:T(8,128)(2,1)S(1)}, bf16[2,128,128]{2,1,0:T(8,128)(2,1)S(1)}, u32[]{:S(2)}, u32[]{:S(2)}) collective-permute-start(bf16[2,128,128]{2,1,0:T(8,128)(2,1)S(1)} %get-tuple-element.30), channel_id=1, source_target_pairs={{0,24},{8,16},{16,8},{24,0},{1,25},{9,17},{17,9},{25,1},{2,26},{10... | collective-permute-start | bytes 196616 | tf_op jit(solution)/shard_map/ppermute | solution.py:11
  101.9 4.9 %collective-permute-start.20 = (bf16[2,128,128]{2,1,0:T(8,128)(2,1)S(1)}, bf16[2,128,128]{2,1,0:T(8,128)(2,1)S(1)}, u32[]{:S(2)}, u32[]{:S(2)}) collective-permute-start(bf16[2,128,128]{2,1,0:T(8,128)(2,1)S(1)} %get-tuple-element.31), channel_id=1, source_target_pairs={{0,16},{8,24},{16,0},{24,8},{1,17},{9,25},{17,1},{25,9},{2,18},{10... | collective-permute-start | bytes 196616 | tf_op jit(solution)/shard_map/ppermute | solution.py:11
  103.3 7.6 %collective-permute-start.12 = (bf16[2,80,128]{2,1,0:T(8,128)(2,1)S(1)}, bf16[2,80,128]{2,1,0:T(8,128)(2,1)S(1)}, u32[]{:S(2)}, u32[]{:S(2)}) collective-permute-start(bf16[2,80,128]{2,1,0:T(8,128)(2,1)S(1)} %copy.105), channel_id=1, source_target_pairs={{0,2},{1,3},{2,0},{3,1},{4,6},{5,7},{6,4},{7,5},{8,10},{9,11},{10,... | collective-permute-start | bytes 122888 | tf_op jit(solution)/shard_map/ppermute | solution.py:11
  106.2 9.0 %collective-permute-start.17 = (bf16[2,80,128]{2,1,0:T(8,128)(2,1)S(1)}, bf16[2,80,128]{2,1,0:T(8,128)(2,1)S(1)}, u32[]{:S(2)}, u32[]{:S(2)}) collective-permute-start(bf16[2,80,128]{2,1,0:T(8,128)(2,1)S(1)} %copy.110), channel_id=1, source_target_pairs={{0,4},{1,5},{2,6},{3,7},{4,0},{5,1},{6,2},{7,3},{8,12},{9,13},{10,... | collective-permute-start | bytes 122888 | tf_op jit(solution)/shard_map/ppermute | solution.py:11
  107.3 7.9 %collective-permute-start.22 = (bf16[2,80,128]{2,1,0:T(8,128)(2,1)S(1)}, bf16[2,80,128]{2,1,0:T(8,128)(2,1)S(1)}, u32[]{:S(2)}, u32[]{:S(2)}) collective-permute-start(bf16[2,80,128]{2,1,0:T(8,128)(2,1)S(1)} %copy.115), channel_id=1, source_target_pairs={{0,6},{1,7},{2,4},{3,5},{4,2},{5,3},{6,0},{7,1},{8,14},{9,15},{10,... | collective-permute-start | bytes 122888 | tf_op jit(solution)/shard_map/ppermute | solution.py:11
  110.9 10.3 %collective-permute-start.27 = (bf16[16,128]{1,0:T(8,128)(2,1)S(1)}, bf16[16,128]{1,0:T(8,128)(2,1)S(1)}, u32[]{:S(2)}, u32[]{:S(2)}) collective-permute-start(bf16[16,128]{1,0:T(8,128)(2,1)S(1)} %fusion.71), channel_id=1, source_target_pairs={{0,8},{8,0},{16,24},{24,16},{1,9},{9,1},{17,25},{25,17},{2,10},{10... | collective-permute-start | bytes 12296 | tf_op jit(solution)/shard_map/ppermute | solution.py:11
  119.9 15.6 %collective-permute-start.25 = (bf16[2,64,768]{2,1,0:T(8,128)(2,1)S(1)}, bf16[2,64,768]{2,1,0:T(8,128)(2,1)S(1)}, u32[]{:S(2)}, u32[]{:S(2)}) collective-permute-start(bf16[2,64,768]{2,1,0:T(8,128)(2,1)S(1)} %get-tuple-element.18), channel_id=1, source_target_pairs={{0,16},{8,24},{16,0},{24,8},{1,17},{9,25},{17,1},{25,9},{2,18},{10... | collective-permute-start | bytes 589832 | tf_op jit(solution)/shard_map/ppermute | solution.py:11
  120.3 15.2 %collective-permute-start.23 = (bf16[2,64,768]{2,1,0:T(8,128)(2,1)S(1)}, bf16[2,64,768]{2,1,0:T(8,128)(2,1)S(1)}, u32[]{:S(2)}, u32[]{:S(2)}) collective-permute-start(bf16[2,64,768]{2,1,0:T(8,128)(2,1)S(1)} %get-tuple-element.19), channel_id=1, source_target_pairs={{0,8},{8,0},{16,24},{24,16},{1,9},{9,1},{17,25},{25,17},{2,10},{10... | collective-permute-start | bytes 589832 | tf_op jit(solution)/shard_map/ppermute | solution.py:11
  135.6 7.2 %collective-permute-start.26 = (bf16[2,64,768]{2,1,0:T(8,128)(2,1)S(1)}, bf16[2,64,768]{2,1,0:T(8,128)(2,1)S(1)}, u32[]{:S(2)}, u32[]{:S(2)}) collective-permute-start(bf16[2,64,768]{2,1,0:T(8,128)(2,1)S(1)} %get-tuple-element.16), channel_id=1, source_target_pairs={{0,8},{8,0},{16,24},{24,16},{1,9},{9,1},{17,25},{25,17},{2,10},{10... | collective-permute-start | bytes 589832 | tf_op jit(solution)/shard_map/ppermute | solution.py:11
  137.0 6.9 %collective-permute-start.24 = (bf16[2,64,768]{2,1,0:T(8,128)(2,1)S(1)}, bf16[2,64,768]{2,1,0:T(8,128)(2,1)S(1)}, u32[]{:S(2)}, u32[]{:S(2)}) collective-permute-start(bf16[2,64,768]{2,1,0:T(8,128)(2,1)S(1)} %get-tuple-element.17), channel_id=1, source_target_pairs={{0,16},{8,24},{16,0},{24,8},{1,17},{9,25},{17,1},{25,9},{2,18},{10... | collective-permute-start | bytes 589832 | tf_op jit(solution)/shard_map/ppermute | solution.py:11
  171.0 23.3 %collective-permute-start.32 = (bf16[640,128]{0,1:T(8,128)(2,1)S(1)}, bf16[640,128]{0,1:T(8,128)(2,1)S(1)}, u32[]{:S(2)}, u32[]{:S(2)}) collective-permute-start(bf16[640,128]{0,1:T(8,128)(2,1)S(1)} %bitcast.248), channel_id=1, source_target_pairs={{0,24},{8,16},{16,8},{24,0},{1,25},{9,17},{17,9},{25,1},{2,26},{10... | collective-permute-start | bytes 491528 | tf_op jit(solution)/shard_map/ppermute | solution.py:11
  172.4 21.9 %collective-permute-start.31 = (bf16[640,128]{0,1:T(8,128)(2,1)S(1)}, bf16[640,128]{0,1:T(8,128)(2,1)S(1)}, u32[]{:S(2)}, u32[]{:S(2)}) collective-permute-start(bf16[640,128]{0,1:T(8,128)(2,1)S(1)} %bitcast.249), channel_id=1, source_target_pairs={{0,16},{8,24},{16,0},{24,8},{1,17},{9,25},{17,1},{25,9},{2,18},{10... | collective-permute-start | bytes 491528 | tf_op jit(solution)/shard_map/ppermute | solution.py:11
  173.4 20.9 %collective-permute-start.30 = (bf16[640,128]{0,1:T(8,128)(2,1)S(1)}, bf16[640,128]{0,1:T(8,128)(2,1)S(1)}, u32[]{:S(2)}, u32[]{:S(2)}) collective-permute-start(bf16[640,128]{0,1:T(8,128)(2,1)S(1)} %bitcast.250), channel_id=1, source_target_pairs={{0,8},{8,0},{16,24},{24,16},{1,9},{9,1},{17,25},{25,17},{2,10},{10... | collective-permute-start | bytes 491528 | tf_op jit(solution)/shard_map/ppermute | solution.py:11
  (5 other events, 66.7 us)
Sparse Core Ops, SparseCore 0:
  27.5 102.9 all-gather.3

commit v2 on v1

v2 whole, which is shorter than its diff:
```python
import functools

import jax
import jax.numpy as jnp
from jax import lax
from jax.experimental import pallas as pl
from jax.experimental.pallas import tpu as pltpu
from jax.sharding import PartitionSpec as P

CORES = 2
VMEM = 24 << 20
HIGHEST = lax.Precision.HIGHEST
NT = (((1,), (1,)), ((), ()))
TN = (((0,), (0,)), ((), ()))


def exchange(value, axis, distance):
    size = lax.axis_size(axis)
    return lax.ppermute(value, axis, [(i, i ^ distance) for i in range(size)])


def shift(value, axis, distance):
    size = lax.axis_size(axis)
    return lax.ppermute(value, axis, [(i, (i + distance) % size) for i in range(size)])


def dense_gates(expert_ids, gates, experts_all):
    labels = jnp.arange(experts_all, dtype=jnp.int32)[:, None]
    dense = jnp.zeros((experts_all, expert_ids.shape[0]), jnp.bfloat16)
    for column in range(expert_ids.shape[1]):
        hit = labels == expert_ids[:, column][None, :]
        dense = dense + jnp.where(hit, gates[:, column][None, :], jnp.zeros((), jnp.bfloat16))
    return dense


def sum_steps(members):
    distances = []
    step = 1
    while step < members:
        distances.append(step)
        step *= 2
    return distances, distances[::-1]


def slots_of(gates):
    tokens = gates.shape[1]
    before = (
        lax.broadcasted_iota(jnp.int32, (tokens, tokens), 0)
        < lax.broadcasted_iota(jnp.int32, (tokens, tokens), 1)
    ).astype(jnp.bfloat16)
    named = (gates > 0).astype(jnp.bfloat16)
    slot = jnp.dot(named, before, preferred_element_type=jnp.float32)
    return jnp.where(gates > 0, slot, -1.0)


def block_of(ref, group, sizes):
    members, tokens, _, _, experts_all = sizes
    chunks = ref.shape[1] // tokens
    start = group * tokens
    gate_row = members * tokens + group // chunks * experts_all
    gate_lane = group % chunks * tokens
    if not isinstance(group, int):
        start = pl.multiple_of(start, tokens)
        gate_row = pl.multiple_of(gate_row, 16)
        gate_lane = pl.multiple_of(gate_lane, tokens)
    return (
        ref[pl.ds(start, tokens), :],
        ref[pl.ds(gate_row, experts_all), pl.ds(gate_lane, tokens)],
    )


def for_each(count, body):
    if count <= 4:
        for index in range(count):
            body(index)
        return

    def step(index, carry):
        body(index)
        return carry

    lax.fori_loop(0, count, step, 0)


def project_kernel(sizes, halves, place_ref, *refs):
    members, tokens, held, rank, experts_all = sizes
    blocks, factors = refs[: 2 * halves], refs[2 * halves : -2]
    out_ref, stacked_ref = refs[-2:]
    chips, padded = len(factors), out_ref.shape[3]
    wide = held * rank
    for k in range(chips):
        stacked_ref[k * wide : (k + 1) * wide] = factors[k][...]
    index = lax.broadcasted_iota(jnp.int32, (chips * held, experts_all), 0)
    owner = ((place_ref[0] ^ (index // held)) * CORES + place_ref[1]) * held + index % held
    pick = (lax.broadcasted_iota(jnp.int32, owner.shape, 1) == owner).astype(jnp.bfloat16)
    row = lax.broadcasted_iota(jnp.int32, (padded, tokens), 0).astype(jnp.float32)
    lane = lax.broadcasted_iota(jnp.int32, (padded, wide), 1)

    def one_block(ref, group, out_group, core):
        columns, dense = block_of(ref, group, sizes)
        gates = jnp.dot(pick, dense, preferred_element_type=jnp.float32)
        slot = slots_of(gates)
        y = lax.dot_general(stacked_ref[...], columns, NT, preferred_element_type=jnp.float32)
        for k in range(chips):
            weighted, choice = [], []
            for i in range(k * held, (k + 1) * held):
                weighted.append(y[i * rank : (i + 1) * rank] * gates[i : i + 1])
                choice.append(jnp.where(slot[i : i + 1] == row, 1.0, 0.0))
            full = lax.dot_general(
                jnp.concatenate(choice).astype(jnp.bfloat16),
                jnp.concatenate(weighted).astype(jnp.bfloat16),
                NT,
                preferred_element_type=jnp.float32,
            )
            packed = full[:padded]
            for h in range(1, held):
                packed = jnp.where(lane >= h * rank, full[h * padded : (h + 1) * padded], packed)
            out_ref[out_group, k, core] = packed.astype(jnp.bfloat16)

    for half in range(halves):
        for core in range(CORES):
            ref = blocks[half * CORES + core]
            for_each(
                members,
                functools.partial(
                    lambda ref, half, core, g: one_block(ref, g, half * members + g, core),
                    ref,
                    half,
                    core,
                ),
            )


def project(place, blocks, factors, sizes, padded):
    members, tokens, held, rank, _ = sizes
    wide = held * rank
    chips, halves = len(factors), len(blocks) // CORES
    return pl.pallas_call(
        functools.partial(project_kernel, sizes, halves),
        out_shape=jax.ShapeDtypeStruct(
            (halves * members, chips, CORES, padded, wide), jnp.bfloat16
        ),
        in_specs=[pl.BlockSpec(memory_space=pltpu.SMEM)]
        + [pl.BlockSpec(memory_space=pltpu.VMEM)] * (len(blocks) + chips),
        out_specs=pl.BlockSpec(memory_space=pltpu.VMEM),
        scratch_shapes=[pltpu.VMEM((chips * wide, blocks[0].shape[1]), jnp.bfloat16)],
        compiler_params=pltpu.CompilerParams(vmem_limit_bytes=VMEM),
    )(place, *blocks, *factors)


def left_kernel(place_ref, *refs):
    arrived, hidden_ref, outs, rows_ref = refs[:-4], refs[-4], refs[-3:-1], refs[-1]
    for k, ref in enumerate(arrived):
        base = (place_ref[0] ^ k) * CORES
        rows_ref[base + place_ref[1]] = ref[0]
        rows_ref[base + 1 - place_ref[1]] = ref[1]
    places, capacity, wide = rows_ref.shape
    held = hidden_ref.shape[0]
    rank = wide // held
    rows = rows_ref[...].reshape(places * capacity, wide)
    half = outs[0].shape[1]
    for h in range(held):
        for index, out_ref in enumerate(outs):
            product = lax.dot_general(
                rows,
                hidden_ref[h, :, index * half : (index + 1) * half],
                TN,
                preferred_element_type=jnp.float32,
            )
            out_ref[h * rank : (h + 1) * rank] = product[h * rank : (h + 1) * rank].astype(
                jnp.bfloat16
            )


def left_partial(place, arrived, own_hidden, capacity):
    held, slots, width = own_hidden.shape
    _, padded, wide = arrived[0].shape
    if padded != capacity:
        chips = len(arrived)
        rows = jnp.take(jnp.stack(arrived), jnp.arange(chips) ^ place[0], axis=0)
        rows = jnp.take(rows, jnp.arange(CORES) ^ place[1], axis=1)[:, :, :capacity]
        rows = rows.reshape(slots, held, wide // held)
        value = jnp.einsum("shr,hsf->hrf", rows, own_hidden, preferred_element_type=jnp.float32)
        value = value.reshape(wide, width).astype(jnp.bfloat16)
        return [value[:, : width // 2], value[:, width // 2 :]]
    shape = jax.ShapeDtypeStruct((wide, width // 2), jnp.bfloat16)
    return pl.pallas_call(
        left_kernel,
        out_shape=(shape, shape),
        in_specs=[pl.BlockSpec(memory_space=pltpu.SMEM)]
        + [pl.BlockSpec(memory_space=pltpu.VMEM)] * (len(arrived) + 1),
        out_specs=(pl.BlockSpec(memory_space=pltpu.VMEM),) * 2,
        scratch_shapes=[pltpu.VMEM((slots // capacity, capacity, wide), jnp.bfloat16)],
        compiler_params=pltpu.CompilerParams(vmem_limit_bytes=VMEM),
    )(place, *arrived, own_hidden)


def whiten_kernel(first_ref, first_got_ref, last_ref, last_got_ref, hidden_ref, mapped_ref, merged_ref):
    held, rank, width = merged_ref.shape
    half = width // 2
    for h in range(held):
        rows = slice(h * rank, (h + 1) * rank)
        merged_ref[h, :, :half] = first_ref[rows].astype(jnp.float32) + first_got_ref[rows].astype(
            jnp.float32
        )
        merged_ref[h, :, half:] = last_ref[rows].astype(jnp.float32) + last_got_ref[rows].astype(
            jnp.float32
        )
    lane = lax.broadcasted_iota(jnp.int32, (8, 2 * rank), 1)
    row = lax.broadcasted_iota(jnp.int32, (8, 2 * rank), 0)
    blocks = rank // 8
    states = []
    for h in range(held):
        factor = merged_ref[h]
        gram = lax.dot_general(
            factor, factor, NT, precision=HIGHEST, preferred_element_type=jnp.float32
        )
        padded = jnp.concatenate([gram, jnp.zeros_like(gram)], axis=1)
        states.append(
            [
                jnp.where(lane == rank + 8 * b + row, 1.0, padded[8 * b : 8 * b + 8])
                for b in range(blocks)
            ]
        )
    for k in range(rank):
        first, inner = k // 8, k % 8
        for state in states:
            pivot_column = jnp.broadcast_to(state[first][:, k : k + 1], (8, 2 * rank))
            scaled = state[first][inner : inner + 1] / pivot_column[inner : inner + 1]
            for b in range(first, blocks):
                column = pivot_column
                if b == first:
                    column = jnp.where(row > inner, column, 0.0)
                else:
                    column = jnp.broadcast_to(state[b][:, k : k + 1], (8, 2 * rank))
                state[b] = state[b] - column * scaled
    for h in range(held):
        inverse = []
        for b, block in enumerate(states[h]):
            pivot = jnp.sum(jnp.where(lane == 8 * b + row, block, 0.0), axis=1, keepdims=True)
            inverse.append(block[:, rank:] / jnp.sqrt(pivot))
        inverse = jnp.concatenate(inverse, axis=0)
        basis = jnp.dot(
            inverse, merged_ref[h], precision=HIGHEST, preferred_element_type=jnp.float32
        ).astype(jnp.bfloat16)
        mapped_ref[:, h * rank : (h + 1) * rank] = lax.dot_general(
            hidden_ref[h], basis, NT, preferred_element_type=jnp.float32
        ).astype(jnp.bfloat16)


def whiten_and_map(parts, own_hidden):
    held, slots, width = own_hidden.shape
    wide = parts[0].shape[0]
    return pl.pallas_call(
        whiten_kernel,
        out_shape=(
            jax.ShapeDtypeStruct((slots, wide), jnp.bfloat16),
            jax.ShapeDtypeStruct((held, wide // held, width), jnp.float32),
        ),
        compiler_params=pltpu.CompilerParams(vmem_limit_bytes=VMEM),
    )(*parts, own_hidden)


def dispatch_kernel(sizes, place_ref, own_ref, other_ref, out_ref):
    members, tokens, held, _, experts_all = sizes
    padded = out_ref.shape[3]
    row = lax.broadcasted_iota(jnp.int32, (padded, tokens), 0).astype(jnp.float32)
    index = lax.broadcasted_iota(jnp.int32, (8, experts_all), 0)
    pick = lax.broadcasted_iota(jnp.int32, (8, experts_all), 1) == place_ref[0] * held + index
    pick = pick.astype(jnp.bfloat16)

    def one_group(g):
        for ref, core in ((own_ref, place_ref[1]), (other_ref, 1 - place_ref[1])):
            columns, dense = block_of(ref, g, sizes)
            gates = jnp.dot(pick, dense, preferred_element_type=jnp.float32)
            slot = slots_of(gates)
            choice = [
                jnp.where(slot[h : h + 1] == row, gates[h : h + 1], 0.0) for h in range(held)
            ]
            rows = jnp.dot(
                jnp.concatenate(choice).astype(jnp.bfloat16),
                columns,
                preferred_element_type=jnp.float32,
            ).astype(jnp.bfloat16)
            for h in range(held):
                out_ref[h, g, core] = rows[h * padded : (h + 1) * padded]

    for_each(members, one_group)


def dispatch(place, own, other, sizes, padded):
    members, tokens, held, _, _ = sizes
    return pl.pallas_call(
        functools.partial(dispatch_kernel, sizes),
        out_shape=jax.ShapeDtypeStruct(
            (held, members, CORES, padded, own.shape[1]), jnp.bfloat16
        ),
        in_specs=[pl.BlockSpec(memory_space=pltpu.SMEM)]
        + [pl.BlockSpec(memory_space=pltpu.VMEM)] * 2,
        out_specs=pl.BlockSpec(memory_space=pltpu.VMEM),
        compiler_params=pltpu.CompilerParams(vmem_limit_bytes=VMEM),
    )(place, own, other)


def right_kernel(steps, members, sources_ref, *refs):
    mapped, dispatched = refs[:members], refs[members : members + len(steps)]
    out_ref = refs[-1]
    held, groups, _, padded, part = dispatched[0].shape
    rank = out_ref.shape[1]
    if len(refs) > members + len(steps) + 1:
        out_ref[...] = refs[-2][...]
    else:
        out_ref[...] = jnp.zeros_like(out_ref)
    for (step, first), ref in zip(steps, dispatched):
        for g in range(groups):
            rows = mapped[first + g][pl.ds(sources_ref[step] * CORES, CORES)]
            rows = rows.reshape(CORES * padded, held * rank)
            for h in range(held):
                product = lax.dot_general(
                    rows,
                    ref[h, g].reshape(CORES * padded, part),
                    TN,
                    preferred_element_type=jnp.float32,
                )
                out_ref[h] += product[h * rank : (h + 1) * rank]


def right_factor(sources, mapped_groups, steps, dispatched, before=None):
    held, _, _, _, part = dispatched[0].shape
    rank = mapped_groups[0].shape[-1] // held
    operands = [*mapped_groups, *dispatched] + ([] if before is None else [before])
    return pl.pallas_call(
        functools.partial(right_kernel, steps, len(mapped_groups)),
        out_shape=jax.ShapeDtypeStruct((held, rank, part), jnp.float32),
        in_specs=[pl.BlockSpec(memory_space=pltpu.SMEM)]
        + [pl.BlockSpec(memory_space=pltpu.VMEM)] * len(operands),
        out_specs=pl.BlockSpec(memory_space=pltpu.VMEM),
        compiler_params=pltpu.CompilerParams(vmem_limit_bytes=VMEM),
    )(sources, *operands)


def local(cotangent, expert_ids, gates, hidden, q_prev):
    members = lax.axis_size("dp")
    places = lax.axis_size("expert")
    chips = places // CORES
    held, _, slots, width = hidden.shape
    rank = q_prev.shape[2]
    tokens, model_width = cotangent.shape
    experts_all = held * places
    capacity = slots // places
    padded = -(-capacity // 16) * 16
    part = model_width // members
    chunks = part // tokens
    halves = 2 if members > 1 else 1
    groups = members // halves
    sizes = (groups, tokens, held, rank, experts_all)
    my_dp = lax.axis_index("dp")
    my_place = lax.axis_index("expert")
    my_chip, my_core = my_place // CORES, my_place % CORES
    place = jnp.stack([my_chip, my_core]).astype(jnp.int32)
    own_place = jnp.stack([my_place, my_core]).astype(jnp.int32)
    own_hidden = hidden[:, 0]
    tie = lax.optimization_barrier

    def over_chips(blocks):
        return [shift(block, "expert", CORES) for block in blocks]

    def over_cores(blocks):
        return [exchange(block, "expert", 1) for block in blocks]

    def dispatch_half(blocks, others, half):
        return dispatch(own_place, blocks[half], others[half], sizes, padded)

    factor = jnp.swapaxes(q_prev, 1, 2).reshape(held * rank, part)
    factors = [factor] + [exchange(factor, "expert", CORES * k) for k in range(1, chips)]

    dense = dense_gates(expert_ids, gates, experts_all)
    tail = jnp.pad(dense, ((0, 0), (0, part - tokens)))
    pieces = []
    for k in range(members):
        piece = lax.dynamic_slice_in_dim(cotangent, (my_dp ^ k) * part, part, 1)
        piece = jnp.concatenate([piece, tail], axis=0)
        pieces.append(exchange(piece, "dp", k) if k else piece)
    pieces, factors = tie((pieces, factors))
    own = []
    for half in range(halves):
        mine = pieces[half * groups : (half + 1) * groups]
        tails = [piece[tokens:, :tokens] for piece in mine]
        while len(tails) % chunks:
            tails.append(jnp.zeros_like(tails[0]))
        tails = [jnp.concatenate(tails[i : i + chunks], 1) for i in range(0, len(tails), chunks)]
        own.append(jnp.concatenate([piece[:tokens] for piece in mine] + tails, axis=0))
    other = over_cores(own)
    ring = over_chips(own) if chips > 1 else None

    blocks = [block for pair in zip(own, other) for block in pair]
    y = project(place, blocks, factors, sizes, padded)
    got = [exchange(y[d], "dp", d) for d in range(1, members)]
    dispatched = [dispatch_half(own, other, half) for half in range(halves)]
    got, dispatched = tie((got, dispatched))
    summed = y[0].astype(jnp.float32)
    for value in got:
        summed = summed + value.astype(jnp.float32)
    summed = summed.astype(jnp.bfloat16)
    arrived = [summed[0]] + [exchange(summed[k], "expert", CORES * k) for k in range(1, chips)]
    steps = [(0, half * groups) for half in range(halves)]
    orders = sum_steps(members)
    rounds = len(orders[0])
    pending = []

    def advance(value, ring, step):
        value, ring = tie((value, ring))
        others = over_cores(ring)
        for half in range(halves):
            pending.append((step, half, ring, others))
        return value, (over_chips(ring) if step < chips - 1 else None)

    def fill(value):
        if not pending:
            return value
        step, half, blocks, others = pending.pop(0)
        done = dispatch_half(blocks, others, half)
        value, done = tie((value, done))
        dispatched.append(done)
        steps.append((step, half * groups))
        return value

    step = 1
    if chips > 1:
        arrived, ring = advance(arrived, ring, step)
        step += 1
    parts = left_partial(place, arrived, own_hidden, capacity)
    for index in range(rounds):
        got = [exchange(p, "dp", order[index]) for p, order in zip(parts, orders)]
        got = fill(got)
        if index < rounds - 1:
            parts = [
                (p.astype(jnp.float32) + q.astype(jnp.float32)).astype(jnp.bfloat16)
                for p, q in zip(parts, got)
            ]
    mapped, merged = whiten_and_map([parts[0], got[0], parts[1], got[1]], own_hidden)
    if ring is not None and step < chips:
        mapped, ring = advance(mapped, ring, step)
        step += 1
    mapped = mapped.reshape(places, capacity, held * rank)
    mapped = jnp.pad(mapped, ((0, 0), (0, padded - capacity), (0, 0)))
    gathered = [exchange(mapped, "dp", k) for k in range(1, members)]
    while pending:
        gathered = fill(gathered)
    mapped_groups = [mapped] + gathered
    sources = ((my_chip - jnp.arange(chips)) % chips).astype(jnp.int32)
    q_next = right_factor(sources, mapped_groups, steps, dispatched)
    while ring is not None and step < chips:
        q_next, ring = advance(q_next, ring, step)
        step += 1
        while pending:
            late, half, blocks, others = pending.pop(0)
            done = dispatch_half(blocks, others, half)
            q_next = right_factor(
                sources, mapped_groups, [(late, half * groups)], [done], q_next
            )
    share = width // members
    p_share = lax.dynamic_slice_in_dim(merged, my_dp * share, share, 2)
    return (jnp.swapaxes(p_share, 1, 2), jnp.swapaxes(q_next, 1, 2))


def solution(mesh):
    placed = (
        P(("dp", "expert"), None),
        P(("dp", "expert"), None),
        P(("dp", "expert"), None),
        P("expert", "dp", None, None),
        P("expert", "dp", None),
    )
    return jax.shard_map(
        local,
        mesh=mesh,
        in_specs=placed,
        out_specs=(P("expert", "dp", None), P("expert", "dp", None)),
        check_vma=False,
    )
```

time: 208 us -> 148 us (0.71)
  Pallas kernels: 0 us -> 37.9 us
  matrix products: 27.9 us -> 0 us
  other arithmetic: 24.4 us -> 0.57 us
  waiting for transfers between devices: 79.5 us -> 61.8 us
  blocking collectives: 14.3 us -> 0 us
  between operations: 14.5 us -> 1.03 us
  local copies, waits for them, and re-layouts: 14.2 us -> 5.02 us
  starting transfers between devices: 33 us -> 41.1 us
    ppermute x33 -> x27, waiting for transfers between devices: 79.5 us -> 32.6 us  [exchange(): return lax.ppermute(value, axis, [(i, i ^ distance) for i in range(size)])]
    pallas_call x0 -> x14, Pallas kernels: none -> 37.9 us  [the longest x8 15.9 us: dispatch(): pl.pallas_call(functools.partial(dispatch_kernel, sizes), out_shape=jax.S...]
    ppermute x0 -> x6, waiting for transfers between devices: none -> 29.3 us  [shift(): lax.ppermute(value, axis, [(i, (i + distance) % size) for i in range(size)])]
    dot_general x18 -> x0, matrix products: 27 us -> none  [the longest x1 8.91 us: local(): jnp.einsum('gphct,gptd->hgpcd', choice, gathered, preferred_element_type=...]
    another operation x11 -> x2, other arithmetic: 23.2 us -> 0.15 us  [the longest x1 0.07 us: local(): place = jnp.stack([my_chip, my_core]).astype(jnp.int32)]
    ppermute x0 -> x6, starting transfers between devices: none -> 14.7 us  [shift(): lax.ppermute(value, axis, [(i, (i + distance) % size) for i in range(size)])]
    all_gather x1 -> x0, blocking collectives: 14.3 us -> none  [local(): gathered_gates = lax.all_gather(dense_groups, 'expert', axis=1)]
    convert_element_type x2 -> x0, local copies, waits for them, and re-layouts: 10.1 us -> none  [the longest x1 10.1 us: local(): dispatched = jnp.einsum('gphct,gptd->hgpcd', choice, gathered, preferred_...]
  transfers between devices with their start and end apart: 34 -> 33, of which waited for: 17 -> 14; matrix products, arithmetic and copies ran while one was open for 28% -> 4% of each run, Pallas kernels for 0% -> 18%
where the time goes in v2:
time: 148 us; the launch traced here: 147 us
  waiting for transfers between devices  61.8 us (42%)
  starting transfers between devices  41.1 us (28%)
  Pallas kernels  37.9 us (26%)
  local copies, waits for them, and re-layouts  5.02 us (3%)
    ppermute x27, waiting for transfers between devices, exchange(): return lax.ppermute(value, axis, [(i, i ^ distance) for i in range(size)])  32.6 us
    ppermute x6, waiting for transfers between devices, shift(): lax.ppermute(value, axis, [(i, (i + distance) % size) for i in range(size)])  29.3 us
    ppermute x27, starting transfers between devices, exchange(): return lax.ppermute(value, axis, [(i, i ^ distance) for i in range(size)])  26.4 us
    pallas_call x8, Pallas kernels, dispatch(): pl.pallas_call(functools.partial(dispatch_kernel, sizes), out_shape=jax.S...  15.9 us
    ppermute x6, starting transfers between devices, shift(): lax.ppermute(value, axis, [(i, (i + distance) % size) for i in range(size)])  14.7 us
    pallas_call x1, Pallas kernels, whiten_and_map(): pl.pallas_call(whiten_kernel, out_shape=(jax.ShapeDtypeStruct((slots, wid...  8.32 us
    pallas_call x1, Pallas kernels, project(): pl.pallas_call(functools.partial(project_kernel, sizes, halves), out_shap...  7.18 us
    pallas_call x3, Pallas kernels, right_factor(): pl.pallas_call(functools.partial(right_kernel, steps, len(mapped_groups))...  5.17 us
  transfers between devices with their start and end apart: 33, of which 14 were waited for; matrix products, arithmetic and copies ran while one was open for 4% of the time, Pallas kernels for 18%

profile of v2, /device:TPU:0, one launch (start us, length us, event | category | flops | bytes accessed | tf_op | source)
XLA Modules:
  0.0 147.4 jit_solution(14458075042141979072)
XLA Ops:
  0.6 3.1 %collective-permute-start.3 = (bf16[128,1024]{1,0:T(8,128)(2,1)}, bf16[128,1024]{1,0:T(8,128)(2,1)S(1)}, u32[]{:S(2)}, u32[]{:S(2)}) collective-permute-start(bf16[128,1024]{1,0:T(8,128)(2,1)} %bitcast.70), channel_id=1, source_target_pairs={{0,2},{1,3},{2,0},{3,1},{4,6},{5,7},{6,4},{7,5},{8,10},{9,11},{10,... | collective-permute-start | bytes 786440 | tf_op jit(solution)/shard_map/ppermute | solution.py:19
  7.1 1.6 %collective-permute-start = (bf16[144,1024]{1,0:T(8,128)(2,1)S(1)}, bf16[144,1024]{1,0:T(8,128)(2,1)S(1)}, u32[]{:S(2)}, u32[]{:S(2)}) collective-permute-start(bf16[144,1024]{1,0:T(8,128)(2,1)S(1)} %get-tuple-element.103), channel_id=1, source_target_pairs={{0,8},{8,0},{16,24},{24,16},{1,9},{9,1},{17,25},{25,17},{2,10},{10... | collective-permute-start | bytes 884744 | tf_op jit(solution)/shard_map/ppermute | solution.py:19
  10.7 2.6 %collective-permute-start.4 = (bf16[128,1024]{1,0:T(8,128)(2,1)S(1)}, bf16[128,1024]{1,0:T(8,128)(2,1)S(1)}, u32[]{:S(2)}, u32[]{:S(2)}) collective-permute-start(bf16[128,1024]{1,0:T(8,128)(2,1)S(1)} %bitcast.71), channel_id=1, source_target_pairs={{0,4},{1,5},{2,6},{3,7},{4,0},{5,1},{6,2},{7,3},{8,12},{9,13},{10,... | collective-permute-start | bytes 786440 | tf_op jit(solution)/shard_map/ppermute | solution.py:19
  14.0 15.7 %collective-permute-done.4.refs_6_ = bf16[128,1024]{1,0:T(8,128)(2,1)S(1)} collective-permute-done((bf16[128,1024]{1,0:T(8,128)(2,1)S(1)}, bf16[128,1024]{1,0:T(8,128)(2,1)S(1)}, u32[]{:S(2)}, u32[]{:S(2)}) %collective-permute-start.4) | collective-permute-done | bytes 262176 | tf_op jit(solution)/shard_map/ppermute | solution.py:19
  32.8 7.2 %shard_map.68 = bf16[4,4,2,80,128]{4,3,2,1,0:T(8,128)(2,1)S(1)} custom-call(s32[2]{0:T(128)S(1)} %pad_add_fusion.place_ref, bf16[272,1024]{1,0:T(8,128)(2,1)S(1)} %get-tuple-element.100.refs_0_.own_ref, bf16[272,1024]{1,0:T(8,128)(2,1)S(1)} %collective-permute-done.6.refs_1_.other_ref, bf16[272,1024]{1,0:T(8,128)(2,1)S(1)} %get-tuple-element.99.refs_2_.own_ref, ...), custom_call_target="tpu_custom_call" | custom-call | tf_op jit(solution)/shard_map/pallas_call | solution.py:138
  40.0 1.6 %collective-permute-start.8 = (bf16[4,2,80,128]{3,2,1,0:T(8,128)(2,1)S(1)}, bf16[4,2,80,128]{3,2,1,0:T(8,128)(2,1)S(1)}, u32[]{:S(2)}, u32[]{:S(2)}) collective-permute-start(bf16[4,2,80,128]{3,2,1,0:T(8,128)(2,1)S(1)} %get-tuple-element.94), channel_id=1, source_target_pairs={{0,8},{8,0},{16,24},{24,16},{1,9},{9,1},{17,25},{25,17},{2,10},{10... | collective-permute-start | bytes 491528 | tf_op jit(solution)/shard_map/ppermute | solution.py:19
  43.6 6.1 %collective-permute-start.14 = (bf16[272,1024]{1,0:T(8,128)(2,1)S(1)}, bf16[272,1024]{1,0:T(8,128)(2,1)S(1)}, u32[]{:S(2)}, u32[]{:S(2)}) collective-permute-start(bf16[272,1024]{1,0:T(8,128)(2,1)S(1)} %get-tuple-element.100.refs_0_.own_ref), channel_id=1, source_target_pairs={{0,2},{1,3},{2,4},{3,5},{4,6},{5,7},{6,0},{7,1},{8,10},{9,11},{10,... | collective-permute-start | bytes 1671176 | tf_op jit(solution)/shard_map/ppermute | solution.py:24
  49.7 1.7 %collective-permute-start.15 = (bf16[272,1024]{1,0:T(8,128)(2,1)S(1)}, bf16[272,1024]{1,0:T(8,128)(2,1)S(1)}, u32[]{:S(2)}, u32[]{:S(2)}) collective-permute-start(bf16[272,1024]{1,0:T(8,128)(2,1)S(1)} %get-tuple-element.99.refs_2_.own_ref), channel_id=1, source_target_pairs={{0,2},{1,3},{2,4},{3,5},{4,6},{5,7},{6,0},{7,1},{8,10},{9,11},{10,... | collective-permute-start | bytes 1671176 | tf_op jit(solution)/shard_map/ppermute | solution.py:24
  51.5 2.0 %shard_map.69.refs_4_ = bf16[2,2,2,80,1024]{4,3,2,1,0:T(8,128)(2,1)S(1)} custom-call(s32[2]{0:T(128)S(1)} %pad_add_fusion.1.place_ref, bf16[272,1024]{1,0:T(8,128)(2,1)S(1)} %get-tuple-element.100.refs_0_.own_ref, bf16[272,1024]{1,0:T(8,128)(2,1)S(1)} %collective-permute-done.6.refs_1_.other_ref), custom_call_target="tpu_custom_call" | custom-call | tf_op jit(solution)/shard_map/pallas_call | solution.py:293
  53.5 2.0 %shard_map.70.refs_5_ = bf16[2,2,2,80,1024]{4,3,2,1,0:T(8,128)(2,1)S(1)} custom-call(s32[2]{0:T(128)S(1)} %pad_add_fusion.1.place_ref, bf16[272,1024]{1,0:T(8,128)(2,1)S(1)} %get-tuple-element.99.refs_2_.own_ref, bf16[272,1024]{1,0:T(8,128)(2,1)S(1)} %collective-permute-done.7.refs_3_.other_ref), custom_call_target="tpu_custom_call" | custom-call | tf_op jit(solution)/shard_map/pallas_call | solution.py:293
  55.6 1.8 %collective-permute-start.11 = (bf16[2,80,128]{2,1,0:T(8,128)(2,1)S(1)}, bf16[2,80,128]{2,1,0:T(8,128)(2,1)S(1)}, u32[]{:S(2)}, u32[]{:S(2)}) collective-permute-start(bf16[2,80,128]{2,1,0:T(8,128)(2,1)S(1)} %get-tuple-element.97), channel_id=1, source_target_pairs={{0,2},{1,3},{2,0},{3,1},{4,6},{5,7},{6,4},{7,5},{8,10},{9,11},{10,... | collective-permute-start | bytes 122888 | tf_op jit(solution)/shard_map/ppermute | solution.py:19
  60.1 2.7 %collective-permute-done.14.own_ref = bf16[272,1024]{1,0:T(8,128)(2,1)S(1)} collective-permute-done((bf16[272,1024]{1,0:T(8,128)(2,1)S(1)}, bf16[272,1024]{1,0:T(8,128)(2,1)S(1)}, u32[]{:S(2)}, u32[]{:S(2)}) %collective-permute-start.14) | collective-permute-done | bytes 557088 | tf_op jit(solution)/shard_map/ppermute | solution.py:24
  62.8 11.5 %collective-permute-done.15.own_ref = bf16[272,1024]{1,0:T(8,128)(2,1)S(1)} collective-permute-done((bf16[272,1024]{1,0:T(8,128)(2,1)S(1)}, bf16[272,1024]{1,0:T(8,128)(2,1)S(1)}, u32[]{:S(2)}, u32[]{:S(2)}) %collective-permute-start.15) | collective-permute-done | bytes 557088 | tf_op jit(solution)/shard_map/ppermute | solution.py:24
  77.0 1.6 %collective-permute-start.16 = (bf16[128,768]{1,0:T(8,128)(2,1)S(1)}, bf16[128,768]{1,0:T(8,128)(2,1)S(1)}, u32[]{:S(2)}, u32[]{:S(2)}) collective-permute-start(bf16[128,768]{1,0:T(8,128)(2,1)S(1)} %get-tuple-element.60), channel_id=1, source_target_pairs={{0,8},{8,0},{16,24},{24,16},{1,9},{9,1},{17,25},{25,17},{2,10},{10... | collective-permute-start | bytes 589832 | tf_op jit(solution)/shard_map/ppermute | solution.py:19
  80.1 2.6 %collective-permute-start.22 = (bf16[272,1024]{1,0:T(8,128)(2,1)S(1)}, bf16[272,1024]{1,0:T(8,128)(2,1)S(1)}, u32[]{:S(2)}, u32[]{:S(2)}) collective-permute-start(bf16[272,1024]{1,0:T(8,128)(2,1)S(1)} %collective-permute-done.14.own_ref), channel_id=1, source_target_pairs={{0,2},{1,3},{2,4},{3,5},{4,6},{5,7},{6,0},{7,1},{8,10},{9,11},{10,... | collective-permute-start | bytes 1671176 | tf_op jit(solution)/shard_map/ppermute | solution.py:24
  82.7 2.5 %collective-permute-start.23 = (bf16[272,1024]{1,0:T(8,128)(2,1)S(1)}, bf16[272,1024]{1,0:T(8,128)(2,1)S(1)}, u32[]{:S(2)}, u32[]{:S(2)}) collective-permute-start(bf16[272,1024]{1,0:T(8,128)(2,1)S(1)} %collective-permute-done.15.own_ref), channel_id=1, source_target_pairs={{0,2},{1,3},{2,4},{3,5},{4,6},{5,7},{6,0},{7,1},{8,10},{9,11},{10,... | collective-permute-start | bytes 1671176 | tf_op jit(solution)/shard_map/ppermute | solution.py:24
  85.1 2.0 %shard_map.72.refs_6_ = bf16[2,2,2,80,1024]{4,3,2,1,0:T(8,128)(2,1)S(1)} custom-call(s32[2]{0:T(128)S(1)} %pad_add_fusion.1.place_ref, bf16[272,1024]{1,0:T(8,128)(2,1)S(1)} %collective-permute-done.14.own_ref, bf16[272,1024]{1,0:T(8,128)(2,1)S(1)} %collective-permute-done.18.other_ref), custom_call_target="tpu_custom_call" | custom-call | tf_op jit(solution)/shard_map/pallas_call | solution.py:293
  88.4 2.0 %shard_map.73.refs_7_ = bf16[2,2,2,80,1024]{4,3,2,1,0:T(8,128)(2,1)S(1)} custom-call(s32[2]{0:T(128)S(1)} %pad_add_fusion.1.place_ref, bf16[272,1024]{1,0:T(8,128)(2,1)S(1)} %collective-permute-done.15.own_ref, bf16[272,1024]{1,0:T(8,128)(2,1)S(1)} %collective-permute-done.21.other_ref), custom_call_target="tpu_custom_call" | custom-call | tf_op jit(solution)/shard_map/pallas_call | solution.py:293
  90.4 3.9 %collective-permute-done.19.first_got_ref = bf16[128,768]{1,0:T(8,128)(2,1)S(1)} collective-permute-done((bf16[128,768]{1,0:T(8,128)(2,1)S(1)}, bf16[128,768]{1,0:T(8,128)(2,1)S(1)}, u32[]{:S(2)}, u32[]{:S(2)}) %collective-permute-start.19) | collective-permute-done | bytes 196640 | tf_op jit(solution)/shard_map/ppermute | solution.py:19
  94.7 8.3 %shard_map.74 = (bf16[640,128]{1,0:T(8,128)(2,1)S(1)}, f32[2,64,1536]{2,1,0:T(8,128)S(1)}) custom-call(bf16[128,768]{1,0:T(8,128)(2,1)S(1)} %add_convert_fusion.1.first_ref, bf16[128,768]{1,0:T(8,128)(2,1)S(1)} %collective-permute-done.19.first_got_ref, bf16[128,768]{1,0:T(8,128)(2,1)S(1)} %add_convert_fusion.last_ref, ...), custom_call_target="tpu_custom_call" | custom-call | tf_op jit(solution)/shard_map/pallas_call | solution.py:254
  103.0 6.7 %collective-permute-done.23.own_ref = bf16[272,1024]{1,0:T(8,128)(2,1)S(1)} collective-permute-done((bf16[272,1024]{1,0:T(8,128)(2,1)S(1)}, bf16[272,1024]{1,0:T(8,128)(2,1)S(1)}, u32[]{:S(2)}, u32[]{:S(2)}) %collective-permute-start.23) | collective-permute-done | bytes 557088 | tf_op jit(solution)/shard_map/ppermute | solution.py:24
  110.2 1.8 %collective-permute-start.30 = (bf16[272,1024]{1,0:T(8,128)(2,1)S(1)}, bf16[272,1024]{1,0:T(8,128)(2,1)S(1)}, u32[]{:S(2)}, u32[]{:S(2)}) collective-permute-start(bf16[272,1024]{1,0:T(8,128)(2,1)S(1)} %collective-permute-done.23.own_ref), channel_id=1, source_target_pairs={{0,2},{1,3},{2,4},{3,5},{4,6},{5,7},{6,0},{7,1},{8,10},{9,11},{10,... | collective-permute-start | bytes 1671176 | tf_op jit(solution)/shard_map/ppermute | solution.py:24
  112.6 5.0 %collective-permute-done.24.refs_1_ = bf16[8,80,128]{2,1,0:T(8,128)(2,1)S(1)} collective-permute-done((bf16[8,80,128]{2,1,0:T(8,128)(2,1)S(1)}, bf16[8,80,128]{2,1,0:T(8,128)(2,1)S(1)}, u32[]{:S(2)}, u32[]{:S(2)}) %collective-permute-start.24) | collective-permute-done | bytes 163872 | tf_op jit(solution)/shard_map/ppermute | solution.py:19
  119.6 2.0 %shard_map.75.refs_8_ = bf16[2,2,2,80,1024]{4,3,2,1,0:T(8,128)(2,1)S(1)} custom-call(s32[2]{0:T(128)S(1)} %pad_add_fusion.1.place_ref, bf16[272,1024]{1,0:T(8,128)(2,1)S(1)} %collective-permute-done.22.own_ref, bf16[272,1024]{1,0:T(8,128)(2,1)S(1)} %collective-permute-done.27.other_ref), custom_call_target="tpu_custom_call" | custom-call | tf_op jit(solution)/shard_map/pallas_call | solution.py:293
  121.6 4.1 %collective-permute-done.25.refs_2_ = bf16[8,80,128]{2,1,0:T(8,128)(2,1)S(1)} collective-permute-done((bf16[8,80,128]{2,1,0:T(8,128)(2,1)S(1)}, bf16[8,80,128]{2,1,0:T(8,128)(2,1)S(1)}, u32[]{:S(2)}, u32[]{:S(2)}) %collective-permute-start.25) | collective-permute-done | bytes 163872 | tf_op jit(solution)/shard_map/ppermute | solution.py:19
  125.8 2.0 %shard_map.76.refs_9_ = bf16[2,2,2,80,1024]{4,3,2,1,0:T(8,128)(2,1)S(1)} custom-call(s32[2]{0:T(128)S(1)} %pad_add_fusion.1.place_ref, bf16[272,1024]{1,0:T(8,128)(2,1)S(1)} %collective-permute-done.23.own_ref, bf16[272,1024]{1,0:T(8,128)(2,1)S(1)} %collective-permute-done.28.other_ref), custom_call_target="tpu_custom_call" | custom-call | tf_op jit(solution)/shard_map/pallas_call | solution.py:293
  127.7 2.4 %shard_map.77.refs_5_ = f32[2,64,1024]{2,1,0:T(8,128)S(1)} custom-call(s32[4]{0:T(128)S(1)} %and_select_fusion.sources_ref, bf16[8,80,128]{2,1,0:T(8,128)(2,1)S(1)} %bitcast.67, bf16[8,80,128]{2,1,0:T(8,128)(2,1)S(1)} %collective-permute-done.24.refs_1_, bf16[8,80,128]{2,1,0:T(8,128)(2,1)S(1)} %collective-permute-done.25.refs_2_, ...), custom_call_target="tpu_custom_call" | custom-call | tf_op jit(solution)/shard_map/pallas_call | solution.py:332
  130.1 8.4 %collective-permute-done.30.own_ref = bf16[272,1024]{1,0:T(8,128)(2,1)S(1)} collective-permute-done((bf16[272,1024]{1,0:T(8,128)(2,1)S(1)}, bf16[272,1024]{1,0:T(8,128)(2,1)S(1)}, u32[]{:S(2)}, u32[]{:S(2)}) %collective-permute-start.30) | collective-permute-done | bytes 557088 | tf_op jit(solution)/shard_map/ppermute | solution.py:24
  139.0 1.6 %dynamic-slice_bitcast_fusion = f32[2,384,64]{1,2,0:T(8,128)} fusion(f32[2,64,1536]{2,1,0:T(8,128)} %copy-done.2, s32[]{:T(128)S(6)} %select_n.71), kind=kLoop, calls=%fused_computation.18 | loop fusion | bytes 393220 | tf_op jit(solution)/shard_map/transpose | solution.py:464
  140.6 2.0 %shard_map.79.refs_4_ = bf16[2,2,2,80,1024]{4,3,2,1,0:T(8,128)(2,1)S(1)} custom-call(s32[2]{0:T(128)S(1)} %pad_add_fusion.1.place_ref, bf16[272,1024]{1,0:T(8,128)(2,1)S(1)} %collective-permute-done.29.own_ref, bf16[272,1024]{1,0:T(8,128)(2,1)S(1)} %collective-permute-done.32.other_ref), custom_call_target="tpu_custom_call" | custom-call | tf_op jit(solution)/shard_map/pallas_call | solution.py:293
  143.6 2.0 %shard_map.78.refs_4_ = bf16[2,2,2,80,1024]{4,3,2,1,0:T(8,128)(2,1)S(1)} custom-call(s32[2]{0:T(128)S(1)} %pad_add_fusion.1.place_ref, bf16[272,1024]{1,0:T(8,128)(2,1)S(1)} %collective-permute-done.30.own_ref, bf16[272,1024]{1,0:T(8,128)(2,1)S(1)} %collective-permute-done.31.other_ref), custom_call_target="tpu_custom_call" | custom-call | tf_op jit(solution)/shard_map/pallas_call | solution.py:293
  145.6 1.8 %shard_map.81 = f32[2,64,1024]{2,1,0:T(8,128)} custom-call(s32[4]{0:T(128)S(1)} %and_select_fusion.sources_ref, bf16[8,80,128]{2,1,0:T(8,128)(2,1)S(1)} %bitcast.69, bf16[8,80,128]{2,1,0:T(8,128)(2,1)S(1)} %collective-permute-done.24.refs_1_, bf16[8,80,128]{2,1,0:T(8,128)(2,1)S(1)} %collective-permute-done.25.refs_2_, ...), custom_call_target="tpu_custom_call" | custom-call | tf_op jit(solution)/shard_map/pallas_call | solution.py:332
  (79 shorter events, 24.4 us)
Async XLA Ops:
  0.6 12.7 %collective-permute-start.3 = (bf16[128,1024]{1,0:T(8,128)(2,1)}, bf16[128,1024]{1,0:T(8,128)(2,1)S(1)}, u32[]{:S(2)}, u32[]{:S(2)}) collective-permute-start(bf16[128,1024]{1,0:T(8,128)(2,1)} %bitcast.70), channel_id=1, source_target_pairs={{0,2},{1,3},{2,0},{3,1},{4,6},{5,7},{6,4},{7,5},{8,10},{9,11},{10,... | collective-permute-start | bytes 786440 | tf_op jit(solution)/shard_map/ppermute | solution.py:19
  7.1 22.6 %collective-permute-start = (bf16[144,1024]{1,0:T(8,128)(2,1)S(1)}, bf16[144,1024]{1,0:T(8,128)(2,1)S(1)}, u32[]{:S(2)}, u32[]{:S(2)}) collective-permute-start(bf16[144,1024]{1,0:T(8,128)(2,1)S(1)} %get-tuple-element.103), channel_id=1, source_target_pairs={{0,8},{8,0},{16,24},{24,16},{1,9},{9,1},{17,25},{25,17},{2,10},{10... | collective-permute-start | bytes 884744 | tf_op jit(solution)/shard_map/ppermute | solution.py:19
  8.7 21.0 %collective-permute-start.1 = (bf16[144,1024]{1,0:T(8,128)(2,1)S(1)}, bf16[144,1024]{1,0:T(8,128)(2,1)S(1)}, u32[]{:S(2)}, u32[]{:S(2)}) collective-permute-start(bf16[144,1024]{1,0:T(8,128)(2,1)S(1)} %get-tuple-element.104), channel_id=1, source_target_pairs={{0,16},{8,24},{16,0},{24,8},{1,17},{9,25},{17,1},{25,9},{2,18},{10... | collective-permute-start | bytes 884744 | tf_op jit(solution)/shard_map/ppermute | solution.py:19
  10.2 19.5 %collective-permute-start.2 = (bf16[144,1024]{1,0:T(8,128)(2,1)S(1)}, bf16[144,1024]{1,0:T(8,128)(2,1)S(1)}, u32[]{:S(2)}, u32[]{:S(2)}) collective-permute-start(bf16[144,1024]{1,0:T(8,128)(2,1)S(1)} %get-tuple-element.101), channel_id=1, source_target_pairs={{0,24},{8,16},{16,8},{24,0},{1,25},{9,17},{17,9},{25,1},{2,26},{10... | collective-permute-start | bytes 884744 | tf_op jit(solution)/shard_map/ppermute | solution.py:19
  10.7 19.0 %collective-permute-start.4 = (bf16[128,1024]{1,0:T(8,128)(2,1)S(1)}, bf16[128,1024]{1,0:T(8,128)(2,1)S(1)}, u32[]{:S(2)}, u32[]{:S(2)}) collective-permute-start(bf16[128,1024]{1,0:T(8,128)(2,1)S(1)} %bitcast.71), channel_id=1, source_target_pairs={{0,4},{1,5},{2,6},{3,7},{4,0},{5,1},{6,2},{7,3},{8,12},{9,13},{10,... | collective-permute-start | bytes 786440 | tf_op jit(solution)/shard_map/ppermute | solution.py:19
  13.3 16.4 %collective-permute-start.5 = (bf16[128,1024]{1,0:T(8,128)(2,1)S(1)}, bf16[128,1024]{1,0:T(8,128)(2,1)S(1)}, u32[]{:S(2)}, u32[]{:S(2)}) collective-permute-start(bf16[128,1024]{1,0:T(8,128)(2,1)S(1)} %bitcast.72), channel_id=1, source_target_pairs={{0,6},{1,7},{2,4},{3,5},{4,2},{5,3},{6,0},{7,1},{8,14},{9,15},{10,... | collective-permute-start | bytes 786440 | tf_op jit(solution)/shard_map/ppermute | solution.py:19
  30.1 2.7 %collective-permute-start.7 = (bf16[272,1024]{1,0:T(8,128)(2,1)S(1)}, bf16[272,1024]{1,0:T(8,128)(2,1)S(1)}, u32[]{:S(2)}, u32[]{:S(2)}) collective-permute-start(bf16[272,1024]{1,0:T(8,128)(2,1)S(1)} %get-tuple-element.99.refs_2_.own_ref), channel_id=1, source_target_pairs={{0,1},{1,0},{2,3},{3,2},{4,5},{5,4},{6,7},{7,6},{8,9},{9,8},{10,11... | collective-permute-start | bytes 1671176 | tf_op jit(solution)/shard_map/ppermute | solution.py:19
  40.0 15.4 %collective-permute-start.8 = (bf16[4,2,80,128]{3,2,1,0:T(8,128)(2,1)S(1)}, bf16[4,2,80,128]{3,2,1,0:T(8,128)(2,1)S(1)}, u32[]{:S(2)}, u32[]{:S(2)}) collective-permute-start(bf16[4,2,80,128]{3,2,1,0:T(8,128)(2,1)S(1)} %get-tuple-element.94), channel_id=1, source_target_pairs={{0,8},{8,0},{16,24},{24,16},{1,9},{9,1},{17,25},{25,17},{2,10},{10... | collective-permute-start | bytes 491528 | tf_op jit(solution)/shard_map/ppermute | solution.py:19
  41.6 13.8 %collective-permute-start.9 = (bf16[4,2,80,128]{3,2,1,0:T(8,128)(2,1)S(1)}, bf16[4,2,80,128]{3,2,1,0:T(8,128)(2,1)S(1)}, u32[]{:S(2)}, u32[]{:S(2)}) collective-permute-start(bf16[4,2,80,128]{3,2,1,0:T(8,128)(2,1)S(1)} %get-tuple-element.93), channel_id=1, source_target_pairs={{0,16},{8,24},{16,0},{24,8},{1,17},{9,25},{17,1},{25,9},{2,18},{10... | collective-permute-start | bytes 491528 | tf_op jit(solution)/shard_map/ppermute | solution.py:19
  43.2 12.3 %collective-permute-start.10 = (bf16[4,2,80,128]{3,2,1,0:T(8,128)(2,1)S(1)}, bf16[4,2,80,128]{3,2,1,0:T(8,128)(2,1)S(1)}, u32[]{:S(2)}, u32[]{:S(2)}) collective-permute-start(bf16[4,2,80,128]{3,2,1,0:T(8,128)(2,1)S(1)} %get-tuple-element.92), channel_id=1, source_target_pairs={{0,24},{8,16},{16,8},{24,0},{1,25},{9,17},{17,9},{25,1},{2,26},{10... | collective-permute-start | bytes 491528 | tf_op jit(solution)/shard_map/ppermute | solution.py:19
  43.6 19.2 %collective-permute-start.14 = (bf16[272,1024]{1,0:T(8,128)(2,1)S(1)}, bf16[272,1024]{1,0:T(8,128)(2,1)S(1)}, u32[]{:S(2)}, u32[]{:S(2)}) collective-permute-start(bf16[272,1024]{1,0:T(8,128)(2,1)S(1)} %get-tuple-element.100.refs_0_.own_ref), channel_id=1, source_target_pairs={{0,2},{1,3},{2,4},{3,5},{4,6},{5,7},{6,0},{7,1},{8,10},{9,11},{10,... | collective-permute-start | bytes 1671176 | tf_op jit(solution)/shard_map/ppermute | solution.py:24
  49.7 24.6 %collective-permute-start.15 = (bf16[272,1024]{1,0:T(8,128)(2,1)S(1)}, bf16[272,1024]{1,0:T(8,128)(2,1)S(1)}, u32[]{:S(2)}, u32[]{:S(2)}) collective-permute-start(bf16[272,1024]{1,0:T(8,128)(2,1)S(1)} %get-tuple-element.99.refs_2_.own_ref), channel_id=1, source_target_pairs={{0,2},{1,3},{2,4},{3,5},{4,6},{5,7},{6,0},{7,1},{8,10},{9,11},{10,... | collective-permute-start | bytes 1671176 | tf_op jit(solution)/shard_map/ppermute | solution.py:24
  55.6 19.1 %collective-permute-start.11 = (bf16[2,80,128]{2,1,0:T(8,128)(2,1)S(1)}, bf16[2,80,128]{2,1,0:T(8,128)(2,1)S(1)}, u32[]{:S(2)}, u32[]{:S(2)}) collective-permute-start(bf16[2,80,128]{2,1,0:T(8,128)(2,1)S(1)} %get-tuple-element.97), channel_id=1, source_target_pairs={{0,2},{1,3},{2,0},{3,1},{4,6},{5,7},{6,4},{7,5},{8,10},{9,11},{10,... | collective-permute-start | bytes 122888 | tf_op jit(solution)/shard_map/ppermute | solution.py:19
  57.4 17.8 %collective-permute-start.12 = (bf16[2,80,128]{2,1,0:T(8,128)(2,1)S(1)}, bf16[2,80,128]{2,1,0:T(8,128)(2,1)S(1)}, u32[]{:S(2)}, u32[]{:S(2)}) collective-permute-start(bf16[2,80,128]{2,1,0:T(8,128)(2,1)S(1)} %get-tuple-element.96), channel_id=1, source_target_pairs={{0,4},{1,5},{2,6},{3,7},{4,0},{5,1},{6,2},{7,3},{8,12},{9,13},{10,... | collective-permute-start | bytes 122888 | tf_op jit(solution)/shard_map/ppermute | solution.py:19
  58.6 17.0 %collective-permute-start.13 = (bf16[2,80,128]{2,1,0:T(8,128)(2,1)S(1)}, bf16[2,80,128]{2,1,0:T(8,128)(2,1)S(1)}, u32[]{:S(2)}, u32[]{:S(2)}) collective-permute-start(bf16[2,80,128]{2,1,0:T(8,128)(2,1)S(1)} %get-tuple-element.95), channel_id=1, source_target_pairs={{0,6},{1,7},{2,4},{3,5},{4,2},{5,3},{6,0},{7,1},{8,14},{9,15},{10,... | collective-permute-start | bytes 122888 | tf_op jit(solution)/shard_map/ppermute | solution.py:19
  75.6 7.1 %collective-permute-start.18 = (bf16[272,1024]{1,0:T(8,128)(2,1)S(1)}, bf16[272,1024]{1,0:T(8,128)(2,1)S(1)}, u32[]{:S(2)}, u32[]{:S(2)}) collective-permute-start(bf16[272,1024]{1,0:T(8,128)(2,1)S(1)} %collective-permute-done.14.own_ref), channel_id=1, source_target_pairs={{0,1},{1,0},{2,3},{3,2},{4,5},{5,4},{6,7},{7,6},{8,9},{9,8},{10,11... | collective-permute-start | bytes 1671176 | tf_op jit(solution)/shard_map/ppermute | solution.py:19
  77.0 10.2 %collective-permute-start.16 = (bf16[128,768]{1,0:T(8,128)(2,1)S(1)}, bf16[128,768]{1,0:T(8,128)(2,1)S(1)}, u32[]{:S(2)}, u32[]{:S(2)}) collective-permute-start(bf16[128,768]{1,0:T(8,128)(2,1)S(1)} %get-tuple-element.60), channel_id=1, source_target_pairs={{0,8},{8,0},{16,24},{24,16},{1,9},{9,1},{17,25},{25,17},{2,10},{10... | collective-permute-start | bytes 589832 | tf_op jit(solution)/shard_map/ppermute | solution.py:19
  78.6 8.6 %collective-permute-start.17 = (bf16[128,768]{1,0:T(8,128)(2,1)S(1)}, bf16[128,768]{1,0:T(8,128)(2,1)S(1)}, u32[]{:S(2)}, u32[]{:S(2)}) collective-permute-start(bf16[128,768]{1,0:T(8,128)(2,1)S(1)} %get-tuple-element.61), channel_id=1, source_target_pairs={{0,16},{8,24},{16,0},{24,8},{1,17},{9,25},{17,1},{25,9},{2,18},{10... | collective-permute-start | bytes 589832 | tf_op jit(solution)/shard_map/ppermute | solution.py:19
  80.1 22.9 %collective-permute-start.22 = (bf16[272,1024]{1,0:T(8,128)(2,1)S(1)}, bf16[272,1024]{1,0:T(8,128)(2,1)S(1)}, u32[]{:S(2)}, u32[]{:S(2)}) collective-permute-start(bf16[272,1024]{1,0:T(8,128)(2,1)S(1)} %collective-permute-done.14.own_ref), channel_id=1, source_target_pairs={{0,2},{1,3},{2,4},{3,5},{4,6},{5,7},{6,0},{7,1},{8,10},{9,11},{10,... | collective-permute-start | bytes 1671176 | tf_op jit(solution)/shard_map/ppermute | solution.py:24
  82.7 5.8 %collective-permute-start.21 = (bf16[272,1024]{1,0:T(8,128)(2,1)S(1)}, bf16[272,1024]{1,0:T(8,128)(2,1)S(1)}, u32[]{:S(2)}, u32[]{:S(2)}) collective-permute-start(bf16[272,1024]{1,0:T(8,128)(2,1)S(1)} %collective-permute-done.15.own_ref), channel_id=1, source_target_pairs={{0,1},{1,0},{2,3},{3,2},{4,5},{5,4},{6,7},{7,6},{8,9},{9,8},{10,11... | collective-permute-start | bytes 1671176 | tf_op jit(solution)/shard_map/ppermute | solution.py:19
  82.7 27.0 %collective-permute-start.23 = (bf16[272,1024]{1,0:T(8,128)(2,1)S(1)}, bf16[272,1024]{1,0:T(8,128)(2,1)S(1)}, u32[]{:S(2)}, u32[]{:S(2)}) collective-permute-start(bf16[272,1024]{1,0:T(8,128)(2,1)S(1)} %collective-permute-done.15.own_ref), channel_id=1, source_target_pairs={{0,2},{1,3},{2,4},{3,5},{4,6},{5,7},{6,0},{7,1},{8,10},{9,11},{10,... | collective-permute-start | bytes 1671176 | tf_op jit(solution)/shard_map/ppermute | solution.py:24
  87.2 7.1 %collective-permute-start.19 = (bf16[128,768]{1,0:T(8,128)(2,1)S(1)}, bf16[128,768]{1,0:T(8,128)(2,1)S(1)}, u32[]{:S(2)}, u32[]{:S(2)}) collective-permute-start(bf16[128,768]{1,0:T(8,128)(2,1)S(1)} %add_convert_fusion.1.first_ref), channel_id=1, source_target_pairs={{0,16},{8,24},{16,0},{24,8},{1,17},{9,25},{17,1},{25,9},{2,18},{10... | collective-permute-start | bytes 589832 | tf_op jit(solution)/shard_map/ppermute | solution.py:19
  87.8 6.8 %collective-permute-start.20 = (bf16[128,768]{1,0:T(8,128)(2,1)S(1)}, bf16[128,768]{1,0:T(8,128)(2,1)S(1)}, u32[]{:S(2)}, u32[]{:S(2)}) collective-permute-start(bf16[128,768]{1,0:T(8,128)(2,1)S(1)} %add_convert_fusion.last_ref), channel_id=1, source_target_pairs={{0,8},{8,0},{16,24},{24,16},{1,9},{9,1},{17,25},{25,17},{2,10},{10... | collective-permute-start | bytes 589832 | tf_op jit(solution)/shard_map/ppermute | solution.py:19
  109.7 8.4 %collective-permute-start.27 = (bf16[272,1024]{1,0:T(8,128)(2,1)S(1)}, bf16[272,1024]{1,0:T(8,128)(2,1)S(1)}, u32[]{:S(2)}, u32[]{:S(2)}) collective-permute-start(bf16[272,1024]{1,0:T(8,128)(2,1)S(1)} %collective-permute-done.22.own_ref), channel_id=1, source_target_pairs={{0,1},{1,0},{2,3},{3,2},{4,5},{5,4},{6,7},{7,6},{8,9},{9,8},{10,11... | collective-permute-start | bytes 1671176 | tf_op jit(solution)/shard_map/ppermute | solution.py:19
  109.7 16.0 %collective-permute-start.28 = (bf16[272,1024]{1,0:T(8,128)(2,1)S(1)}, bf16[272,1024]{1,0:T(8,128)(2,1)S(1)}, u32[]{:S(2)}, u32[]{:S(2)}) collective-permute-start(bf16[272,1024]{1,0:T(8,128)(2,1)S(1)} %collective-permute-done.23.own_ref), channel_id=1, source_target_pairs={{0,1},{1,0},{2,3},{3,2},{4,5},{5,4},{6,7},{7,6},{8,9},{9,8},{10,11... | collective-permute-start | bytes 1671176 | tf_op jit(solution)/shard_map/ppermute | solution.py:19
  110.2 19.9 %collective-permute-start.29 = (bf16[272,1024]{1,0:T(8,128)(2,1)S(1)}, bf16[272,1024]{1,0:T(8,128)(2,1)S(1)}, u32[]{:S(2)}, u32[]{:S(2)}) collective-permute-start(bf16[272,1024]{1,0:T(8,128)(2,1)S(1)} %collective-permute-done.22.own_ref), channel_id=1, source_target_pairs={{0,2},{1,3},{2,4},{3,5},{4,6},{5,7},{6,0},{7,1},{8,10},{9,11},{10,... | collective-permute-start | bytes 1671176 | tf_op jit(solution)/shard_map/ppermute | solution.py:24
  110.2 28.3 %collective-permute-start.30 = (bf16[272,1024]{1,0:T(8,128)(2,1)S(1)}, bf16[272,1024]{1,0:T(8,128)(2,1)S(1)}, u32[]{:S(2)}, u32[]{:S(2)}) collective-permute-start(bf16[272,1024]{1,0:T(8,128)(2,1)S(1)} %collective-permute-done.23.own_ref), channel_id=1, source_target_pairs={{0,2},{1,3},{2,4},{3,5},{4,6},{5,7},{6,0},{7,1},{8,10},{9,11},{10,... | collective-permute-start | bytes 1671176 | tf_op jit(solution)/shard_map/ppermute | solution.py:24
  112.1 5.5 %collective-permute-start.24 = (bf16[8,80,128]{2,1,0:T(8,128)(2,1)S(1)}, bf16[8,80,128]{2,1,0:T(8,128)(2,1)S(1)}, u32[]{:S(2)}, u32[]{:S(2)}) collective-permute-start(bf16[8,80,128]{2,1,0:T(8,128)(2,1)S(1)} %bitcast.64), channel_id=1, source_target_pairs={{0,8},{8,0},{16,24},{24,16},{1,9},{9,1},{17,25},{25,17},{2,10},{10... | collective-permute-start | bytes 491528 | tf_op jit(solution)/shard_map/ppermute | solution.py:19
  117.6 8.1 %collective-permute-start.25 = (bf16[8,80,128]{2,1,0:T(8,128)(2,1)S(1)}, bf16[8,80,128]{2,1,0:T(8,128)(2,1)S(1)}, u32[]{:S(2)}, u32[]{:S(2)}) collective-permute-start(bf16[8,80,128]{2,1,0:T(8,128)(2,1)S(1)} %bitcast.65), channel_id=1, source_target_pairs={{0,16},{8,24},{16,0},{24,8},{1,17},{9,25},{17,1},{25,9},{2,18},{10... | collective-permute-start | bytes 491528 | tf_op jit(solution)/shard_map/ppermute | solution.py:19
  118.1 7.6 %collective-permute-start.26 = (bf16[8,80,128]{2,1,0:T(8,128)(2,1)S(1)}, bf16[8,80,128]{2,1,0:T(8,128)(2,1)S(1)}, u32[]{:S(2)}, u32[]{:S(2)}) collective-permute-start(bf16[8,80,128]{2,1,0:T(8,128)(2,1)S(1)} %bitcast.66), channel_id=1, source_target_pairs={{0,24},{8,16},{16,8},{24,0},{1,25},{9,17},{17,9},{25,1},{2,26},{10... | collective-permute-start | bytes 491528 | tf_op jit(solution)/shard_map/ppermute | solution.py:19
  138.5 2.1 %collective-permute-start.32 = (bf16[272,1024]{1,0:T(8,128)(2,1)S(1)}, bf16[272,1024]{1,0:T(8,128)(2,1)S(1)}, u32[]{:S(2)}, u32[]{:S(2)}) collective-permute-start(bf16[272,1024]{1,0:T(8,128)(2,1)S(1)} %collective-permute-done.29.own_ref), channel_id=1, source_target_pairs={{0,1},{1,0},{2,3},{3,2},{4,5},{5,4},{6,7},{7,6},{8,9},{9,8},{10,11... | collective-permute-start | bytes 1671176 | tf_op jit(solution)/shard_map/ppermute | solution.py:19
  138.5 5.1 %collective-permute-start.31 = (bf16[272,1024]{1,0:T(8,128)(2,1)S(1)}, bf16[272,1024]{1,0:T(8,128)(2,1)S(1)}, u32[]{:S(2)}, u32[]{:S(2)}) collective-permute-start(bf16[272,1024]{1,0:T(8,128)(2,1)S(1)} %collective-permute-done.30.own_ref), channel_id=1, source_target_pairs={{0,1},{1,0},{2,3},{3,2},{4,5},{5,4},{6,7},{7,6},{8,9},{9,8},{10,11... | collective-permute-start | bytes 1671176 | tf_op jit(solution)/shard_map/ppermute | solution.py:19
  (4 other events, 48.5 us)

commit v3 on v2

v3 whole, which is shorter than its diff:
```python
import functools

import jax
import jax.numpy as jnp
from jax import lax
from jax.experimental import pallas as pl
from jax.experimental.pallas import tpu as pltpu
from jax.sharding import PartitionSpec as P

CORES = 2
VMEM = 24 << 20
HIGHEST = lax.Precision.HIGHEST
NT = (((1,), (1,)), ((), ()))
TN = (((0,), (0,)), ((), ()))


def exchange(value, axis, distance):
    size = lax.axis_size(axis)
    return lax.ppermute(value, axis, [(i, i ^ distance) for i in range(size)])


def pieces_kernel(place_ref, cotangent_ref, ids_ref, gates_ref, *out_refs):
    tokens = cotangent_ref.shape[0]
    part = out_refs[0].shape[1]
    experts_all = out_refs[0].shape[0] - tokens
    label = lax.broadcasted_iota(jnp.int32, (experts_all, tokens), 0)
    dense = jnp.zeros((experts_all, tokens), jnp.float32)
    for k in range(ids_ref.shape[0]):
        gate = gates_ref[k : k + 1].astype(jnp.float32)
        dense = dense + jnp.where(label == ids_ref[k : k + 1], gate, 0.0)
    dense = dense.astype(jnp.bfloat16)
    for k, out_ref in enumerate(out_refs):
        start = pl.multiple_of((place_ref[0] ^ k) * part, part)
        out_ref[:tokens] = cotangent_ref[:, pl.ds(start, part)]
        out_ref[tokens:] = jnp.zeros((experts_all, part), jnp.bfloat16)
        out_ref[tokens:, :tokens] = dense


def cut_pieces(place, cotangent, expert_ids, gates, members, experts_all):
    tokens, model_width = cotangent.shape
    shape = jax.ShapeDtypeStruct(
        (tokens + experts_all, model_width // members), jnp.bfloat16
    )
    return pl.pallas_call(
        pieces_kernel,
        out_shape=(shape,) * members,
        in_specs=[pl.BlockSpec(memory_space=pltpu.SMEM)]
        + [pl.BlockSpec(memory_space=pltpu.VMEM)] * 3,
        out_specs=(pl.BlockSpec(memory_space=pltpu.VMEM),) * members,
        compiler_params=pltpu.CompilerParams(vmem_limit_bytes=VMEM),
    )(place, cotangent, jnp.swapaxes(expert_ids, 0, 1), jnp.swapaxes(gates, 0, 1))


def sum_steps(members):
    distances = []
    step = 1
    while step < members:
        distances.append(step)
        step *= 2
    return distances, distances[::-1]


def slots_of(gates):
    tokens = gates.shape[1]
    before = (
        lax.broadcasted_iota(jnp.int32, (tokens, tokens), 0)
        < lax.broadcasted_iota(jnp.int32, (tokens, tokens), 1)
    ).astype(jnp.bfloat16)
    named = (gates > 0).astype(jnp.bfloat16)
    slot = jnp.dot(named, before, preferred_element_type=jnp.float32)
    return jnp.where(gates > 0, slot, -1.0)


def aligned(value, multiple):
    return value if isinstance(value, int) else pl.multiple_of(value, multiple)


def columns_of(ref, first, group, sizes):
    tokens = sizes[1]
    return ref[pl.ds(aligned(first + group * tokens, 16), tokens), :]


def gates_of(ref, group, sizes):
    _, tokens, _, _, experts_all = sizes
    chunks = ref.shape[1] // tokens
    row = aligned(group // chunks * experts_all, 16)
    return ref[pl.ds(row, experts_all), pl.ds(aligned(group % chunks * tokens, tokens), tokens)]


def for_each(count, body):
    if count <= 4:
        for index in range(count):
            body(index)
        return

    def step(index, carry):
        body(index)
        return carry

    lax.fori_loop(0, count, step, 0)


def project_kernel(sizes, place_ref, block_ref, factors_ref, *refs):
    members, tokens, held, rank, experts_all = sizes
    out_ref = refs[-1]
    cores, padded = out_ref.shape[2:4]
    wide = held * rank
    chips = out_ref.shape[1]
    count = chips * held
    first = block_ref.shape[0] - members * tokens
    index = lax.broadcasted_iota(jnp.int32, (count, experts_all), 0)
    owner = place_ref[0] ^ (chips - 1 - index // held)
    owner = (owner * CORES + place_ref[1]) * held + index % held
    pick = (lax.broadcasted_iota(jnp.int32, owner.shape, 1) == owner).astype(jnp.bfloat16)
    row = lax.broadcasted_iota(jnp.int32, (padded, tokens), 0).astype(jnp.float32)
    lane = lax.broadcasted_iota(jnp.int32, (padded, wide), 1)
    if cores > 1:
        out_ref[:, :, 0] = refs[0][:, :, 0]
    batch = min(4, members)

    def one_batch(number):
        base = number * batch
        dense = [gates_of(block_ref, base + g, sizes) for g in range(batch)]
        gates = jnp.dot(pick, jnp.concatenate(dense, 1), preferred_element_type=jnp.float32)
        slot = slots_of(
            jnp.concatenate([gates[:, g * tokens : (g + 1) * tokens] for g in range(batch)])
        )
        start = aligned(first + base * tokens, 16)
        y = lax.dot_general(
            factors_ref[...],
            block_ref[pl.ds(start, batch * tokens), :],
            NT,
            preferred_element_type=jnp.float32,
        )
        weighted = [
            (y[i * rank : (i + 1) * rank] * gates[i : i + 1]).astype(jnp.bfloat16)
            for i in range(count)
        ]
        for g in range(batch):
            here = slice(g * tokens, (g + 1) * tokens)
            for k in range(chips):
                mine = range(k * held, (k + 1) * held)
                choice = [
                    jnp.where(slot[g * count + i : g * count + i + 1] == row, 1.0, 0.0)
                    for i in mine
                ]
                full = lax.dot_general(
                    jnp.concatenate(choice).astype(jnp.bfloat16),
                    jnp.concatenate([weighted[i][:, here] for i in mine]),
                    NT,
                    preferred_element_type=jnp.float32,
                )
                packed = full[:padded]
                for h in range(1, held):
                    packed = jnp.where(
                        lane >= h * rank, full[h * padded : (h + 1) * padded], packed
                    )
                out_ref[base + g, k, cores - 1] = packed.astype(jnp.bfloat16)

    for_each(members // batch, one_batch)


def project(place, block, factors, sizes, padded, before=None):
    members, tokens, held, rank, _ = sizes
    wide = held * rank
    chips = factors.shape[0] // wide
    cores = 1 if before is None else CORES
    operands = [block, factors] + ([] if before is None else [before])
    return pl.pallas_call(
        functools.partial(project_kernel, sizes),
        out_shape=jax.ShapeDtypeStruct((members, chips, cores, padded, wide), jnp.bfloat16),
        in_specs=[pl.BlockSpec(memory_space=pltpu.SMEM)]
        + [pl.BlockSpec(memory_space=pltpu.VMEM)] * len(operands),
        out_specs=pl.BlockSpec(memory_space=pltpu.VMEM),
        compiler_params=pltpu.CompilerParams(vmem_limit_bytes=VMEM),
    )(place, *operands)


def left_kernel(place_ref, *refs):
    arrived, hidden_ref, outs, rows_ref = refs[:-4], refs[-4], refs[-3:-1], refs[-1]
    for k, ref in enumerate(arrived):
        base = (place_ref[0] ^ k) * CORES
        rows_ref[base + place_ref[1]] = ref[0]
        rows_ref[base + 1 - place_ref[1]] = ref[1]
    places, capacity, wide = rows_ref.shape
    held = hidden_ref.shape[0]
    rank = wide // held
    rows = rows_ref[...].reshape(places * capacity, wide)
    half = outs[0].shape[1]
    for h in range(held):
        for index, out_ref in enumerate(outs):
            product = lax.dot_general(
                rows,
                hidden_ref[h, :, index * half : (index + 1) * half],
                TN,
                preferred_element_type=jnp.float32,
            )
            out_ref[h * rank : (h + 1) * rank] = product[h * rank : (h + 1) * rank]


def left_partial(place, arrived, own_hidden, capacity):
    held, slots, width = own_hidden.shape
    _, padded, wide = arrived[0].shape
    if padded != capacity:
        chips = len(arrived)
        rows = jnp.take(jnp.stack(arrived), jnp.arange(chips) ^ place[0], axis=0)
        rows = jnp.take(rows, jnp.arange(CORES) ^ place[1], axis=1)[:, :, :capacity]
        rows = rows.reshape(slots, held, wide // held)
        value = jnp.einsum("shr,hsf->hrf", rows, own_hidden, preferred_element_type=jnp.float32)
        value = value.reshape(wide, width)
        return [value[:, : width // 2], value[:, width // 2 :]]
    shape = jax.ShapeDtypeStruct((wide, width // 2), jnp.float32)
    return pl.pallas_call(
        left_kernel,
        out_shape=(shape, shape),
        in_specs=[pl.BlockSpec(memory_space=pltpu.SMEM)]
        + [pl.BlockSpec(memory_space=pltpu.VMEM)] * (len(arrived) + 1),
        out_specs=(pl.BlockSpec(memory_space=pltpu.VMEM),) * 2,
        scratch_shapes=[pltpu.VMEM((slots // capacity, capacity, wide), jnp.bfloat16)],
        compiler_params=pltpu.CompilerParams(vmem_limit_bytes=VMEM),
    )(place, *arrived, own_hidden)


def whiten_kernel(first_ref, first_got_ref, last_ref, last_got_ref, hidden_ref, mapped_ref, merged_ref):
    held, rank, width = merged_ref.shape
    half = width // 2
    for h in range(held):
        rows = slice(h * rank, (h + 1) * rank)
        merged_ref[h, :, :half] = first_ref[rows] + first_got_ref[rows].astype(
            jnp.float32
        )
        merged_ref[h, :, half:] = last_ref[rows] + last_got_ref[rows].astype(
            jnp.float32
        )
    lane = lax.broadcasted_iota(jnp.int32, (8, 2 * rank), 1)
    row = lax.broadcasted_iota(jnp.int32, (8, 2 * rank), 0)
    blocks = rank // 8
    states = []
    for h in range(held):
        factor = merged_ref[h]
        gram = lax.dot_general(
            factor, factor, NT, precision=HIGHEST, preferred_element_type=jnp.float32
        )
        padded = jnp.concatenate([gram, jnp.zeros_like(gram)], axis=1)
        states.append(
            [
                jnp.where(lane == rank + 8 * b + row, 1.0, padded[8 * b : 8 * b + 8])
                for b in range(blocks)
            ]
        )
    for k in range(rank):
        first, inner = k // 8, k % 8
        for state in states:
            pivot_column = jnp.broadcast_to(state[first][:, k : k + 1], (8, 2 * rank))
            scaled = state[first][inner : inner + 1] / pivot_column[inner : inner + 1]
            for b in range(first, blocks):
                column = pivot_column
                if b == first:
                    column = jnp.where(row > inner, column, 0.0)
                else:
                    column = jnp.broadcast_to(state[b][:, k : k + 1], (8, 2 * rank))
                state[b] = state[b] - column * scaled
    for h in range(held):
        inverse = []
        for b, block in enumerate(states[h]):
            pivot = jnp.sum(jnp.where(lane == 8 * b + row, block, 0.0), axis=1, keepdims=True)
            inverse.append(block[:, rank:] / jnp.sqrt(pivot))
        inverse = jnp.concatenate(inverse, axis=0)
        basis = jnp.dot(
            inverse, merged_ref[h], precision=HIGHEST, preferred_element_type=jnp.float32
        ).astype(jnp.bfloat16)
        mapped_ref[:, h * rank : (h + 1) * rank] = lax.dot_general(
            hidden_ref[h], basis, NT, preferred_element_type=jnp.float32
        ).astype(jnp.bfloat16)


def whiten_and_map(parts, own_hidden):
    held, slots, width = own_hidden.shape
    wide = parts[0].shape[0]
    return pl.pallas_call(
        whiten_kernel,
        out_shape=(
            jax.ShapeDtypeStruct((slots, wide), jnp.bfloat16),
            jax.ShapeDtypeStruct((held, wide // held, width), jnp.float32),
        ),
        compiler_params=pltpu.CompilerParams(vmem_limit_bytes=VMEM),
    )(*parts, own_hidden)


def dispatch_kernel(sizes, place_ref, block_ref, out_ref):
    members, tokens, held, _, experts_all = sizes
    count, _, padded, _ = out_ref.shape
    first = block_ref.shape[0] - members * tokens
    row = lax.broadcasted_iota(jnp.int32, (padded, tokens), 0).astype(jnp.float32)
    index = lax.broadcasted_iota(jnp.int32, (max(8, count), experts_all), 0)
    owner = place_ref[0] ^ (index // held * (2 * CORES))
    pick = lax.broadcasted_iota(jnp.int32, index.shape, 1) == owner * held + index % held
    pick = pick.astype(jnp.bfloat16)

    def one_group(g):
        gates = jnp.dot(pick, gates_of(block_ref, g, sizes), preferred_element_type=jnp.float32)
        slot = slots_of(gates)
        choice = [jnp.where(slot[i : i + 1] == row, gates[i : i + 1], 0.0) for i in range(count)]
        rows = jnp.dot(
            jnp.concatenate(choice).astype(jnp.bfloat16),
            columns_of(block_ref, first, g, sizes),
            preferred_element_type=jnp.float32,
        ).astype(jnp.bfloat16)
        for i in range(count):
            out_ref[i, g] = rows[i * padded : (i + 1) * padded]

    for_each(members, one_group)


def dispatch(place, block, sizes, padded, owners):
    members, _, held, _, _ = sizes
    return pl.pallas_call(
        functools.partial(dispatch_kernel, sizes),
        out_shape=jax.ShapeDtypeStruct(
            (owners * held, members, padded, block.shape[1]), jnp.bfloat16
        ),
        in_specs=[
            pl.BlockSpec(memory_space=pltpu.SMEM),
            pl.BlockSpec(memory_space=pltpu.VMEM),
        ],
        out_specs=pl.BlockSpec(memory_space=pltpu.VMEM),
        compiler_params=pltpu.CompilerParams(vmem_limit_bytes=VMEM),
    )(place, block)


def right_kernel(members, owner, where_ref, *refs):
    mapped, slabs, out_ref = refs[:members], refs[members:-1], refs[-1]
    held, rank, _ = out_ref.shape
    batch = min(4, members)
    for h in range(held):
        total = None
        for base in range(0, members, batch):
            groups = range(base, base + batch)
            rows = [mapped[g][where_ref[b]] for g in groups for b in range(len(slabs))]
            columns = [slab[owner * held + h, g] for g in groups for slab in slabs]
            product = lax.dot_general(
                jnp.concatenate(rows),
                jnp.concatenate(columns),
                TN,
                preferred_element_type=jnp.float32,
            )[h * rank : (h + 1) * rank]
            total = product if total is None else total + product
        out_ref[h] = total.astype(out_ref.dtype)


def right_factor(where, mapped_groups, slabs, owner, sizes, kind):
    _, _, held, rank, _ = sizes
    operands = [*mapped_groups, *slabs]
    return pl.pallas_call(
        functools.partial(right_kernel, len(mapped_groups), owner),
        out_shape=jax.ShapeDtypeStruct((held, rank, slabs[0].shape[-1]), kind),
        in_specs=[pl.BlockSpec(memory_space=pltpu.SMEM)]
        + [pl.BlockSpec(memory_space=pltpu.VMEM)] * len(operands),
        out_specs=pl.BlockSpec(memory_space=pltpu.VMEM),
        compiler_params=pltpu.CompilerParams(vmem_limit_bytes=VMEM),
    )(where, *operands)


def local(cotangent, expert_ids, gates, hidden, q_prev):
    members = lax.axis_size("dp")
    places = lax.axis_size("expert")
    chips = places // CORES
    held, _, slots, width = hidden.shape
    rank = q_prev.shape[2]
    tokens, model_width = cotangent.shape
    experts_all = held * places
    capacity = slots // places
    padded = -(-capacity // 16) * 16
    part = model_width // members
    chunks = part // tokens
    sizes = (members, tokens, held, rank, experts_all)
    my_dp = lax.axis_index("dp")
    my_place = lax.axis_index("expert")
    my_chip, my_core = my_place // CORES, my_place % CORES
    place = jnp.stack([my_chip, my_core]).astype(jnp.int32)
    own_hidden = hidden[:, 0]
    tie = lax.optimization_barrier

    def swap(block):
        return exchange(block, "expert", 1)

    pieces = cut_pieces(
        my_dp.reshape(1).astype(jnp.int32), cotangent, expert_ids, gates, members, experts_all
    )
    pieces = [exchange(piece, "dp", k) if k else piece for k, piece in enumerate(pieces)]
    factor = jnp.swapaxes(q_prev, 1, 2).reshape(held * rank, part)
    factors = [factor] + [exchange(factor, "expert", CORES * k) for k in range(1, chips)]

    factors = jnp.concatenate(factors[::-1])
    pieces, factors = tie((pieces, factors))
    tails = [piece[tokens:, :tokens] for piece in pieces]
    while len(tails) % chunks:
        tails.append(jnp.zeros_like(tails[0]))
    tails = [jnp.concatenate(tails[i : i + chunks], 1) for i in range(0, len(tails), chunks)]
    own = jnp.concatenate(tails + [piece[:tokens] for piece in pieces], axis=0)

    span = min(2, chips)
    owners = chips // span

    def spread(block):
        return dispatch(my_place.reshape(1).astype(jnp.int32), block, sizes, padded, owners)

    y = project(place, own, factors, sizes, padded)
    y, own = tie((y, own))
    other = swap(own)
    y = project(place, other, factors, sizes, padded, y)
    got = [exchange(y[d], "dp", d) for d in range(1, members)]
    slabs = [spread(own), spread(other)]
    got, slabs = tie((got, slabs))
    summed = y[0].astype(jnp.float32)
    for value in got:
        summed = summed + value.astype(jnp.float32)
    summed = summed.astype(jnp.bfloat16)[::-1]
    arrived = [summed[0]] + [exchange(summed[k], "expert", CORES * k) for k in range(1, chips)]
    parts = left_partial(place, arrived, own_hidden, capacity)
    if span > 1:
        parts, own = tie((parts, own))
        near = exchange(own, "expert", CORES)
    turns = sum_steps(members)
    rounds = len(turns[0])
    for index in range(rounds):
        if index:
            parts = [p + q.astype(jnp.float32) for p, q in zip(parts, got)]
        got = [
            exchange(p.astype(jnp.bfloat16), "dp", turn[index]) for p, turn in zip(parts, turns)
        ]
    mapped, merged = whiten_and_map([parts[0], got[0], parts[1], got[1]], own_hidden)
    mapped = mapped.reshape(places, capacity, held * rank)
    mapped = jnp.pad(mapped, ((0, 0), (0, padded - capacity), (0, 0)))
    if span > 1:
        mapped, near = tie((mapped, near))
        near_other = swap(near)

    def rows_for(chip):
        return lax.dynamic_slice_in_dim(mapped, chip // span * span * CORES, span * CORES, 0)

    def over_groups(value):
        return [value] + [exchange(value, "dp", d) for d in range(1, members)]

    sent = [
        exchange(rows_for(my_chip ^ (span * m)), "expert", span * m * CORES)
        for m in range(1, owners)
    ]
    if span > 1:
        slab = spread(near)
        if owners > 1:
            sent, slab = tie((sent, slab))
        slabs.append(slab)
    gathered = [over_groups(value) for value in sent]
    if span > 1:
        slab = spread(near_other)
        if owners > 1:
            gathered, slab = tie((gathered, slab))
        slabs.append(slab)
    where = jnp.stack([my_chip % span, my_chip % span, (my_chip ^ 1) % span, (my_chip ^ 1) % span])
    where = where * CORES + jnp.stack([my_core, 1 - my_core, my_core, 1 - my_core])
    where = where.astype(jnp.int32)

    def product(groups, owner, kind):
        return right_factor(where, groups, slabs, owner, sizes, kind)

    parts = [product(groups, m, jnp.bfloat16) for m, groups in enumerate(gathered, 1)]
    mine = rows_for(my_chip)
    if owners > 1:
        mine, parts = tie((mine, parts))
    parts = [exchange(value, "expert", span * m * CORES) for m, value in enumerate(parts, 1)]
    q_next = product(over_groups(mine), 0, jnp.float32)
    for value in parts:
        q_next = q_next + value.astype(jnp.float32)
    share = width // members
    p_share = lax.dynamic_slice_in_dim(merged, my_dp * share, share, 2)
    return (jnp.swapaxes(p_share, 1, 2), jnp.swapaxes(q_next, 1, 2))


def solution(mesh):
    placed = (
        P(("dp", "expert"), None),
        P(("dp", "expert"), None),
        P(("dp", "expert"), None),
        P("expert", "dp", None, None),
        P("expert", "dp", None),
    )
    return jax.shard_map(
        local,
        mesh=mesh,
        in_specs=placed,
        out_specs=(P("expert", "dp", None), P("expert", "dp", None)),
        check_vma=False,
    )
```

time: 148 us -> 116 us (0.78)
  waiting for transfers between devices: 61.8 us -> 33.6 us
  Pallas kernels: 37.9 us -> 26 us
  local copies, waits for them, and re-layouts: 5.02 us -> 16.9 us
  starting transfers between devices: 41.1 us -> 36.4 us
    ppermute x6 -> x0, waiting for transfers between devices: 29.3 us -> none  [shift(): lax.ppermute(value, axis, [(i, (i + distance) % size) for i in range(size)])]
    ppermute x6 -> x0, starting transfers between devices: 14.7 us -> none  [shift(): lax.ppermute(value, axis, [(i, (i + distance) % size) for i in range(size)])]
    unnamed x6 -> x34, local copies, waits for them, and re-layouts: 0.01 us -> 14.3 us
    ppermute x27, starting transfers between devices: 26.4 us -> 36.4 us  [exchange(): return lax.ppermute(value, axis, [(i, i ^ distance) for i in range(size)])]
    pallas_call x4 -> x5, Pallas kernels: 12.4 us -> 6.39 us  [the longest x2 3.44 us: project(): pl.pallas_call(functools.partial(project_kernel, sizes), out_shape=jax.Sh...]
    pallas_call x8 -> x4, Pallas kernels: 15.9 us -> 9.94 us  [dispatch(): pl.pallas_call(functools.partial(dispatch_kernel, sizes), out_shape=jax.S...]
  transfers between devices with their start and end apart: 33 -> 27, of which waited for: 14 -> 16; matrix products, arithmetic and copies ran while one was open for 4% -> 2% of each run, Pallas kernels for 18% -> 17%
where the time goes in v3:
time: 116 us; the launch traced here: 115 us
  starting transfers between devices  36.4 us (31%)
  waiting for transfers between devices  33.6 us (29%)
  Pallas kernels  26 us (22%)
  local copies, waits for them, and re-layouts  16.9 us (15%)
  other arithmetic  1.32 us (1%)
    ppermute x27, starting transfers between devices, exchange(): return lax.ppermute(value, axis, [(i, i ^ distance) for i in range(size)])  36.4 us
    ppermute x27, waiting for transfers between devices, exchange(): return lax.ppermute(value, axis, [(i, i ^ distance) for i in range(size)])  33.6 us
    unnamed x34, local copies, waits for them, and re-layouts  14.3 us
    pallas_call x4, Pallas kernels, dispatch(): pl.pallas_call(functools.partial(dispatch_kernel, sizes), out_shape=jax.S...  9.94 us
    pallas_call x1, Pallas kernels, whiten_and_map(): pl.pallas_call(whiten_kernel, out_shape=(jax.ShapeDtypeStruct((slots, wid...  8.32 us
    pallas_call x2, Pallas kernels, project(): pl.pallas_call(functools.partial(project_kernel, sizes), out_shape=jax.Sh...  3.44 us
    pallas_call x2, Pallas kernels, right_factor(): pl.pallas_call(functools.partial(right_kernel, len(mapped_groups), owner)...  2.87 us
  transfers between devices with their start and end apart: 27, of which 16 were waited for; matrix products, arithmetic and copies ran while one was open for 2% of the time, Pallas kernels for 17%

profile of v3, /device:TPU:0, one launch (start us, length us, event | category | flops | bytes accessed | tf_op | source)
XLA Modules:
  0.0 115.2 jit_solution(8638548212932614698)
XLA Ops:
  0.6 3.1 %collective-permute-start.5 = (bf16[128,1024]{1,0:T(8,128)(2,1)}, bf16[128,1024]{1,0:T(8,128)(2,1)S(1)}, u32[]{:S(2)}, u32[]{:S(2)}) collective-permute-start(bf16[128,1024]{1,0:T(8,128)(2,1)} %bitcast.42), channel_id=1, source_target_pairs={{0,2},{1,3},{2,0},{3,1},{4,6},{5,7},{6,4},{7,5},{8,10},{9,11},{10,... | collective-permute-start | bytes 786440 | tf_op jit(solution)/shard_map/ppermute | solution.py:19
  3.7 2.6 %collective-permute-start.4 = (bf16[128,1024]{1,0:T(8,128)(2,1)}, bf16[128,1024]{1,0:T(8,128)(2,1)S(1)}, u32[]{:S(2)}, u32[]{:S(2)}) collective-permute-start(bf16[128,1024]{1,0:T(8,128)(2,1)} %bitcast.43), channel_id=1, source_target_pairs={{0,4},{1,5},{2,6},{3,7},{4,0},{5,1},{6,2},{7,3},{8,12},{9,13},{10,... | collective-permute-start | bytes 786440 | tf_op jit(solution)/shard_map/ppermute | solution.py:19
  9.0 1.8 %collective-permute-start = (bf16[144,1024]{1,0:T(8,128)(2,1)S(1)}, bf16[144,1024]{1,0:T(8,128)(2,1)}, u32[]{:S(2)}, u32[]{:S(2)}) collective-permute-start(bf16[144,1024]{1,0:T(8,128)(2,1)S(1)} %get-tuple-element.37), channel_id=1, source_target_pairs={{0,8},{8,0},{16,24},{24,16},{1,9},{9,1},{17,25},{25,17},{2,10},{10... | collective-permute-start | bytes 884744 | tf_op jit(solution)/shard_map/ppermute | solution.py:19
  10.8 1.5 %collective-permute-start.1 = (bf16[144,1024]{1,0:T(8,128)(2,1)S(1)}, bf16[144,1024]{1,0:T(8,128)(2,1)}, u32[]{:S(2)}, u32[]{:S(2)}) collective-permute-start(bf16[144,1024]{1,0:T(8,128)(2,1)S(1)} %get-tuple-element.38), channel_id=1, source_target_pairs={{0,16},{8,24},{16,0},{24,8},{1,17},{9,25},{17,1},{25,9},{2,18},{10... | collective-permute-start | bytes 884744 | tf_op jit(solution)/shard_map/ppermute | solution.py:19
  12.3 2.8 %collective-permute-done.5 = bf16[128,1024]{1,0:T(8,128)(2,1)S(1)} collective-permute-done((bf16[128,1024]{1,0:T(8,128)(2,1)}, bf16[128,1024]{1,0:T(8,128)(2,1)S(1)}, u32[]{:S(2)}, u32[]{:S(2)}) %collective-permute-start.5) | collective-permute-done | bytes 262176 | tf_op jit(solution)/shard_map/ppermute | solution.py:19
  15.1 2.6 %collective-permute-start.2 = (bf16[144,1024]{1,0:T(8,128)(2,1)S(1)}, bf16[144,1024]{1,0:T(8,128)(2,1)}, u32[]{:S(2)}, u32[]{:S(2)}) collective-permute-start(bf16[144,1024]{1,0:T(8,128)(2,1)S(1)} %get-tuple-element.39), channel_id=1, source_target_pairs={{0,24},{8,16},{16,8},{24,0},{1,25},{9,17},{17,9},{25,1},{2,26},{10... | collective-permute-start | bytes 884744 | tf_op jit(solution)/shard_map/ppermute | solution.py:19
  17.8 7.5 %collective-permute-done.4 = bf16[128,1024]{1,0:T(8,128)(2,1)S(1)} collective-permute-done((bf16[128,1024]{1,0:T(8,128)(2,1)}, bf16[128,1024]{1,0:T(8,128)(2,1)S(1)}, u32[]{:S(2)}, u32[]{:S(2)}) %collective-permute-start.4) | collective-permute-done | bytes 262176 | tf_op jit(solution)/shard_map/ppermute | solution.py:19
  30.4 1.7 %shard_map.69.refs_0_ = bf16[4,4,1,80,128]{4,3,2,1,0:T(8,128)(2,1)S(1)} custom-call(s32[2]{0:T(128)S(1)} %pad_add_fusion.place_ref, bf16[528,1024]{1,0:T(8,128)(2,1)S(1)} %slice_dynamic-update-slice_fusion.block_ref, bf16[512,1024]{1,0:T(8,128)(2,1)S(1)} %pad_maximum_fusion.factors_ref), custom_call_target="tpu_custom_call" | custom-call | tf_op jit(solution)/shard_map/pallas_call | solution.py:169
  32.2 2.7 %collective-permute-done.6.block_ref = bf16[528,1024]{1,0:T(8,128)(2,1)S(1)} collective-permute-done((bf16[528,1024]{1,0:T(8,128)(2,1)S(1)}, bf16[528,1024]{1,0:T(8,128)(2,1)S(1)}, u32[]{:S(2)}, u32[]{:S(2)}) %collective-permute-start.6) | collective-permute-done | bytes 1081376 | tf_op jit(solution)/shard_map/ppermute | solution.py:19
  34.9 1.7 %shard_map.70 = bf16[4,4,2,80,128]{4,3,2,1,0:T(8,128)(2,1)S(1)} custom-call(s32[2]{0:T(128)S(1)} %pad_add_fusion.place_ref, bf16[528,1024]{1,0:T(8,128)(2,1)S(1)} %collective-permute-done.6.block_ref, bf16[512,1024]{1,0:T(8,128)(2,1)S(1)} %pad_maximum_fusion.factors_ref, bf16[4,4,1,80,128]{4,3,2,1,0:T(8,128)(2,1)S(1)} %shard_map.69.refs_0_), custom_call_target="tpu_custom_call" | custom-call | tf_op jit(solution)/shard_map/pallas_call | solution.py:169
  36.7 2.5 %collective-permute-start.9 = (bf16[4,2,80,128]{3,2,1,0:T(8,128)(2,1)S(1)}, bf16[4,2,80,128]{3,2,1,0:T(8,128)(2,1)S(1)}, u32[]{:S(2)}, u32[]{:S(2)}) collective-permute-start(bf16[4,2,80,128]{3,2,1,0:T(8,128)(2,1)S(1)} %get-tuple-element.74), channel_id=1, source_target_pairs={{0,24},{8,16},{16,8},{24,0},{1,25},{9,17},{17,9},{25,1},{2,26},{10... | collective-permute-start | bytes 491528 | tf_op jit(solution)/shard_map/ppermute | solution.py:19
  40.2 1.8 %shard_map.71.refs_4_ = bf16[4,4,80,1024]{3,2,1,0:T(8,128)(2,1)S(1)} custom-call(s32[1]{0:T(128)} %bitcast.12.place_ref, bf16[528,1024]{1,0:T(8,128)(2,1)S(1)} %slice_dynamic-update-slice_fusion.block_ref), custom_call_target="tpu_custom_call" | custom-call | tf_op jit(solution)/shard_map/pallas_call | solution.py:317
  42.0 1.8 %shard_map.72.refs_5_ = bf16[4,4,80,1024]{3,2,1,0:T(8,128)(2,1)S(1)} custom-call(s32[1]{0:T(128)} %bitcast.12.place_ref, bf16[528,1024]{1,0:T(8,128)(2,1)S(1)} %collective-permute-done.6.block_ref), custom_call_target="tpu_custom_call" | custom-call | tf_op jit(solution)/shard_map/pallas_call | solution.py:317
  45.3 2.1 %collective-permute-done.8 = bf16[4,2,80,128]{3,2,1,0:T(8,128)(2,1)S(1)} collective-permute-done((bf16[4,2,80,128]{3,2,1,0:T(8,128)(2,1)S(1)}, bf16[4,2,80,128]{3,2,1,0:T(8,128)(2,1)S(1)}, u32[]{:S(2)}, u32[]{:S(2)}) %collective-permute-start.8) | collective-permute-done | bytes 163872 | tf_op jit(solution)/shard_map/ppermute | solution.py:19
  47.6 3.1 %collective-permute-start.12 = (bf16[2,80,128]{2,1,0:T(8,128)(2,1)S(1)}, bf16[2,80,128]{2,1,0:T(8,128)(2,1)S(1)}, u32[]{:S(2)}, u32[]{:S(2)}) collective-permute-start(bf16[2,80,128]{2,1,0:T(8,128)(2,1)S(1)} %get-tuple-element.79), channel_id=1, source_target_pairs={{0,6},{1,7},{2,4},{3,5},{4,2},{5,3},{6,0},{7,1},{8,14},{9,15},{10,... | collective-permute-start | bytes 122888 | tf_op jit(solution)/shard_map/ppermute | solution.py:19
  50.7 3.2 %collective-permute-start.11 = (bf16[2,80,128]{2,1,0:T(8,128)(2,1)S(1)}, bf16[2,80,128]{2,1,0:T(8,128)(2,1)S(1)}, u32[]{:S(2)}, u32[]{:S(2)}) collective-permute-start(bf16[2,80,128]{2,1,0:T(8,128)(2,1)S(1)} %get-tuple-element.80), channel_id=1, source_target_pairs={{0,4},{1,5},{2,6},{3,7},{4,0},{5,1},{6,2},{7,3},{8,12},{9,13},{10,... | collective-permute-start | bytes 122888 | tf_op jit(solution)/shard_map/ppermute | solution.py:19
  54.0 2.4 %collective-permute-done.11.refs_2_ = bf16[2,80,128]{2,1,0:T(8,128)(2,1)S(1)} collective-permute-done((bf16[2,80,128]{2,1,0:T(8,128)(2,1)S(1)}, bf16[2,80,128]{2,1,0:T(8,128)(2,1)S(1)}, u32[]{:S(2)}, u32[]{:S(2)}) %collective-permute-start.11) | collective-permute-done | bytes 40992 | tf_op jit(solution)/shard_map/ppermute | solution.py:19
  62.7 3.4 %collective-permute-done.15 = bf16[128,768]{1,0:T(8,128)(2,1)S(1)} collective-permute-done((bf16[128,768]{1,0:T(8,128)(2,1)S(1)}, bf16[128,768]{1,0:T(8,128)(2,1)S(1)}, u32[]{:S(2)}, u32[]{:S(2)}) %collective-permute-start.15) | collective-permute-done | bytes 196640 | tf_op jit(solution)/shard_map/ppermute | solution.py:19
  66.2 1.6 %collective-permute-start.16 = (bf16[128,768]{1,0:T(8,128)(2,1)S(1)}, bf16[128,768]{1,0:T(8,128)(2,1)S(1)}, u32[]{:S(2)}, u32[]{:S(2)}) collective-permute-start(bf16[128,768]{1,0:T(8,128)(2,1)S(1)} %get-tuple-element.70), channel_id=1, source_target_pairs={{0,8},{8,0},{16,24},{24,16},{1,9},{9,1},{17,25},{25,17},{2,10},{10... | collective-permute-start | bytes 589832 | tf_op jit(solution)/shard_map/ppermute | solution.py:19
  69.1 2.8 %collective-permute-done.16.last_got_ref = bf16[128,768]{1,0:T(8,128)(2,1)S(1)} collective-permute-done((bf16[128,768]{1,0:T(8,128)(2,1)S(1)}, bf16[128,768]{1,0:T(8,128)(2,1)S(1)}, u32[]{:S(2)}, u32[]{:S(2)}) %collective-permute-start.16) | collective-permute-done | bytes 196640 | tf_op jit(solution)/shard_map/ppermute | solution.py:19
  71.9 2.9 %collective-permute-done.14.first_got_ref = bf16[128,768]{1,0:T(8,128)(2,1)S(1)} collective-permute-done((bf16[128,768]{1,0:T(8,128)(2,1)S(1)}, bf16[128,768]{1,0:T(8,128)(2,1)S(1)}, u32[]{:S(2)}, u32[]{:S(2)}) %collective-permute-start.14) | collective-permute-done | bytes 196640 | tf_op jit(solution)/shard_map/ppermute | solution.py:19
  74.8 8.3 %shard_map.74 = (bf16[640,128]{1,0:T(8,128)(2,1)S(1)}, f32[2,64,1536]{2,1,0:T(8,128)S(1)}) custom-call(f32[128,768]{1,0:T(8,128)S(1)} %get-tuple-element.73.first_ref, bf16[128,768]{1,0:T(8,128)(2,1)S(1)} %collective-permute-done.14.first_got_ref, f32[128,768]{1,0:T(8,128)S(1)} %get-tuple-element.71.last_ref, ...), custom_call_target="tpu_custom_call" | custom-call | tf_op jit(solution)/shard_map/pallas_call | solution.py:280
  84.1 2.3 %collective-permute-start.18 = (bf16[4,80,128]{2,1,0:T(8,128)(2,1)S(1)}, bf16[4,80,128]{2,1,0:T(8,128)(2,1)S(1)}, u32[]{:S(2)}, u32[]{:S(2)}) collective-permute-start(bf16[4,80,128]{2,1,0:T(8,128)(2,1)S(1)} %get-tuple-element.77), channel_id=1, source_target_pairs={{0,4},{1,5},{2,6},{3,7},{4,0},{5,1},{6,2},{7,3},{8,12},{9,13},{10,... | collective-permute-start | bytes 245768 | tf_op jit(solution)/shard_map/ppermute | solution.py:19
  86.4 3.0 %shard_map.75.refs_6_ = bf16[4,4,80,1024]{3,2,1,0:T(8,128)(2,1)S(1)} custom-call(s32[1]{0:T(128)} %bitcast.12.place_ref, bf16[528,1024]{1,0:T(8,128)(2,1)} %collective-permute-done.17.block_ref), custom_call_target="tpu_custom_call" | custom-call | tf_op jit(solution)/shard_map/pallas_call | solution.py:317
  89.5 2.2 %collective-permute-done.18.refs_0_ = bf16[4,80,128]{2,1,0:T(8,128)(2,1)S(1)} collective-permute-done((bf16[4,80,128]{2,1,0:T(8,128)(2,1)S(1)}, bf16[4,80,128]{2,1,0:T(8,128)(2,1)S(1)}, u32[]{:S(2)}, u32[]{:S(2)}) %collective-permute-start.18) | collective-permute-done | bytes 81952 | tf_op jit(solution)/shard_map/ppermute | solution.py:19
  91.7 1.9 %collective-permute-start.21 = (bf16[4,80,128]{2,1,0:T(8,128)(2,1)S(1)}, bf16[4,80,128]{2,1,0:T(8,128)(2,1)S(1)}, u32[]{:S(2)}, u32[]{:S(2)}) collective-permute-start(bf16[4,80,128]{2,1,0:T(8,128)(2,1)S(1)} %collective-permute-done.18.refs_0_), channel_id=1, source_target_pairs={{0,24},{8,16},{16,8},{24,0},{1,25},{9,17},{17,9},{25,1},{2,26},{10... | collective-permute-start | bytes 245768 | tf_op jit(solution)/shard_map/ppermute | solution.py:19
  95.3 3.3 %shard_map.76.refs_7_ = bf16[4,4,80,1024]{3,2,1,0:T(8,128)(2,1)S(1)} custom-call(s32[1]{0:T(128)} %bitcast.12.place_ref, bf16[528,1024]{1,0:T(8,128)(2,1)} %collective-permute-done.22.block_ref), custom_call_target="tpu_custom_call" | custom-call | tf_op jit(solution)/shard_map/pallas_call | solution.py:317
  100.8 1.6 %collective-permute-start.25 = (bf16[4,80,128]{2,1,0:T(8,128)(2,1)S(1)}, bf16[4,80,128]{2,1,0:T(8,128)(2,1)S(1)}, u32[]{:S(2)}, u32[]{:S(2)}) collective-permute-start(bf16[4,80,128]{2,1,0:T(8,128)(2,1)S(1)} %get-tuple-element.68.refs_0_), channel_id=1, source_target_pairs={{0,24},{8,16},{16,8},{24,0},{1,25},{9,17},{17,9},{25,1},{2,26},{10... | collective-permute-start | bytes 245768 | tf_op jit(solution)/shard_map/ppermute | solution.py:19
  104.3 1.6 %dynamic-slice_bitcast_fusion = f32[2,384,64]{1,2,0:T(8,128)} fusion(f32[2,64,1536]{2,1,0:T(8,128)} %copy-done.9, s32[]{:T(128)S(6)} %select_n.40), kind=kLoop, calls=%fused_computation.12 | loop fusion | bytes 393220 | tf_op jit(solution)/shard_map/transpose | solution.py:477
  107.6 1.7 %copy-done.2 = bf16[4,4,80,1024]{3,2,1,0:T(8,128)(2,1)S(1)} copy-done((bf16[4,4,80,1024]{3,2,1,0:T(8,128)(2,1)S(1)}, bf16[4,4,80,1024]{3,2,1,0:T(8,128)(2,1)}, u32[]{:S(2)}) %copy-start.2) | copy-done | bytes 2621464
  109.4 1.7 %copy-done.4 = bf16[4,4,80,1024]{3,2,1,0:T(8,128)(2,1)S(1)} copy-done((bf16[4,4,80,1024]{3,2,1,0:T(8,128)(2,1)S(1)}, bf16[4,4,80,1024]{3,2,1,0:T(8,128)(2,1)}, u32[]{:S(2)}) %copy-start.4) | copy-done | bytes 2621464
  111.1 1.7 %copy-done.6 = bf16[4,4,80,1024]{3,2,1,0:T(8,128)(2,1)S(1)} copy-done((bf16[4,4,80,1024]{3,2,1,0:T(8,128)(2,1)S(1)}, bf16[4,4,80,1024]{3,2,1,0:T(8,128)(2,1)}, u32[]{:S(2)}) %copy-start.6) | copy-done | bytes 2621464
  (81 shorter events, 29.2 us)
Async XLA Ops:
  0.6 14.5 %collective-permute-start.5 = (bf16[128,1024]{1,0:T(8,128)(2,1)}, bf16[128,1024]{1,0:T(8,128)(2,1)S(1)}, u32[]{:S(2)}, u32[]{:S(2)}) collective-permute-start(bf16[128,1024]{1,0:T(8,128)(2,1)} %bitcast.42), channel_id=1, source_target_pairs={{0,2},{1,3},{2,0},{3,1},{4,6},{5,7},{6,4},{7,5},{8,10},{9,11},{10,... | collective-permute-start | bytes 786440 | tf_op jit(solution)/shard_map/ppermute | solution.py:19
  3.7 21.6 %collective-permute-start.4 = (bf16[128,1024]{1,0:T(8,128)(2,1)}, bf16[128,1024]{1,0:T(8,128)(2,1)S(1)}, u32[]{:S(2)}, u32[]{:S(2)}) collective-permute-start(bf16[128,1024]{1,0:T(8,128)(2,1)} %bitcast.43), channel_id=1, source_target_pairs={{0,4},{1,5},{2,6},{3,7},{4,0},{5,1},{6,2},{7,3},{8,12},{9,13},{10,... | collective-permute-start | bytes 786440 | tf_op jit(solution)/shard_map/ppermute | solution.py:19
  6.3 19.0 %collective-permute-start.3 = (bf16[128,1024]{1,0:T(8,128)(2,1)}, bf16[128,1024]{1,0:T(8,128)(2,1)S(1)}, u32[]{:S(2)}, u32[]{:S(2)}) collective-permute-start(bf16[128,1024]{1,0:T(8,128)(2,1)} %bitcast.44), channel_id=1, source_target_pairs={{0,6},{1,7},{2,4},{3,5},{4,2},{5,3},{6,0},{7,1},{8,14},{9,15},{10,... | collective-permute-start | bytes 786440 | tf_op jit(solution)/shard_map/ppermute | solution.py:19
  8.9 16.4 %copy-start.12 = (bf16[2,1024,64]{1,2,0:T(8,128)(2,1)S(1)}, bf16[2,1024,64]{1,2,0:T(8,128)(2,1)}, u32[]{:S(2)}) copy-start(bf16[2,1024,64]{1,2,0:T(8,128)(2,1)} %param.9) | copy-start | bytes 786436
  9.0 16.4 %collective-permute-start = (bf16[144,1024]{1,0:T(8,128)(2,1)S(1)}, bf16[144,1024]{1,0:T(8,128)(2,1)}, u32[]{:S(2)}, u32[]{:S(2)}) collective-permute-start(bf16[144,1024]{1,0:T(8,128)(2,1)S(1)} %get-tuple-element.37), channel_id=1, source_target_pairs={{0,8},{8,0},{16,24},{24,16},{1,9},{9,1},{17,25},{25,17},{2,10},{10... | collective-permute-start | bytes 884744 | tf_op jit(solution)/shard_map/ppermute | solution.py:19
  10.8 14.6 %collective-permute-start.1 = (bf16[144,1024]{1,0:T(8,128)(2,1)S(1)}, bf16[144,1024]{1,0:T(8,128)(2,1)}, u32[]{:S(2)}, u32[]{:S(2)}) collective-permute-start(bf16[144,1024]{1,0:T(8,128)(2,1)S(1)} %get-tuple-element.38), channel_id=1, source_target_pairs={{0,16},{8,24},{16,0},{24,8},{1,17},{9,25},{17,1},{25,9},{2,18},{10... | collective-permute-start | bytes 884744 | tf_op jit(solution)/shard_map/ppermute | solution.py:19
  15.1 10.3 %collective-permute-start.2 = (bf16[144,1024]{1,0:T(8,128)(2,1)S(1)}, bf16[144,1024]{1,0:T(8,128)(2,1)}, u32[]{:S(2)}, u32[]{:S(2)}) collective-permute-start(bf16[144,1024]{1,0:T(8,128)(2,1)S(1)} %get-tuple-element.39), channel_id=1, source_target_pairs={{0,24},{8,16},{16,8},{24,0},{1,25},{9,17},{17,9},{25,1},{2,26},{10... | collective-permute-start | bytes 884744 | tf_op jit(solution)/shard_map/ppermute | solution.py:19
  32.1 2.8 %collective-permute-start.6 = (bf16[528,1024]{1,0:T(8,128)(2,1)S(1)}, bf16[528,1024]{1,0:T(8,128)(2,1)S(1)}, u32[]{:S(2)}, u32[]{:S(2)}) collective-permute-start(bf16[528,1024]{1,0:T(8,128)(2,1)S(1)} %slice_dynamic-update-slice_fusion.block_ref), channel_id=1, source_target_pairs={{0,1},{1,0},{2,3},{3,2},{4,5},{5,4},{6,7},{7,6},{8,9},{9,8},{10,11... | collective-permute-start | bytes 3244040 | tf_op jit(solution)/shard_map/ppermute | solution.py:19
  36.7 8.6 %collective-permute-start.9 = (bf16[4,2,80,128]{3,2,1,0:T(8,128)(2,1)S(1)}, bf16[4,2,80,128]{3,2,1,0:T(8,128)(2,1)S(1)}, u32[]{:S(2)}, u32[]{:S(2)}) collective-permute-start(bf16[4,2,80,128]{3,2,1,0:T(8,128)(2,1)S(1)} %get-tuple-element.74), channel_id=1, source_target_pairs={{0,24},{8,16},{16,8},{24,0},{1,25},{9,17},{17,9},{25,1},{2,26},{10... | collective-permute-start | bytes 491528 | tf_op jit(solution)/shard_map/ppermute | solution.py:19
  39.2 8.2 %collective-permute-start.8 = (bf16[4,2,80,128]{3,2,1,0:T(8,128)(2,1)S(1)}, bf16[4,2,80,128]{3,2,1,0:T(8,128)(2,1)S(1)}, u32[]{:S(2)}, u32[]{:S(2)}) collective-permute-start(bf16[4,2,80,128]{3,2,1,0:T(8,128)(2,1)S(1)} %get-tuple-element.75), channel_id=1, source_target_pairs={{0,16},{8,24},{16,0},{24,8},{1,17},{9,25},{17,1},{25,9},{2,18},{10... | collective-permute-start | bytes 491528 | tf_op jit(solution)/shard_map/ppermute | solution.py:19
  39.7 7.8 %collective-permute-start.7 = (bf16[4,2,80,128]{3,2,1,0:T(8,128)(2,1)S(1)}, bf16[4,2,80,128]{3,2,1,0:T(8,128)(2,1)S(1)}, u32[]{:S(2)}, u32[]{:S(2)}) collective-permute-start(bf16[4,2,80,128]{3,2,1,0:T(8,128)(2,1)S(1)} %get-tuple-element.76), channel_id=1, source_target_pairs={{0,8},{8,0},{16,24},{24,16},{1,9},{9,1},{17,25},{25,17},{2,10},{10... | collective-permute-start | bytes 491528 | tf_op jit(solution)/shard_map/ppermute | solution.py:19
  42.0 15.9 %copy-start.7 = (bf16[2,1,640,1536]{3,2,1,0:T(8,128)(2,1)S(1)}, bf16[2,1,640,1536]{3,2,1,0:T(8,128)(2,1)}, u32[]{:S(2)}) copy-start(bf16[2,1,640,1536]{3,2,1,0:T(8,128)(2,1)} %param.8) | copy-start | bytes 11796484
  47.6 6.4 %collective-permute-start.12 = (bf16[2,80,128]{2,1,0:T(8,128)(2,1)S(1)}, bf16[2,80,128]{2,1,0:T(8,128)(2,1)S(1)}, u32[]{:S(2)}, u32[]{:S(2)}) collective-permute-start(bf16[2,80,128]{2,1,0:T(8,128)(2,1)S(1)} %get-tuple-element.79), channel_id=1, source_target_pairs={{0,6},{1,7},{2,4},{3,5},{4,2},{5,3},{6,0},{7,1},{8,14},{9,15},{10,... | collective-permute-start | bytes 122888 | tf_op jit(solution)/shard_map/ppermute | solution.py:19
  50.7 5.7 %collective-permute-start.11 = (bf16[2,80,128]{2,1,0:T(8,128)(2,1)S(1)}, bf16[2,80,128]{2,1,0:T(8,128)(2,1)S(1)}, u32[]{:S(2)}, u32[]{:S(2)}) collective-permute-start(bf16[2,80,128]{2,1,0:T(8,128)(2,1)S(1)} %get-tuple-element.80), channel_id=1, source_target_pairs={{0,4},{1,5},{2,6},{3,7},{4,0},{5,1},{6,2},{7,3},{8,12},{9,13},{10,... | collective-permute-start | bytes 122888 | tf_op jit(solution)/shard_map/ppermute | solution.py:19
  53.9 4.0 %collective-permute-start.10 = (bf16[2,80,128]{2,1,0:T(8,128)(2,1)S(1)}, bf16[2,80,128]{2,1,0:T(8,128)(2,1)S(1)}, u32[]{:S(2)}, u32[]{:S(2)}) collective-permute-start(bf16[2,80,128]{2,1,0:T(8,128)(2,1)S(1)} %get-tuple-element.81), channel_id=1, source_target_pairs={{0,2},{1,3},{2,0},{3,1},{4,6},{5,7},{6,4},{7,5},{8,10},{9,11},{10,... | collective-permute-start | bytes 122888 | tf_op jit(solution)/shard_map/ppermute | solution.py:19
  59.3 24.8 %collective-permute-start.17 = (bf16[528,1024]{1,0:T(8,128)(2,1)S(1)}, bf16[528,1024]{1,0:T(8,128)(2,1)}, u32[]{:S(2)}, u32[]{:S(2)}) collective-permute-start(bf16[528,1024]{1,0:T(8,128)(2,1)S(1)} %slice_dynamic-update-slice_fusion.block_ref), channel_id=1, source_target_pairs={{0,2},{1,3},{2,0},{3,1},{4,6},{5,7},{6,4},{7,5},{8,10},{9,11},{10,... | collective-permute-start | bytes 3244040 | tf_op jit(solution)/shard_map/ppermute | solution.py:19
  60.4 5.7 %collective-permute-start.15 = (bf16[128,768]{1,0:T(8,128)(2,1)S(1)}, bf16[128,768]{1,0:T(8,128)(2,1)S(1)}, u32[]{:S(2)}, u32[]{:S(2)}) collective-permute-start(bf16[128,768]{1,0:T(8,128)(2,1)S(1)} %convert_element_type.48), channel_id=1, source_target_pairs={{0,16},{8,24},{16,0},{24,8},{1,17},{9,25},{17,1},{25,9},{2,18},{10... | collective-permute-start | bytes 589832 | tf_op jit(solution)/shard_map/ppermute | solution.py:19
  61.9 7.1 %collective-permute-start.13 = (bf16[128,768]{1,0:T(8,128)(2,1)S(1)}, bf16[128,768]{1,0:T(8,128)(2,1)S(1)}, u32[]{:S(2)}, u32[]{:S(2)}) collective-permute-start(bf16[128,768]{1,0:T(8,128)(2,1)S(1)} %convert_element_type.45), channel_id=1, source_target_pairs={{0,8},{8,0},{16,24},{24,16},{1,9},{9,1},{17,25},{25,17},{2,10},{10... | collective-permute-start | bytes 589832 | tf_op jit(solution)/shard_map/ppermute | solution.py:19
  66.2 5.7 %collective-permute-start.16 = (bf16[128,768]{1,0:T(8,128)(2,1)S(1)}, bf16[128,768]{1,0:T(8,128)(2,1)S(1)}, u32[]{:S(2)}, u32[]{:S(2)}) collective-permute-start(bf16[128,768]{1,0:T(8,128)(2,1)S(1)} %get-tuple-element.70), channel_id=1, source_target_pairs={{0,8},{8,0},{16,24},{24,16},{1,9},{9,1},{17,25},{25,17},{2,10},{10... | collective-permute-start | bytes 589832 | tf_op jit(solution)/shard_map/ppermute | solution.py:19
  69.0 5.7 %collective-permute-start.14 = (bf16[128,768]{1,0:T(8,128)(2,1)S(1)}, bf16[128,768]{1,0:T(8,128)(2,1)S(1)}, u32[]{:S(2)}, u32[]{:S(2)}) collective-permute-start(bf16[128,768]{1,0:T(8,128)(2,1)S(1)} %get-tuple-element.72), channel_id=1, source_target_pairs={{0,16},{8,24},{16,0},{24,8},{1,17},{9,25},{17,1},{25,9},{2,18},{10... | collective-permute-start | bytes 589832 | tf_op jit(solution)/shard_map/ppermute | solution.py:19
  84.1 11.2 %collective-permute-start.22 = (bf16[528,1024]{1,0:T(8,128)(2,1)}, bf16[528,1024]{1,0:T(8,128)(2,1)}, u32[]{:S(2)}, u32[]{:S(2)}) collective-permute-start(bf16[528,1024]{1,0:T(8,128)(2,1)} %collective-permute-done.17.block_ref), channel_id=1, source_target_pairs={{0,1},{1,0},{2,3},{3,2},{4,5},{5,4},{6,7},{7,6},{8,9},{9,8},{10,11... | collective-permute-start | bytes 3244040 | tf_op jit(solution)/shard_map/ppermute | solution.py:19
  84.1 7.6 %collective-permute-start.18 = (bf16[4,80,128]{2,1,0:T(8,128)(2,1)S(1)}, bf16[4,80,128]{2,1,0:T(8,128)(2,1)S(1)}, u32[]{:S(2)}, u32[]{:S(2)}) collective-permute-start(bf16[4,80,128]{2,1,0:T(8,128)(2,1)S(1)} %get-tuple-element.77), channel_id=1, source_target_pairs={{0,4},{1,5},{2,6},{3,7},{4,0},{5,1},{6,2},{7,3},{8,12},{9,13},{10,... | collective-permute-start | bytes 245768 | tf_op jit(solution)/shard_map/ppermute | solution.py:19
  89.5 9.4 %copy-start.3 = (bf16[4,4,80,1024]{3,2,1,0:T(8,128)(2,1)}, bf16[4,4,80,1024]{3,2,1,0:T(8,128)(2,1)S(1)}, u32[]{:S(2)}) copy-start(bf16[4,4,80,1024]{3,2,1,0:T(8,128)(2,1)S(1)} %shard_map.75.refs_6_) | copy-start | bytes 7864324
  91.7 6.9 %collective-permute-start.21 = (bf16[4,80,128]{2,1,0:T(8,128)(2,1)S(1)}, bf16[4,80,128]{2,1,0:T(8,128)(2,1)S(1)}, u32[]{:S(2)}, u32[]{:S(2)}) collective-permute-start(bf16[4,80,128]{2,1,0:T(8,128)(2,1)S(1)} %collective-permute-done.18.refs_0_), channel_id=1, source_target_pairs={{0,24},{8,16},{16,8},{24,0},{1,25},{9,17},{17,9},{25,1},{2,26},{10... | collective-permute-start | bytes 245768 | tf_op jit(solution)/shard_map/ppermute | solution.py:19
  93.5 5.1 %collective-permute-start.20 = (bf16[4,80,128]{2,1,0:T(8,128)(2,1)S(1)}, bf16[4,80,128]{2,1,0:T(8,128)(2,1)S(1)}, u32[]{:S(2)}, u32[]{:S(2)}) collective-permute-start(bf16[4,80,128]{2,1,0:T(8,128)(2,1)S(1)} %collective-permute-done.18.refs_0_), channel_id=1, source_target_pairs={{0,16},{8,24},{16,0},{24,8},{1,17},{9,25},{17,1},{25,9},{2,18},{10... | collective-permute-start | bytes 245768 | tf_op jit(solution)/shard_map/ppermute | solution.py:19
  94.4 4.4 %collective-permute-start.19 = (bf16[4,80,128]{2,1,0:T(8,128)(2,1)S(1)}, bf16[4,80,128]{2,1,0:T(8,128)(2,1)S(1)}, u32[]{:S(2)}, u32[]{:S(2)}) collective-permute-start(bf16[4,80,128]{2,1,0:T(8,128)(2,1)S(1)} %collective-permute-done.18.refs_0_), channel_id=1, source_target_pairs={{0,8},{8,0},{16,24},{24,16},{1,9},{9,1},{17,25},{25,17},{2,10},{10... | collective-permute-start | bytes 245768 | tf_op jit(solution)/shard_map/ppermute | solution.py:19
  95.3 3.6 %copy-start.1 = (bf16[4,4,80,1024]{3,2,1,0:T(8,128)(2,1)S(1)}, bf16[4,4,80,1024]{3,2,1,0:T(8,128)(2,1)}, u32[]{:S(2)}) copy-start(bf16[4,4,80,1024]{3,2,1,0:T(8,128)(2,1)} %copy-done) | copy-start | bytes 7864324
  100.3 14.0 %collective-permute-start.26 = (bf16[2,64,1024]{2,1,0:T(8,128)(2,1)S(1)}, bf16[2,64,1024]{2,1,0:T(8,128)(2,1)S(1)}, u32[]{:S(2)}, u32[]{:S(2)}) collective-permute-start(bf16[2,64,1024]{2,1,0:T(8,128)(2,1)S(1)} %shard_map.77), channel_id=1, source_target_pairs={{0,4},{1,5},{2,6},{3,7},{4,0},{5,1},{6,2},{7,3},{8,12},{9,13},{10,... | collective-permute-start | bytes 786440 | tf_op jit(solution)/shard_map/ppermute | solution.py:19
  100.8 6.0 %collective-permute-start.25 = (bf16[4,80,128]{2,1,0:T(8,128)(2,1)S(1)}, bf16[4,80,128]{2,1,0:T(8,128)(2,1)S(1)}, u32[]{:S(2)}, u32[]{:S(2)}) collective-permute-start(bf16[4,80,128]{2,1,0:T(8,128)(2,1)S(1)} %get-tuple-element.68.refs_0_), channel_id=1, source_target_pairs={{0,24},{8,16},{16,8},{24,0},{1,25},{9,17},{17,9},{25,1},{2,26},{10... | collective-permute-start | bytes 245768 | tf_op jit(solution)/shard_map/ppermute | solution.py:19
  102.4 5.0 %collective-permute-start.24 = (bf16[4,80,128]{2,1,0:T(8,128)(2,1)S(1)}, bf16[4,80,128]{2,1,0:T(8,128)(2,1)S(1)}, u32[]{:S(2)}, u32[]{:S(2)}) collective-permute-start(bf16[4,80,128]{2,1,0:T(8,128)(2,1)S(1)} %get-tuple-element.68.refs_0_), channel_id=1, source_target_pairs={{0,16},{8,24},{16,0},{24,8},{1,17},{9,25},{17,1},{25,9},{2,18},{10... | collective-permute-start | bytes 245768 | tf_op jit(solution)/shard_map/ppermute | solution.py:19
  103.2 4.4 %collective-permute-start.23 = (bf16[4,80,128]{2,1,0:T(8,128)(2,1)S(1)}, bf16[4,80,128]{2,1,0:T(8,128)(2,1)S(1)}, u32[]{:S(2)}, u32[]{:S(2)}) collective-permute-start(bf16[4,80,128]{2,1,0:T(8,128)(2,1)S(1)} %get-tuple-element.68.refs_0_), channel_id=1, source_target_pairs={{0,8},{8,0},{16,24},{24,16},{1,9},{9,1},{17,25},{25,17},{2,10},{10... | collective-permute-start | bytes 245768 | tf_op jit(solution)/shard_map/ppermute | solution.py:19
  107.6 1.7 %copy-start.2 = (bf16[4,4,80,1024]{3,2,1,0:T(8,128)(2,1)S(1)}, bf16[4,4,80,1024]{3,2,1,0:T(8,128)(2,1)}, u32[]{:S(2)}) copy-start(bf16[4,4,80,1024]{3,2,1,0:T(8,128)(2,1)} %copy-done) | copy-start | bytes 7864324
  (8 other events, 10.2 us)

commit v4 on v3

--- a/solution.py
+++ b/solution.py
@@ -8,7 +8,8 @@
 from jax.sharding import PartitionSpec as P
 
 CORES = 2
-VMEM = 24 << 20
+PIVOTS = 4
+VMEM = 16 << 20
 HIGHEST = lax.Precision.HIGHEST
 NT = (((1,), (1,)), ((), ()))
 TN = (((0,), (0,)), ((), ()))
@@ -49,6 +50,52 @@
         out_specs=(pl.BlockSpec(memory_space=pltpu.VMEM),) * members,
         compiler_params=pltpu.CompilerParams(vmem_limit_bytes=VMEM),
     )(place, cotangent, jnp.swapaxes(expert_ids, 0, 1), jnp.swapaxes(gates, 0, 1))
+
+
+def stack_kernel(sizes, *refs):
+    members, tokens, _, _, experts_all = sizes
+    pieces, out_ref, sems = refs[:members], refs[-2], refs[-1]
+    part = out_ref.shape[1]
+    chunks = part // tokens
+    first = out_ref.shape[0] - members * tokens
+    copies = []
+    for k, piece in enumerate(pieces):
+        row, lane = k // chunks * experts_all, k % chunks * tokens
+        copies += [
+            pltpu.make_async_copy(
+                piece.at[pl.ds(0, tokens)],
+                out_ref.at[pl.ds(first + k * tokens, tokens)],
+                sems.at[2 * k],
+            ),
+            pltpu.make_async_copy(
+                piece.at[pl.ds(tokens, experts_all), pl.ds(0, tokens)],
+                out_ref.at[pl.ds(row, experts_all), pl.ds(lane, tokens)],
+                sems.at[2 * k + 1],
+            ),
+        ]
+    for copy in copies:
+        copy.start()
+    used = members % chunks * tokens
+    if used:
+        out_ref[first - experts_all : first, used:] = jnp.zeros(
+            (experts_all, part - used), out_ref.dtype
+        )
+    for copy in copies:
+        copy.wait()
+
+
+def stack_pieces(pieces, sizes):
+    members, tokens, _, _, experts_all = sizes
+    part = pieces[0].shape[1]
+    rows = -(-members // (part // tokens)) * experts_all + members * tokens
+    return pl.pallas_call(
+        functools.partial(stack_kernel, sizes),
+        out_shape=jax.ShapeDtypeStruct((rows, part), pieces[0].dtype),
+        in_specs=[pl.BlockSpec(memory_space=pl.ANY)] * members,
+        out_specs=pl.BlockSpec(memory_space=pltpu.VMEM),
+        scratch_shapes=[pltpu.SemaphoreType.DMA((2 * members,))],
+        compiler_params=pltpu.CompilerParams(vmem_limit_bytes=VMEM),
+    )(*pieces)
 
 
 def sum_steps(members):
@@ -221,7 +268,47 @@
     )(place, *arrived, own_hidden)
 
 
-def whiten_kernel(first_ref, first_got_ref, last_ref, last_got_ref, hidden_ref, mapped_ref, merged_ref):
+def eliminate(state, k, first, inner, row):
+    top = state[first]
+
+    def columns_at(block):
+        return [jnp.broadcast_to(block[:, k + j : k + j + 1], block.shape) for j in range(PIVOTS)]
+
+    columns = columns_at(top)
+    grid = [[column[inner + i : inner + i + 1] for column in columns] for i in range(PIVOTS)]
+    lines = [top[inner + i : inner + i + 1] for i in range(PIVOTS)]
+    scaled, ratio = [], []
+    for p in range(PIVOTS):
+        scaled.append(lines[p] / grid[p][p])
+        ratio.append([value / grid[p][p] for value in grid[p]])
+        for i in range(p + 1, PIVOTS):
+            lines[i] = lines[i] - grid[i][p] * scaled[p]
+            for j in range(p + 1, PIVOTS):
+                grid[i][j] = grid[i][j] - grid[i][p] * ratio[p][j]
+    for b in range(first, len(state)):
+        factors = []
+        for j, factor in enumerate(columns if b == first else columns_at(state[b])):
+            for p in range(j):
+                factor = factor - ratio[p][j] * factors[p]
+            factors.append(factor)
+        for j in range(PIVOTS):
+            factor = factors[j]
+            if b == first:
+                factor = jnp.where(row > inner + j, factor, 0.0)
+            state[b] = state[b] - factor * scaled[j]
+
+
+def whiten_kernel(
+    place_ref,
+    first_ref,
+    first_got_ref,
+    last_ref,
+    last_got_ref,
+    hidden_ref,
+    mapped_ref,
+    share_ref,
+    merged_ref,
+):
     held, rank, width = merged_ref.shape
     half = width // 2
     for h in range(held):
@@ -232,6 +319,12 @@
         merged_ref[h, :, half:] = last_ref[rows] + last_got_ref[rows].astype(
             jnp.float32
         )
+    kept = share_ref.shape[2]
+    if kept == width:
+        share_ref[...] = merged_ref[...]
+    else:
+        start = pl.multiple_of(place_ref[0] * kept, 128)
+        share_ref[...] = merged_ref[:, :, pl.ds(start, kept)]
     lane = lax.broadcasted_iota(jnp.int32, (8, 2 * rank), 1)
     row = lax.broadcasted_iota(jnp.int32, (8, 2 * rank), 0)
     blocks = rank // 8
@@ -248,18 +341,10 @@
                 for b in range(blocks)
             ]
         )
-    for k in range(rank):
+    for k in range(0, rank, PIVOTS):
         first, inner = k // 8, k % 8
         for state in states:
-            pivot_column = jnp.broadcast_to(state[first][:, k : k + 1], (8, 2 * rank))
-            scaled = state[first][inner : inner + 1] / pivot_column[inner : inner + 1]
-            for b in range(first, blocks):
-                column = pivot_column
-                if b == first:
-                    column = jnp.where(row > inner, column, 0.0)
-                else:
-                    column = jnp.broadcast_to(state[b][:, k : k + 1], (8, 2 * rank))
-                state[b] = state[b] - column * scaled
+            eliminate(state, k, first, inner, row)
     for h in range(held):
         inverse = []
         for b, block in enumerate(states[h]):
@@ -274,17 +359,26 @@
         ).astype(jnp.bfloat16)
 
 
-def whiten_and_map(parts, own_hidden):
+def whiten_and_map(place, parts, own_hidden, members):
     held, slots, width = own_hidden.shape
     wide = parts[0].shape[0]
-    return pl.pallas_call(
+    share = width // members
+    kept = share if share % 128 == 0 else width
+    mapped, merged = pl.pallas_call(
         whiten_kernel,
         out_shape=(
             jax.ShapeDtypeStruct((slots, wide), jnp.bfloat16),
-            jax.ShapeDtypeStruct((held, wide // held, width), jnp.float32),
+            jax.ShapeDtypeStruct((held, wide // held, kept), jnp.float32),
         ),
-        compiler_params=pltpu.CompilerParams(vmem_limit_bytes=VMEM),
-    )(*parts, own_hidden)
+        in_specs=[pl.BlockSpec(memory_space=pltpu.SMEM)]
+        + [pl.BlockSpec(memory_space=pltpu.VMEM)] * 5,
+        out_specs=(pl.BlockSpec(memory_space=pltpu.VMEM),) * 2,
+        scratch_shapes=[pltpu.VMEM((held, wide // held, width), jnp.float32)],
+        compiler_params=pltpu.CompilerParams(vmem_limit_bytes=VMEM),
+    )(place, *parts, own_hidden)
+    if kept != share:
+        merged = lax.dynamic_slice_in_dim(merged, place[0] * share, share, 2)
+    return mapped, merged
 
 
 def dispatch_kernel(sizes, place_ref, block_ref, out_ref):
@@ -372,7 +466,6 @@
     capacity = slots // places
     padded = -(-capacity // 16) * 16
     part = model_width // members
-    chunks = part // tokens
     sizes = (members, tokens, held, rank, experts_all)
     my_dp = lax.axis_index("dp")
     my_place = lax.axis_index("expert")
@@ -384,20 +477,15 @@
     def swap(block):
         return exchange(block, "expert", 1)
 
-    pieces = cut_pieces(
-        my_dp.reshape(1).astype(jnp.int32), cotangent, expert_ids, gates, members, experts_all
-    )
+    dp_place = my_dp.reshape(1).astype(jnp.int32)
+    pieces = cut_pieces(dp_place, cotangent, expert_ids, gates, members, experts_all)
     pieces = [exchange(piece, "dp", k) if k else piece for k, piece in enumerate(pieces)]
     factor = jnp.swapaxes(q_prev, 1, 2).reshape(held * rank, part)
     factors = [factor] + [exchange(factor, "expert", CORES * k) for k in range(1, chips)]
 
     factors = jnp.concatenate(factors[::-1])
     pieces, factors = tie((pieces, factors))
-    tails = [piece[tokens:, :tokens] for piece in pieces]
-    while len(tails) % chunks:
-        tails.append(jnp.zeros_like(tails[0]))
-    tails = [jnp.concatenate(tails[i : i + chunks], 1) for i in range(0, len(tails), chunks)]
-    own = jnp.concatenate(tails + [piece[:tokens] for piece in pieces], axis=0)
+    own = stack_pieces(pieces, sizes)
 
     span = min(2, chips)
     owners = chips // span
@@ -417,10 +505,10 @@
         summed = summed + value.astype(jnp.float32)
     summed = summed.astype(jnp.bfloat16)[::-1]
     arrived = [summed[0]] + [exchange(summed[k], "expert", CORES * k) for k in range(1, chips)]
+    if span > 1:
+        arrived, own = tie((arrived, own))
+        near = exchange(own, "expert", CORES)
     parts = left_partial(place, arrived, own_hidden, capacity)
-    if span > 1:
-        parts, own = tie((parts, own))
-        near = exchange(own, "expert", CORES)
     turns = sum_steps(members)
     rounds = len(turns[0])
     for index in range(rounds):
@@ -429,7 +517,9 @@
         got = [
             exchange(p.astype(jnp.bfloat16), "dp", turn[index]) for p, turn in zip(parts, turns)
         ]
-    mapped, merged = whiten_and_map([parts[0], got[0], parts[1], got[1]], own_hidden)
+    mapped, p_share = whiten_and_map(
+        dp_place, [parts[0], got[0], parts[1], got[1]], own_hidden, members
+    )
     mapped = mapped.reshape(places, capacity, held * rank)
     mapped = jnp.pad(mapped, ((0, 0), (0, padded - capacity), (0, 0)))
     if span > 1:
@@ -472,8 +562,6 @@
     q_next = product(over_groups(mine), 0, jnp.float32)
     for value in parts:
         q_next = q_next + value.astype(jnp.float32)
-    share = width // members
-    p_share = lax.dynamic_slice_in_dim(merged, my_dp * share, share, 2)
     return (jnp.swapaxes(p_share, 1, 2), jnp.swapaxes(q_next, 1, 2))
 
 

time: 116 us -> 110 us (0.948)
  local copies, waits for them, and re-layouts: 16.9 us -> 4.14 us
  waiting for transfers between devices: 33.6 us -> 43.5 us
  Pallas kernels: 26 us -> 23.3 us
  starting transfers between devices: 36.4 us -> 35.2 us
    unnamed x34 -> x12, local copies, waits for them, and re-layouts: 14.3 us -> 4.08 us
    ppermute x27, waiting for transfers between devices: 33.6 us -> 43.5 us  [exchange(): return lax.ppermute(value, axis, [(i, i ^ distance) for i in range(size)])]
    pallas_call x1, Pallas kernels: 8.32 us -> 5.78 us  [whiten_and_map(): pl.pallas_call(whiten_kernel, out_shape=(jax.ShapeDtypeStruct((slots, wid...]
    transpose x1 -> x0, local copies, waits for them, and re-layouts: 1.62 us -> none  [local(): return (jnp.swapaxes(p_share, 1, 2), jnp.swapaxes(q_next, 1, 2))]
    ppermute x27, starting transfers between devices: 36.4 us -> 35.2 us  [exchange(): return lax.ppermute(value, axis, [(i, i ^ distance) for i in range(size)])]
  transfers between devices with their start and end apart: 27 -> 27, of which waited for: 16 -> 19; matrix products, arithmetic and copies ran while one was open for 2% -> 1% of each run, Pallas kernels for 17% -> 17%
where the time goes in v4:
time: 110 us; the launch traced here: 109 us
  waiting for transfers between devices  43.5 us (40%)
  starting transfers between devices  35.2 us (32%)
  Pallas kernels  23.3 us (21%)
  local copies, waits for them, and re-layouts  4.14 us (4%)
  other arithmetic  2.25 us (2%)
    ppermute x27, waiting for transfers between devices, exchange(): return lax.ppermute(value, axis, [(i, i ^ distance) for i in range(size)])  43.5 us
    ppermute x27, starting transfers between devices, exchange(): return lax.ppermute(value, axis, [(i, i ^ distance) for i in range(size)])  35.2 us
    pallas_call x4, Pallas kernels, dispatch(): pl.pallas_call(functools.partial(dispatch_kernel, sizes), out_shape=jax.S...  9.62 us
    pallas_call x1, Pallas kernels, whiten_and_map(): pl.pallas_call(whiten_kernel, out_shape=(jax.ShapeDtypeStruct((slots, wid...  5.78 us
    unnamed x12, local copies, waits for them, and re-layouts  4.08 us
    pallas_call x2, Pallas kernels, project(): pl.pallas_call(functools.partial(project_kernel, sizes), out_shape=jax.Sh...  3.44 us
    pallas_call x2, Pallas kernels, right_factor(): pl.pallas_call(functools.partial(right_kernel, len(mapped_groups), owner)...  2.89 us
  transfers between devices with their start and end apart: 27, of which 19 were waited for; matrix products, arithmetic and copies ran while one was open for 1% of the time, Pallas kernels for 17%

profile of v4, /device:TPU:0, one launch (start us, length us, event | category | flops | bytes accessed | tf_op | source)
XLA Modules:
  0.0 109.3 jit_solution(9561466299746597156)
XLA Ops:
  0.6 3.1 %collective-permute-start.5 = (bf16[128,1024]{1,0:T(8,128)(2,1)}, bf16[128,1024]{1,0:T(8,128)(2,1)S(1)}, u32[]{:S(2)}, u32[]{:S(2)}) collective-permute-start(bf16[128,1024]{1,0:T(8,128)(2,1)} %bitcast.41), channel_id=1, source_target_pairs={{0,2},{1,3},{2,0},{3,1},{4,6},{5,7},{6,4},{7,5},{8,10},{9,11},{10,... | collective-permute-start | bytes 786440 | tf_op jit(solution)/shard_map/ppermute | solution.py:20
  3.7 2.6 %collective-permute-start.4 = (bf16[128,1024]{1,0:T(8,128)(2,1)}, bf16[128,1024]{1,0:T(8,128)(2,1)S(1)}, u32[]{:S(2)}, u32[]{:S(2)}) collective-permute-start(bf16[128,1024]{1,0:T(8,128)(2,1)} %bitcast.42), channel_id=1, source_target_pairs={{0,4},{1,5},{2,6},{3,7},{4,0},{5,1},{6,2},{7,3},{8,12},{9,13},{10,... | collective-permute-start | bytes 786440 | tf_op jit(solution)/shard_map/ppermute | solution.py:20
  9.0 1.8 %collective-permute-start = (bf16[144,1024]{1,0:T(8,128)(2,1)S(1)}, bf16[144,1024]{1,0:T(8,128)(2,1)S(1)}, u32[]{:S(2)}, u32[]{:S(2)}) collective-permute-start(bf16[144,1024]{1,0:T(8,128)(2,1)S(1)} %get-tuple-element.39), channel_id=1, source_target_pairs={{0,8},{8,0},{16,24},{24,16},{1,9},{9,1},{17,25},{25,17},{2,10},{10... | collective-permute-start | bytes 884744 | tf_op jit(solution)/shard_map/ppermute | solution.py:20
  10.8 1.5 %collective-permute-start.1 = (bf16[144,1024]{1,0:T(8,128)(2,1)S(1)}, bf16[144,1024]{1,0:T(8,128)(2,1)S(1)}, u32[]{:S(2)}, u32[]{:S(2)}) collective-permute-start(bf16[144,1024]{1,0:T(8,128)(2,1)S(1)} %get-tuple-element.40), channel_id=1, source_target_pairs={{0,16},{8,24},{16,0},{24,8},{1,17},{9,25},{17,1},{25,9},{2,18},{10... | collective-permute-start | bytes 884744 | tf_op jit(solution)/shard_map/ppermute | solution.py:20
  12.3 2.8 %collective-permute-done.5 = bf16[128,1024]{1,0:T(8,128)(2,1)S(1)} collective-permute-done((bf16[128,1024]{1,0:T(8,128)(2,1)}, bf16[128,1024]{1,0:T(8,128)(2,1)S(1)}, u32[]{:S(2)}, u32[]{:S(2)}) %collective-permute-start.5) | collective-permute-done | bytes 262176 | tf_op jit(solution)/shard_map/ppermute | solution.py:20
  15.1 2.6 %collective-permute-start.2 = (bf16[144,1024]{1,0:T(8,128)(2,1)S(1)}, bf16[144,1024]{1,0:T(8,128)(2,1)S(1)}, u32[]{:S(2)}, u32[]{:S(2)}) collective-permute-start(bf16[144,1024]{1,0:T(8,128)(2,1)S(1)} %get-tuple-element.41), channel_id=1, source_target_pairs={{0,24},{8,16},{16,8},{24,0},{1,25},{9,17},{17,9},{25,1},{2,26},{10... | collective-permute-start | bytes 884744 | tf_op jit(solution)/shard_map/ppermute | solution.py:20
  17.8 7.5 %collective-permute-done.4 = bf16[128,1024]{1,0:T(8,128)(2,1)S(1)} collective-permute-done((bf16[128,1024]{1,0:T(8,128)(2,1)}, bf16[128,1024]{1,0:T(8,128)(2,1)S(1)}, u32[]{:S(2)}, u32[]{:S(2)}) %collective-permute-start.4) | collective-permute-done | bytes 262176 | tf_op jit(solution)/shard_map/ppermute | solution.py:20
  26.5 1.7 %shard_map.70.refs_0_ = bf16[4,4,1,80,128]{4,3,2,1,0:T(8,128)(2,1)S(1)} custom-call(s32[2]{0:T(128)S(1)} %pad_add_fusion.place_ref, bf16[528,1024]{1,0:T(8,128)(2,1)S(1)} %shard_map.69.block_ref, bf16[512,1024]{1,0:T(8,128)(2,1)S(1)} %pad_maximum_fusion.factors_ref), custom_call_target="tpu_custom_call" | custom-call | tf_op jit(solution)/shard_map/pallas_call | solution.py:216
  28.3 2.7 %collective-permute-done.6.block_ref = bf16[528,1024]{1,0:T(8,128)(2,1)S(1)} collective-permute-done((bf16[528,1024]{1,0:T(8,128)(2,1)S(1)}, bf16[528,1024]{1,0:T(8,128)(2,1)S(1)}, u32[]{:S(2)}, u32[]{:S(2)}) %collective-permute-start.6) | collective-permute-done | bytes 1081376 | tf_op jit(solution)/shard_map/ppermute | solution.py:20
  31.0 1.7 %shard_map.71 = bf16[4,4,2,80,128]{4,3,2,1,0:T(8,128)(2,1)S(1)} custom-call(s32[2]{0:T(128)S(1)} %pad_add_fusion.place_ref, bf16[528,1024]{1,0:T(8,128)(2,1)S(1)} %collective-permute-done.6.block_ref, bf16[512,1024]{1,0:T(8,128)(2,1)S(1)} %pad_maximum_fusion.factors_ref, bf16[4,4,1,80,128]{4,3,2,1,0:T(8,128)(2,1)S(1)} %shard_map.70.refs_0_), custom_call_target="tpu_custom_call" | custom-call | tf_op jit(solution)/shard_map/pallas_call | solution.py:216
  32.8 2.5 %collective-permute-start.9 = (bf16[4,2,80,128]{3,2,1,0:T(8,128)(2,1)S(1)}, bf16[4,2,80,128]{3,2,1,0:T(8,128)(2,1)S(1)}, u32[]{:S(2)}, u32[]{:S(2)}) collective-permute-start(bf16[4,2,80,128]{3,2,1,0:T(8,128)(2,1)S(1)} %get-tuple-element.78), channel_id=1, source_target_pairs={{0,24},{8,16},{16,8},{24,0},{1,25},{9,17},{17,9},{25,1},{2,26},{10... | collective-permute-start | bytes 491528 | tf_op jit(solution)/shard_map/ppermute | solution.py:20
  36.4 1.8 %shard_map.72.refs_4_ = bf16[4,4,80,1024]{3,2,1,0:T(8,128)(2,1)S(1)} custom-call(s32[1]{0:T(128)} %bitcast.12.place_ref, bf16[528,1024]{1,0:T(8,128)(2,1)S(1)} %shard_map.69.block_ref), custom_call_target="tpu_custom_call" | custom-call | tf_op jit(solution)/shard_map/pallas_call | solution.py:411
  38.2 1.8 %shard_map.73.refs_5_ = bf16[4,4,80,1024]{3,2,1,0:T(8,128)(2,1)S(1)} custom-call(s32[1]{0:T(128)} %bitcast.12.place_ref, bf16[528,1024]{1,0:T(8,128)(2,1)S(1)} %collective-permute-done.6.block_ref), custom_call_target="tpu_custom_call" | custom-call | tf_op jit(solution)/shard_map/pallas_call | solution.py:411
  41.4 2.1 %collective-permute-done.8 = bf16[4,2,80,128]{3,2,1,0:T(8,128)(2,1)S(1)} collective-permute-done((bf16[4,2,80,128]{3,2,1,0:T(8,128)(2,1)S(1)}, bf16[4,2,80,128]{3,2,1,0:T(8,128)(2,1)S(1)}, u32[]{:S(2)}, u32[]{:S(2)}) %collective-permute-start.8) | collective-permute-done | bytes 163872 | tf_op jit(solution)/shard_map/ppermute | solution.py:20
  43.7 2.5 %collective-permute-start.12 = (bf16[2,80,128]{2,1,0:T(8,128)(2,1)S(1)}, bf16[2,80,128]{2,1,0:T(8,128)(2,1)S(1)}, u32[]{:S(2)}, u32[]{:S(2)}) collective-permute-start(bf16[2,80,128]{2,1,0:T(8,128)(2,1)S(1)} %get-tuple-element.83), channel_id=1, source_target_pairs={{0,6},{1,7},{2,4},{3,5},{4,2},{5,3},{6,0},{7,1},{8,14},{9,15},{10,... | collective-permute-start | bytes 122888 | tf_op jit(solution)/shard_map/ppermute | solution.py:20
  46.3 3.8 %collective-permute-start.11 = (bf16[2,80,128]{2,1,0:T(8,128)(2,1)S(1)}, bf16[2,80,128]{2,1,0:T(8,128)(2,1)S(1)}, u32[]{:S(2)}, u32[]{:S(2)}) collective-permute-start(bf16[2,80,128]{2,1,0:T(8,128)(2,1)S(1)} %get-tuple-element.84), channel_id=1, source_target_pairs={{0,4},{1,5},{2,6},{3,7},{4,0},{5,1},{6,2},{7,3},{8,12},{9,13},{10,... | collective-permute-start | bytes 122888 | tf_op jit(solution)/shard_map/ppermute | solution.py:20
  50.1 2.4 %collective-permute-done.11.refs_2_ = bf16[2,80,128]{2,1,0:T(8,128)(2,1)S(1)} collective-permute-done((bf16[2,80,128]{2,1,0:T(8,128)(2,1)S(1)}, bf16[2,80,128]{2,1,0:T(8,128)(2,1)S(1)}, u32[]{:S(2)}, u32[]{:S(2)}) %collective-permute-start.11) | collective-permute-done | bytes 40992 | tf_op jit(solution)/shard_map/ppermute | solution.py:20
  56.4 1.5 %collective-permute-start.15 = (bf16[128,768]{1,0:T(8,128)(2,1)S(1)}, bf16[128,768]{1,0:T(8,128)(2,1)S(1)}, u32[]{:S(2)}, u32[]{:S(2)}) collective-permute-start(bf16[128,768]{1,0:T(8,128)(2,1)S(1)} %convert_element_type.48), channel_id=1, source_target_pairs={{0,16},{8,24},{16,0},{24,8},{1,17},{9,25},{17,1},{25,9},{2,18},{10... | collective-permute-start | bytes 589832 | tf_op jit(solution)/shard_map/ppermute | solution.py:20
  58.8 3.4 %collective-permute-done.15 = bf16[128,768]{1,0:T(8,128)(2,1)S(1)} collective-permute-done((bf16[128,768]{1,0:T(8,128)(2,1)S(1)}, bf16[128,768]{1,0:T(8,128)(2,1)S(1)}, u32[]{:S(2)}, u32[]{:S(2)}) %collective-permute-start.15) | collective-permute-done | bytes 196640 | tf_op jit(solution)/shard_map/ppermute | solution.py:20
  62.2 1.6 %collective-permute-start.16 = (bf16[128,768]{1,0:T(8,128)(2,1)S(1)}, bf16[128,768]{1,0:T(8,128)(2,1)S(1)}, u32[]{:S(2)}, u32[]{:S(2)}) collective-permute-start(bf16[128,768]{1,0:T(8,128)(2,1)S(1)} %get-tuple-element.74), channel_id=1, source_target_pairs={{0,8},{8,0},{16,24},{24,16},{1,9},{9,1},{17,25},{25,17},{2,10},{10... | collective-permute-start | bytes 589832 | tf_op jit(solution)/shard_map/ppermute | solution.py:20
  65.2 2.8 %collective-permute-done.16.last_got_ref = bf16[128,768]{1,0:T(8,128)(2,1)S(1)} collective-permute-done((bf16[128,768]{1,0:T(8,128)(2,1)S(1)}, bf16[128,768]{1,0:T(8,128)(2,1)S(1)}, u32[]{:S(2)}, u32[]{:S(2)}) %collective-permute-start.16) | collective-permute-done | bytes 196640 | tf_op jit(solution)/shard_map/ppermute | solution.py:20
  67.9 2.9 %collective-permute-done.14.first_got_ref = bf16[128,768]{1,0:T(8,128)(2,1)S(1)} collective-permute-done((bf16[128,768]{1,0:T(8,128)(2,1)S(1)}, bf16[128,768]{1,0:T(8,128)(2,1)S(1)}, u32[]{:S(2)}, u32[]{:S(2)}) %collective-permute-start.14) | collective-permute-done | bytes 196640 | tf_op jit(solution)/shard_map/ppermute | solution.py:20
  70.8 5.8 %shard_map.75 = (bf16[640,128]{1,0:T(8,128)(2,1)S(1)}, f32[2,64,384]{2,1,0:T(8,128)}) custom-call(s32[1]{0:T(128)} %bitcast.place_ref, f32[128,768]{1,0:T(8,128)S(1)} %get-tuple-element.77.first_ref, bf16[128,768]{1,0:T(8,128)(2,1)S(1)} %collective-permute-done.14.first_got_ref, f32[128,768]{1,0:T(8,128)S(1)} %get-tuple-element.75.last_ref, ...), custom_call_target="tpu_custom_call" | custom-call | tf_op jit(solution)/shard_map/pallas_call | solution.py:367
  76.6 1.9 %collective-permute-done.17.block_ref = bf16[528,1024]{1,0:T(8,128)(2,1)} collective-permute-done((bf16[528,1024]{1,0:T(8,128)(2,1)S(1)}, bf16[528,1024]{1,0:T(8,128)(2,1)}, u32[]{:S(2)}, u32[]{:S(2)}) %collective-permute-start.17) | collective-permute-done | bytes 1081376 | tf_op jit(solution)/shard_map/ppermute | solution.py:20
  78.6 1.5 %collective-permute-start.18 = (bf16[4,80,128]{2,1,0:T(8,128)(2,1)S(1)}, bf16[4,80,128]{2,1,0:T(8,128)(2,1)S(1)}, u32[]{:S(2)}, u32[]{:S(2)}) collective-permute-start(bf16[4,80,128]{2,1,0:T(8,128)(2,1)S(1)} %get-tuple-element.81), channel_id=1, source_target_pairs={{0,4},{1,5},{2,6},{3,7},{4,0},{5,1},{6,2},{7,3},{8,12},{9,13},{10,... | collective-permute-start | bytes 245768 | tf_op jit(solution)/shard_map/ppermute | solution.py:20
  80.1 3.0 %shard_map.76.refs_6_ = bf16[4,4,80,1024]{3,2,1,0:T(8,128)(2,1)S(1)} custom-call(s32[1]{0:T(128)} %bitcast.12.place_ref, bf16[528,1024]{1,0:T(8,128)(2,1)} %collective-permute-done.17.block_ref), custom_call_target="tpu_custom_call" | custom-call | tf_op jit(solution)/shard_map/pallas_call | solution.py:411
  83.1 3.0 %collective-permute-done.18.refs_0_ = bf16[4,80,128]{2,1,0:T(8,128)(2,1)S(1)} collective-permute-done((bf16[4,80,128]{2,1,0:T(8,128)(2,1)S(1)}, bf16[4,80,128]{2,1,0:T(8,128)(2,1)S(1)}, u32[]{:S(2)}, u32[]{:S(2)}) %collective-permute-start.18) | collective-permute-done | bytes 81952 | tf_op jit(solution)/shard_map/ppermute | solution.py:20
  86.7 2.4 %collective-permute-start.20 = (bf16[4,80,128]{2,1,0:T(8,128)(2,1)S(1)}, bf16[4,80,128]{2,1,0:T(8,128)(2,1)S(1)}, u32[]{:S(2)}, u32[]{:S(2)}) collective-permute-start(bf16[4,80,128]{2,1,0:T(8,128)(2,1)S(1)} %collective-permute-done.18.refs_0_), channel_id=1, source_target_pairs={{0,16},{8,24},{16,0},{24,8},{1,17},{9,25},{17,1},{25,9},{2,18},{10... | collective-permute-start | bytes 245768 | tf_op jit(solution)/shard_map/ppermute | solution.py:20
  89.7 3.0 %shard_map.77.refs_7_ = bf16[4,4,80,1024]{3,2,1,0:T(8,128)(2,1)S(1)} custom-call(s32[1]{0:T(128)} %bitcast.12.place_ref, bf16[528,1024]{1,0:T(8,128)(2,1)} %collective-permute-done.22.block_ref), custom_call_target="tpu_custom_call" | custom-call | tf_op jit(solution)/shard_map/pallas_call | solution.py:411
  95.1 1.5 %collective-permute-start.25 = (bf16[4,80,128]{2,1,0:T(8,128)(2,1)S(1)}, bf16[4,80,128]{2,1,0:T(8,128)(2,1)S(1)}, u32[]{:S(2)}, u32[]{:S(2)}) collective-permute-start(bf16[4,80,128]{2,1,0:T(8,128)(2,1)S(1)} %get-tuple-element.72.refs_0_), channel_id=1, source_target_pairs={{0,24},{8,16},{16,8},{24,0},{1,25},{9,17},{17,9},{25,1},{2,26},{10... | collective-permute-start | bytes 245768 | tf_op jit(solution)/shard_map/ppermute | solution.py:20
  98.6 2.3 %collective-permute-done.25.refs_3_ = bf16[4,80,128]{2,1,0:T(8,128)(2,1)S(1)} collective-permute-done((bf16[4,80,128]{2,1,0:T(8,128)(2,1)S(1)}, bf16[4,80,128]{2,1,0:T(8,128)(2,1)S(1)}, u32[]{:S(2)}, u32[]{:S(2)}) %collective-permute-start.25) | collective-permute-done | bytes 81952 | tf_op jit(solution)/shard_map/ppermute | solution.py:20
  103.4 5.0 %collective-permute-done.26 = bf16[2,64,1024]{2,1,0:T(8,128)(2,1)S(1)} collective-permute-done((bf16[2,64,1024]{2,1,0:T(8,128)(2,1)S(1)}, bf16[2,64,1024]{2,1,0:T(8,128)(2,1)S(1)}, u32[]{:S(2)}, u32[]{:S(2)}) %collective-permute-start.26) | collective-permute-done | bytes 262176 | tf_op jit(solution)/shard_map/ppermute | solution.py:20
  (58 shorter events, 22.0 us)
Async XLA Ops:
  0.6 14.5 %collective-permute-start.5 = (bf16[128,1024]{1,0:T(8,128)(2,1)}, bf16[128,1024]{1,0:T(8,128)(2,1)S(1)}, u32[]{:S(2)}, u32[]{:S(2)}) collective-permute-start(bf16[128,1024]{1,0:T(8,128)(2,1)} %bitcast.41), channel_id=1, source_target_pairs={{0,2},{1,3},{2,0},{3,1},{4,6},{5,7},{6,4},{7,5},{8,10},{9,11},{10,... | collective-permute-start | bytes 786440 | tf_op jit(solution)/shard_map/ppermute | solution.py:20
  3.7 21.6 %collective-permute-start.4 = (bf16[128,1024]{1,0:T(8,128)(2,1)}, bf16[128,1024]{1,0:T(8,128)(2,1)S(1)}, u32[]{:S(2)}, u32[]{:S(2)}) collective-permute-start(bf16[128,1024]{1,0:T(8,128)(2,1)} %bitcast.42), channel_id=1, source_target_pairs={{0,4},{1,5},{2,6},{3,7},{4,0},{5,1},{6,2},{7,3},{8,12},{9,13},{10,... | collective-permute-start | bytes 786440 | tf_op jit(solution)/shard_map/ppermute | solution.py:20
  6.3 19.0 %collective-permute-start.3 = (bf16[128,1024]{1,0:T(8,128)(2,1)}, bf16[128,1024]{1,0:T(8,128)(2,1)S(1)}, u32[]{:S(2)}, u32[]{:S(2)}) collective-permute-start(bf16[128,1024]{1,0:T(8,128)(2,1)} %bitcast.43), channel_id=1, source_target_pairs={{0,6},{1,7},{2,4},{3,5},{4,2},{5,3},{6,0},{7,1},{8,14},{9,15},{10,... | collective-permute-start | bytes 786440 | tf_op jit(solution)/shard_map/ppermute | solution.py:20
  6.3 1.2 %copy-start.3 = (bf16[128,4096]{1,0:T(8,128)(2,1)S(1)}, bf16[128,4096]{1,0:T(8,128)(2,1)}, u32[]{:S(2)}) copy-start(bf16[128,4096]{1,0:T(8,128)(2,1)} %cotangent_ref.1) | copy-start | bytes 3145732
  7.5 0.7 copy-start.4
  9.0 17.3 %collective-permute-start = (bf16[144,1024]{1,0:T(8,128)(2,1)S(1)}, bf16[144,1024]{1,0:T(8,128)(2,1)S(1)}, u32[]{:S(2)}, u32[]{:S(2)}) collective-permute-start(bf16[144,1024]{1,0:T(8,128)(2,1)S(1)} %get-tuple-element.39), channel_id=1, source_target_pairs={{0,8},{8,0},{16,24},{24,16},{1,9},{9,1},{17,25},{25,17},{2,10},{10... | collective-permute-start | bytes 884744 | tf_op jit(solution)/shard_map/ppermute | solution.py:20
  10.8 15.6 %collective-permute-start.1 = (bf16[144,1024]{1,0:T(8,128)(2,1)S(1)}, bf16[144,1024]{1,0:T(8,128)(2,1)S(1)}, u32[]{:S(2)}, u32[]{:S(2)}) collective-permute-start(bf16[144,1024]{1,0:T(8,128)(2,1)S(1)} %get-tuple-element.40), channel_id=1, source_target_pairs={{0,16},{8,24},{16,0},{24,8},{1,17},{9,25},{17,1},{25,9},{2,18},{10... | collective-permute-start | bytes 884744 | tf_op jit(solution)/shard_map/ppermute | solution.py:20
  15.1 11.3 %collective-permute-start.2 = (bf16[144,1024]{1,0:T(8,128)(2,1)S(1)}, bf16[144,1024]{1,0:T(8,128)(2,1)S(1)}, u32[]{:S(2)}, u32[]{:S(2)}) collective-permute-start(bf16[144,1024]{1,0:T(8,128)(2,1)S(1)} %get-tuple-element.41), channel_id=1, source_target_pairs={{0,24},{8,16},{16,8},{24,0},{1,25},{9,17},{17,9},{25,1},{2,26},{10... | collective-permute-start | bytes 884744 | tf_op jit(solution)/shard_map/ppermute | solution.py:20
  28.3 2.8 %collective-permute-start.6 = (bf16[528,1024]{1,0:T(8,128)(2,1)S(1)}, bf16[528,1024]{1,0:T(8,128)(2,1)S(1)}, u32[]{:S(2)}, u32[]{:S(2)}) collective-permute-start(bf16[528,1024]{1,0:T(8,128)(2,1)S(1)} %shard_map.69.block_ref), channel_id=1, source_target_pairs={{0,1},{1,0},{2,3},{3,2},{4,5},{5,4},{6,7},{7,6},{8,9},{9,8},{10,11... | collective-permute-start | bytes 3244040 | tf_op jit(solution)/shard_map/ppermute | solution.py:20
  32.8 8.6 %collective-permute-start.9 = (bf16[4,2,80,128]{3,2,1,0:T(8,128)(2,1)S(1)}, bf16[4,2,80,128]{3,2,1,0:T(8,128)(2,1)S(1)}, u32[]{:S(2)}, u32[]{:S(2)}) collective-permute-start(bf16[4,2,80,128]{3,2,1,0:T(8,128)(2,1)S(1)} %get-tuple-element.78), channel_id=1, source_target_pairs={{0,24},{8,16},{16,8},{24,0},{1,25},{9,17},{17,9},{25,1},{2,26},{10... | collective-permute-start | bytes 491528 | tf_op jit(solution)/shard_map/ppermute | solution.py:20
  35.3 8.2 %collective-permute-start.8 = (bf16[4,2,80,128]{3,2,1,0:T(8,128)(2,1)S(1)}, bf16[4,2,80,128]{3,2,1,0:T(8,128)(2,1)S(1)}, u32[]{:S(2)}, u32[]{:S(2)}) collective-permute-start(bf16[4,2,80,128]{3,2,1,0:T(8,128)(2,1)S(1)} %get-tuple-element.79), channel_id=1, source_target_pairs={{0,16},{8,24},{16,0},{24,8},{1,17},{9,25},{17,1},{25,9},{2,18},{10... | collective-permute-start | bytes 491528 | tf_op jit(solution)/shard_map/ppermute | solution.py:20
  35.8 7.8 %collective-permute-start.7 = (bf16[4,2,80,128]{3,2,1,0:T(8,128)(2,1)S(1)}, bf16[4,2,80,128]{3,2,1,0:T(8,128)(2,1)S(1)}, u32[]{:S(2)}, u32[]{:S(2)}) collective-permute-start(bf16[4,2,80,128]{3,2,1,0:T(8,128)(2,1)S(1)} %get-tuple-element.80), channel_id=1, source_target_pairs={{0,8},{8,0},{16,24},{24,16},{1,9},{9,1},{17,25},{25,17},{2,10},{10... | collective-permute-start | bytes 491528 | tf_op jit(solution)/shard_map/ppermute | solution.py:20
  38.1 16.9 %copy-start.2 = (bf16[2,1,640,1536]{3,2,1,0:T(8,128)(2,1)S(1)}, bf16[2,1,640,1536]{3,2,1,0:T(8,128)(2,1)}, u32[]{:S(2)}) copy-start(bf16[2,1,640,1536]{3,2,1,0:T(8,128)(2,1)} %param.8) | copy-start | bytes 11796484
  40.0 1.5 %copy-start = (bf16[4,4,80,1024]{3,2,1,0:T(8,128)(2,1)}, bf16[4,4,80,1024]{3,2,1,0:T(8,128)(2,1)S(1)}, u32[]{:S(2)}) copy-start(bf16[4,4,80,1024]{3,2,1,0:T(8,128)(2,1)S(1)} %shard_map.73.refs_5_) | copy-start | bytes 7864324
  43.7 6.4 %collective-permute-start.12 = (bf16[2,80,128]{2,1,0:T(8,128)(2,1)S(1)}, bf16[2,80,128]{2,1,0:T(8,128)(2,1)S(1)}, u32[]{:S(2)}, u32[]{:S(2)}) collective-permute-start(bf16[2,80,128]{2,1,0:T(8,128)(2,1)S(1)} %get-tuple-element.83), channel_id=1, source_target_pairs={{0,6},{1,7},{2,4},{3,5},{4,2},{5,3},{6,0},{7,1},{8,14},{9,15},{10,... | collective-permute-start | bytes 122888 | tf_op jit(solution)/shard_map/ppermute | solution.py:20
  46.3 6.3 %collective-permute-start.11 = (bf16[2,80,128]{2,1,0:T(8,128)(2,1)S(1)}, bf16[2,80,128]{2,1,0:T(8,128)(2,1)S(1)}, u32[]{:S(2)}, u32[]{:S(2)}) collective-permute-start(bf16[2,80,128]{2,1,0:T(8,128)(2,1)S(1)} %get-tuple-element.84), channel_id=1, source_target_pairs={{0,4},{1,5},{2,6},{3,7},{4,0},{5,1},{6,2},{7,3},{8,12},{9,13},{10,... | collective-permute-start | bytes 122888 | tf_op jit(solution)/shard_map/ppermute | solution.py:20
  50.0 4.0 %collective-permute-start.10 = (bf16[2,80,128]{2,1,0:T(8,128)(2,1)S(1)}, bf16[2,80,128]{2,1,0:T(8,128)(2,1)S(1)}, u32[]{:S(2)}, u32[]{:S(2)}) collective-permute-start(bf16[2,80,128]{2,1,0:T(8,128)(2,1)S(1)} %get-tuple-element.85), channel_id=1, source_target_pairs={{0,2},{1,3},{2,0},{3,1},{4,6},{5,7},{6,4},{7,5},{8,10},{9,11},{10,... | collective-permute-start | bytes 122888 | tf_op jit(solution)/shard_map/ppermute | solution.py:20
  54.0 24.5 %collective-permute-start.17 = (bf16[528,1024]{1,0:T(8,128)(2,1)S(1)}, bf16[528,1024]{1,0:T(8,128)(2,1)}, u32[]{:S(2)}, u32[]{:S(2)}) collective-permute-start(bf16[528,1024]{1,0:T(8,128)(2,1)S(1)} %shard_map.69.block_ref), channel_id=1, source_target_pairs={{0,2},{1,3},{2,0},{3,1},{4,6},{5,7},{6,4},{7,5},{8,10},{9,11},{10,... | collective-permute-start | bytes 3244040 | tf_op jit(solution)/shard_map/ppermute | solution.py:20
  56.4 5.7 %collective-permute-start.15 = (bf16[128,768]{1,0:T(8,128)(2,1)S(1)}, bf16[128,768]{1,0:T(8,128)(2,1)S(1)}, u32[]{:S(2)}, u32[]{:S(2)}) collective-permute-start(bf16[128,768]{1,0:T(8,128)(2,1)S(1)} %convert_element_type.48), channel_id=1, source_target_pairs={{0,16},{8,24},{16,0},{24,8},{1,17},{9,25},{17,1},{25,9},{2,18},{10... | collective-permute-start | bytes 589832 | tf_op jit(solution)/shard_map/ppermute | solution.py:20
  57.9 7.1 %collective-permute-start.13 = (bf16[128,768]{1,0:T(8,128)(2,1)S(1)}, bf16[128,768]{1,0:T(8,128)(2,1)S(1)}, u32[]{:S(2)}, u32[]{:S(2)}) collective-permute-start(bf16[128,768]{1,0:T(8,128)(2,1)S(1)} %convert_element_type.45), channel_id=1, source_target_pairs={{0,8},{8,0},{16,24},{24,16},{1,9},{9,1},{17,25},{25,17},{2,10},{10... | collective-permute-start | bytes 589832 | tf_op jit(solution)/shard_map/ppermute | solution.py:20
  62.2 5.7 %collective-permute-start.16 = (bf16[128,768]{1,0:T(8,128)(2,1)S(1)}, bf16[128,768]{1,0:T(8,128)(2,1)S(1)}, u32[]{:S(2)}, u32[]{:S(2)}) collective-permute-start(bf16[128,768]{1,0:T(8,128)(2,1)S(1)} %get-tuple-element.74), channel_id=1, source_target_pairs={{0,8},{8,0},{16,24},{24,16},{1,9},{9,1},{17,25},{25,17},{2,10},{10... | collective-permute-start | bytes 589832 | tf_op jit(solution)/shard_map/ppermute | solution.py:20
  65.1 5.7 %collective-permute-start.14 = (bf16[128,768]{1,0:T(8,128)(2,1)S(1)}, bf16[128,768]{1,0:T(8,128)(2,1)S(1)}, u32[]{:S(2)}, u32[]{:S(2)}) collective-permute-start(bf16[128,768]{1,0:T(8,128)(2,1)S(1)} %get-tuple-element.76), channel_id=1, source_target_pairs={{0,16},{8,24},{16,0},{24,8},{1,17},{9,25},{17,1},{25,9},{2,18},{10... | collective-permute-start | bytes 589832 | tf_op jit(solution)/shard_map/ppermute | solution.py:20
  78.6 11.2 %collective-permute-start.22 = (bf16[528,1024]{1,0:T(8,128)(2,1)}, bf16[528,1024]{1,0:T(8,128)(2,1)}, u32[]{:S(2)}, u32[]{:S(2)}) collective-permute-start(bf16[528,1024]{1,0:T(8,128)(2,1)} %collective-permute-done.17.block_ref), channel_id=1, source_target_pairs={{0,1},{1,0},{2,3},{3,2},{4,5},{5,4},{6,7},{7,6},{8,9},{9,8},{10,11... | collective-permute-start | bytes 3244040 | tf_op jit(solution)/shard_map/ppermute | solution.py:20
  78.6 7.6 %collective-permute-start.18 = (bf16[4,80,128]{2,1,0:T(8,128)(2,1)S(1)}, bf16[4,80,128]{2,1,0:T(8,128)(2,1)S(1)}, u32[]{:S(2)}, u32[]{:S(2)}) collective-permute-start(bf16[4,80,128]{2,1,0:T(8,128)(2,1)S(1)} %get-tuple-element.81), channel_id=1, source_target_pairs={{0,4},{1,5},{2,6},{3,7},{4,0},{5,1},{6,2},{7,3},{8,12},{9,13},{10,... | collective-permute-start | bytes 245768 | tf_op jit(solution)/shard_map/ppermute | solution.py:20
  83.1 10.4 %copy-start.1 = (bf16[4,4,80,1024]{3,2,1,0:T(8,128)(2,1)S(1)}, bf16[4,4,80,1024]{3,2,1,0:T(8,128)(2,1)}, u32[]{:S(2)}) copy-start(bf16[4,4,80,1024]{3,2,1,0:T(8,128)(2,1)} %copy-done) | copy-start | bytes 7864324
  86.2 6.6 %collective-permute-start.21 = (bf16[4,80,128]{2,1,0:T(8,128)(2,1)S(1)}, bf16[4,80,128]{2,1,0:T(8,128)(2,1)S(1)}, u32[]{:S(2)}, u32[]{:S(2)}) collective-permute-start(bf16[4,80,128]{2,1,0:T(8,128)(2,1)S(1)} %collective-permute-done.18.refs_0_), channel_id=1, source_target_pairs={{0,24},{8,16},{16,8},{24,0},{1,25},{9,17},{17,9},{25,1},{2,26},{10... | collective-permute-start | bytes 245768 | tf_op jit(solution)/shard_map/ppermute | solution.py:20
  86.7 6.2 %collective-permute-start.20 = (bf16[4,80,128]{2,1,0:T(8,128)(2,1)S(1)}, bf16[4,80,128]{2,1,0:T(8,128)(2,1)S(1)}, u32[]{:S(2)}, u32[]{:S(2)}) collective-permute-start(bf16[4,80,128]{2,1,0:T(8,128)(2,1)S(1)} %collective-permute-done.18.refs_0_), channel_id=1, source_target_pairs={{0,16},{8,24},{16,0},{24,8},{1,17},{9,25},{17,1},{25,9},{2,18},{10... | collective-permute-start | bytes 245768 | tf_op jit(solution)/shard_map/ppermute | solution.py:20
  89.1 4.4 %collective-permute-start.19 = (bf16[4,80,128]{2,1,0:T(8,128)(2,1)S(1)}, bf16[4,80,128]{2,1,0:T(8,128)(2,1)S(1)}, u32[]{:S(2)}, u32[]{:S(2)}) collective-permute-start(bf16[4,80,128]{2,1,0:T(8,128)(2,1)S(1)} %collective-permute-done.18.refs_0_), channel_id=1, source_target_pairs={{0,8},{8,0},{16,24},{24,16},{1,9},{9,1},{17,25},{25,17},{2,10},{10... | collective-permute-start | bytes 245768 | tf_op jit(solution)/shard_map/ppermute | solution.py:20
  95.0 13.4 %collective-permute-start.26 = (bf16[2,64,1024]{2,1,0:T(8,128)(2,1)S(1)}, bf16[2,64,1024]{2,1,0:T(8,128)(2,1)S(1)}, u32[]{:S(2)}, u32[]{:S(2)}) collective-permute-start(bf16[2,64,1024]{2,1,0:T(8,128)(2,1)S(1)} %shard_map.78), channel_id=1, source_target_pairs={{0,4},{1,5},{2,6},{3,7},{4,0},{5,1},{6,2},{7,3},{8,12},{9,13},{10,... | collective-permute-start | bytes 786440 | tf_op jit(solution)/shard_map/ppermute | solution.py:20
  95.1 5.8 %collective-permute-start.25 = (bf16[4,80,128]{2,1,0:T(8,128)(2,1)S(1)}, bf16[4,80,128]{2,1,0:T(8,128)(2,1)S(1)}, u32[]{:S(2)}, u32[]{:S(2)}) collective-permute-start(bf16[4,80,128]{2,1,0:T(8,128)(2,1)S(1)} %get-tuple-element.72.refs_0_), channel_id=1, source_target_pairs={{0,24},{8,16},{16,8},{24,0},{1,25},{9,17},{17,9},{25,1},{2,26},{10... | collective-permute-start | bytes 245768 | tf_op jit(solution)/shard_map/ppermute | solution.py:20
  96.6 5.0 %collective-permute-start.24 = (bf16[4,80,128]{2,1,0:T(8,128)(2,1)S(1)}, bf16[4,80,128]{2,1,0:T(8,128)(2,1)S(1)}, u32[]{:S(2)}, u32[]{:S(2)}) collective-permute-start(bf16[4,80,128]{2,1,0:T(8,128)(2,1)S(1)} %get-tuple-element.72.refs_0_), channel_id=1, source_target_pairs={{0,16},{8,24},{16,0},{24,8},{1,17},{9,25},{17,1},{25,9},{2,18},{10... | collective-permute-start | bytes 245768 | tf_op jit(solution)/shard_map/ppermute | solution.py:20
  97.5 4.4 %collective-permute-start.23 = (bf16[4,80,128]{2,1,0:T(8,128)(2,1)S(1)}, bf16[4,80,128]{2,1,0:T(8,128)(2,1)S(1)}, u32[]{:S(2)}, u32[]{:S(2)}) collective-permute-start(bf16[4,80,128]{2,1,0:T(8,128)(2,1)S(1)} %get-tuple-element.72.refs_0_), channel_id=1, source_target_pairs={{0,8},{8,0},{16,24},{24,16},{1,9},{9,1},{17,25},{25,17},{2,10},{10... | collective-permute-start | bytes 245768 | tf_op jit(solution)/shard_map/ppermute | solution.py:20
  (1 other events, 0.7 us)

commit v5 on v4

--- a/solution.py
+++ b/solution.py
@@ -9,7 +9,7 @@
 
 CORES = 2
 PIVOTS = 4
-VMEM = 16 << 20
+VMEM = 32 << 20
 HIGHEST = lax.Precision.HIGHEST
 NT = (((1,), (1,)), ((), ()))
 TN = (((0,), (0,)), ((), ()))
@@ -505,10 +505,10 @@
         summed = summed + value.astype(jnp.float32)
     summed = summed.astype(jnp.bfloat16)[::-1]
     arrived = [summed[0]] + [exchange(summed[k], "expert", CORES * k) for k in range(1, chips)]
+    parts = left_partial(place, arrived, own_hidden, capacity)
     if span > 1:
-        arrived, own = tie((arrived, own))
-        near = exchange(own, "expert", CORES)
-    parts = left_partial(place, arrived, own_hidden, capacity)
+        _, near = tie((arrived, own))
+        near = exchange(near, "expert", CORES)
     turns = sum_steps(members)
     rounds = len(turns[0])
     for index in range(rounds):

time: 110 us -> 110 us (level)
  no operation moved by 1% of the time
where the time goes in v5:
time: 110 us; the launch traced here: 109 us
  waiting for transfers between devices  43.5 us (40%)
  starting transfers between devices  35.2 us (32%)
  Pallas kernels  23.3 us (21%)
  local copies, waits for them, and re-layouts  4.14 us (4%)
  other arithmetic  2.25 us (2%)
    ppermute x27, waiting for transfers between devices, exchange(): return lax.ppermute(value, axis, [(i, i ^ distance) for i in range(size)])  43.5 us
    ppermute x27, starting transfers between devices, exchange(): return lax.ppermute(value, axis, [(i, i ^ distance) for i in range(size)])  35.2 us
    pallas_call x4, Pallas kernels, dispatch(): pl.pallas_call(functools.partial(dispatch_kernel, sizes), out_shape=jax.S...  9.62 us
    pallas_call x1, Pallas kernels, whiten_and_map(): pl.pallas_call(whiten_kernel, out_shape=(jax.ShapeDtypeStruct((slots, wid...  5.78 us
    unnamed x12, local copies, waits for them, and re-layouts  4.08 us
    pallas_call x2, Pallas kernels, project(): pl.pallas_call(functools.partial(project_kernel, sizes), out_shape=jax.Sh...  3.44 us
    pallas_call x2, Pallas kernels, right_factor(): pl.pallas_call(functools.partial(right_kernel, len(mapped_groups), owner)...  2.89 us
  transfers between devices with their start and end apart: 27, of which 19 were waited for; matrix products, arithmetic and copies ran while one was open for 1% of the time, Pallas kernels for 17%

profile of v5, /device:TPU:0, one launch (start us, length us, event | category | flops | bytes accessed | tf_op | source)
XLA Modules:
  0.0 109.3 jit_solution(539255735350236123)
XLA Ops:
  0.6 3.1 %collective-permute-start.5 = (bf16[128,1024]{1,0:T(8,128)(2,1)}, bf16[128,1024]{1,0:T(8,128)(2,1)S(1)}, u32[]{:S(2)}, u32[]{:S(2)}) collective-permute-start(bf16[128,1024]{1,0:T(8,128)(2,1)} %bitcast.41), channel_id=1, source_target_pairs={{0,2},{1,3},{2,0},{3,1},{4,6},{5,7},{6,4},{7,5},{8,10},{9,11},{10,... | collective-permute-start | bytes 786440 | tf_op jit(solution)/shard_map/ppermute | solution.py:20
  3.7 2.6 %collective-permute-start.4 = (bf16[128,1024]{1,0:T(8,128)(2,1)}, bf16[128,1024]{1,0:T(8,128)(2,1)S(1)}, u32[]{:S(2)}, u32[]{:S(2)}) collective-permute-start(bf16[128,1024]{1,0:T(8,128)(2,1)} %bitcast.42), channel_id=1, source_target_pairs={{0,4},{1,5},{2,6},{3,7},{4,0},{5,1},{6,2},{7,3},{8,12},{9,13},{10,... | collective-permute-start | bytes 786440 | tf_op jit(solution)/shard_map/ppermute | solution.py:20
  9.0 1.8 %collective-permute-start = (bf16[144,1024]{1,0:T(8,128)(2,1)S(1)}, bf16[144,1024]{1,0:T(8,128)(2,1)S(1)}, u32[]{:S(2)}, u32[]{:S(2)}) collective-permute-start(bf16[144,1024]{1,0:T(8,128)(2,1)S(1)} %get-tuple-element.35), channel_id=1, source_target_pairs={{0,8},{8,0},{16,24},{24,16},{1,9},{9,1},{17,25},{25,17},{2,10},{10... | collective-permute-start | bytes 884744 | tf_op jit(solution)/shard_map/ppermute | solution.py:20
  10.8 1.5 %collective-permute-start.1 = (bf16[144,1024]{1,0:T(8,128)(2,1)S(1)}, bf16[144,1024]{1,0:T(8,128)(2,1)S(1)}, u32[]{:S(2)}, u32[]{:S(2)}) collective-permute-start(bf16[144,1024]{1,0:T(8,128)(2,1)S(1)} %get-tuple-element.36), channel_id=1, source_target_pairs={{0,16},{8,24},{16,0},{24,8},{1,17},{9,25},{17,1},{25,9},{2,18},{10... | collective-permute-start | bytes 884744 | tf_op jit(solution)/shard_map/ppermute | solution.py:20
  12.3 2.8 %collective-permute-done.5 = bf16[128,1024]{1,0:T(8,128)(2,1)S(1)} collective-permute-done((bf16[128,1024]{1,0:T(8,128)(2,1)}, bf16[128,1024]{1,0:T(8,128)(2,1)S(1)}, u32[]{:S(2)}, u32[]{:S(2)}) %collective-permute-start.5) | collective-permute-done | bytes 262176 | tf_op jit(solution)/shard_map/ppermute | solution.py:20
  15.1 2.6 %collective-permute-start.2 = (bf16[144,1024]{1,0:T(8,128)(2,1)S(1)}, bf16[144,1024]{1,0:T(8,128)(2,1)S(1)}, u32[]{:S(2)}, u32[]{:S(2)}) collective-permute-start(bf16[144,1024]{1,0:T(8,128)(2,1)S(1)} %get-tuple-element.37), channel_id=1, source_target_pairs={{0,24},{8,16},{16,8},{24,0},{1,25},{9,17},{17,9},{25,1},{2,26},{10... | collective-permute-start | bytes 884744 | tf_op jit(solution)/shard_map/ppermute | solution.py:20
  17.8 7.5 %collective-permute-done.4 = bf16[128,1024]{1,0:T(8,128)(2,1)S(1)} collective-permute-done((bf16[128,1024]{1,0:T(8,128)(2,1)}, bf16[128,1024]{1,0:T(8,128)(2,1)S(1)}, u32[]{:S(2)}, u32[]{:S(2)}) %collective-permute-start.4) | collective-permute-done | bytes 262176 | tf_op jit(solution)/shard_map/ppermute | solution.py:20
  26.5 1.7 %shard_map.70.refs_0_ = bf16[4,4,1,80,128]{4,3,2,1,0:T(8,128)(2,1)S(1)} custom-call(s32[2]{0:T(128)S(1)} %pad_add_fusion.place_ref, bf16[528,1024]{1,0:T(8,128)(2,1)S(1)} %shard_map.69.block_ref, bf16[512,1024]{1,0:T(8,128)(2,1)S(1)} %pad_maximum_fusion.factors_ref), custom_call_target="tpu_custom_call" | custom-call | tf_op jit(solution)/shard_map/pallas_call | solution.py:216
  28.3 2.7 %collective-permute-done.6.block_ref = bf16[528,1024]{1,0:T(8,128)(2,1)S(1)} collective-permute-done((bf16[528,1024]{1,0:T(8,128)(2,1)S(1)}, bf16[528,1024]{1,0:T(8,128)(2,1)S(1)}, u32[]{:S(2)}, u32[]{:S(2)}) %collective-permute-start.6) | collective-permute-done | bytes 1081376 | tf_op jit(solution)/shard_map/ppermute | solution.py:20
  31.0 1.7 %shard_map.71 = bf16[4,4,2,80,128]{4,3,2,1,0:T(8,128)(2,1)S(1)} custom-call(s32[2]{0:T(128)S(1)} %pad_add_fusion.place_ref, bf16[528,1024]{1,0:T(8,128)(2,1)S(1)} %collective-permute-done.6.block_ref, bf16[512,1024]{1,0:T(8,128)(2,1)S(1)} %pad_maximum_fusion.factors_ref, bf16[4,4,1,80,128]{4,3,2,1,0:T(8,128)(2,1)S(1)} %shard_map.70.refs_0_), custom_call_target="tpu_custom_call" | custom-call | tf_op jit(solution)/shard_map/pallas_call | solution.py:216
  32.8 2.5 %collective-permute-start.9 = (bf16[4,2,80,128]{3,2,1,0:T(8,128)(2,1)S(1)}, bf16[4,2,80,128]{3,2,1,0:T(8,128)(2,1)S(1)}, u32[]{:S(2)}, u32[]{:S(2)}) collective-permute-start(bf16[4,2,80,128]{3,2,1,0:T(8,128)(2,1)S(1)} %get-tuple-element.70), channel_id=1, source_target_pairs={{0,24},{8,16},{16,8},{24,0},{1,25},{9,17},{17,9},{25,1},{2,26},{10... | collective-permute-start | bytes 491528 | tf_op jit(solution)/shard_map/ppermute | solution.py:20
  36.4 1.8 %shard_map.72.refs_4_ = bf16[4,4,80,1024]{3,2,1,0:T(8,128)(2,1)S(1)} custom-call(s32[1]{0:T(128)} %bitcast.12.place_ref, bf16[528,1024]{1,0:T(8,128)(2,1)S(1)} %shard_map.69.block_ref), custom_call_target="tpu_custom_call" | custom-call | tf_op jit(solution)/shard_map/pallas_call | solution.py:411
  38.2 1.8 %shard_map.73.refs_5_ = bf16[4,4,80,1024]{3,2,1,0:T(8,128)(2,1)S(1)} custom-call(s32[1]{0:T(128)} %bitcast.12.place_ref, bf16[528,1024]{1,0:T(8,128)(2,1)S(1)} %collective-permute-done.6.block_ref), custom_call_target="tpu_custom_call" | custom-call | tf_op jit(solution)/shard_map/pallas_call | solution.py:411
  41.4 2.1 %collective-permute-done.8 = bf16[4,2,80,128]{3,2,1,0:T(8,128)(2,1)S(1)} collective-permute-done((bf16[4,2,80,128]{3,2,1,0:T(8,128)(2,1)S(1)}, bf16[4,2,80,128]{3,2,1,0:T(8,128)(2,1)S(1)}, u32[]{:S(2)}, u32[]{:S(2)}) %collective-permute-start.8) | collective-permute-done | bytes 163872 | tf_op jit(solution)/shard_map/ppermute | solution.py:20
  43.7 2.5 %collective-permute-start.12 = (bf16[2,80,128]{2,1,0:T(8,128)(2,1)S(1)}, bf16[2,80,128]{2,1,0:T(8,128)(2,1)S(1)}, u32[]{:S(2)}, u32[]{:S(2)}) collective-permute-start(bf16[2,80,128]{2,1,0:T(8,128)(2,1)S(1)} %get-tuple-element.75), channel_id=1, source_target_pairs={{0,6},{1,7},{2,4},{3,5},{4,2},{5,3},{6,0},{7,1},{8,14},{9,15},{10,... | collective-permute-start | bytes 122888 | tf_op jit(solution)/shard_map/ppermute | solution.py:20
  46.3 3.8 %collective-permute-start.11 = (bf16[2,80,128]{2,1,0:T(8,128)(2,1)S(1)}, bf16[2,80,128]{2,1,0:T(8,128)(2,1)S(1)}, u32[]{:S(2)}, u32[]{:S(2)}) collective-permute-start(bf16[2,80,128]{2,1,0:T(8,128)(2,1)S(1)} %get-tuple-element.76), channel_id=1, source_target_pairs={{0,4},{1,5},{2,6},{3,7},{4,0},{5,1},{6,2},{7,3},{8,12},{9,13},{10,... | collective-permute-start | bytes 122888 | tf_op jit(solution)/shard_map/ppermute | solution.py:20
  50.1 2.4 %collective-permute-done.11.refs_2_ = bf16[2,80,128]{2,1,0:T(8,128)(2,1)S(1)} collective-permute-done((bf16[2,80,128]{2,1,0:T(8,128)(2,1)S(1)}, bf16[2,80,128]{2,1,0:T(8,128)(2,1)S(1)}, u32[]{:S(2)}, u32[]{:S(2)}) %collective-permute-start.11) | collective-permute-done | bytes 40992 | tf_op jit(solution)/shard_map/ppermute | solution.py:20
  56.4 1.5 %collective-permute-start.15 = (bf16[128,768]{1,0:T(8,128)(2,1)S(1)}, bf16[128,768]{1,0:T(8,128)(2,1)S(1)}, u32[]{:S(2)}, u32[]{:S(2)}) collective-permute-start(bf16[128,768]{1,0:T(8,128)(2,1)S(1)} %convert_element_type.48), channel_id=1, source_target_pairs={{0,16},{8,24},{16,0},{24,8},{1,17},{9,25},{17,1},{25,9},{2,18},{10... | collective-permute-start | bytes 589832 | tf_op jit(solution)/shard_map/ppermute | solution.py:20
  58.8 3.4 %collective-permute-done.15 = bf16[128,768]{1,0:T(8,128)(2,1)S(1)} collective-permute-done((bf16[128,768]{1,0:T(8,128)(2,1)S(1)}, bf16[128,768]{1,0:T(8,128)(2,1)S(1)}, u32[]{:S(2)}, u32[]{:S(2)}) %collective-permute-start.15) | collective-permute-done | bytes 196640 | tf_op jit(solution)/shard_map/ppermute | solution.py:20
  62.2 1.6 %collective-permute-start.16 = (bf16[128,768]{1,0:T(8,128)(2,1)S(1)}, bf16[128,768]{1,0:T(8,128)(2,1)S(1)}, u32[]{:S(2)}, u32[]{:S(2)}) collective-permute-start(bf16[128,768]{1,0:T(8,128)(2,1)S(1)} %get-tuple-element.66), channel_id=1, source_target_pairs={{0,8},{8,0},{16,24},{24,16},{1,9},{9,1},{17,25},{25,17},{2,10},{10... | collective-permute-start | bytes 589832 | tf_op jit(solution)/shard_map/ppermute | solution.py:20
  65.2 2.8 %collective-permute-done.16.last_got_ref = bf16[128,768]{1,0:T(8,128)(2,1)S(1)} collective-permute-done((bf16[128,768]{1,0:T(8,128)(2,1)S(1)}, bf16[128,768]{1,0:T(8,128)(2,1)S(1)}, u32[]{:S(2)}, u32[]{:S(2)}) %collective-permute-start.16) | collective-permute-done | bytes 196640 | tf_op jit(solution)/shard_map/ppermute | solution.py:20
  67.9 2.9 %collective-permute-done.14.first_got_ref = bf16[128,768]{1,0:T(8,128)(2,1)S(1)} collective-permute-done((bf16[128,768]{1,0:T(8,128)(2,1)S(1)}, bf16[128,768]{1,0:T(8,128)(2,1)S(1)}, u32[]{:S(2)}, u32[]{:S(2)}) %collective-permute-start.14) | collective-permute-done | bytes 196640 | tf_op jit(solution)/shard_map/ppermute | solution.py:20
  70.8 5.8 %shard_map.75 = (bf16[640,128]{1,0:T(8,128)(2,1)S(1)}, f32[2,64,384]{2,1,0:T(8,128)}) custom-call(s32[1]{0:T(128)} %bitcast.place_ref, f32[128,768]{1,0:T(8,128)S(1)} %get-tuple-element.69.first_ref, bf16[128,768]{1,0:T(8,128)(2,1)S(1)} %collective-permute-done.14.first_got_ref, f32[128,768]{1,0:T(8,128)S(1)} %get-tuple-element.67.last_ref, ...), custom_call_target="tpu_custom_call" | custom-call | tf_op jit(solution)/shard_map/pallas_call | solution.py:367
  76.6 1.9 %collective-permute-done.17.block_ref = bf16[528,1024]{1,0:T(8,128)(2,1)} collective-permute-done((bf16[528,1024]{1,0:T(8,128)(2,1)S(1)}, bf16[528,1024]{1,0:T(8,128)(2,1)}, u32[]{:S(2)}, u32[]{:S(2)}) %collective-permute-start.17) | collective-permute-done | bytes 1081376 | tf_op jit(solution)/shard_map/ppermute | solution.py:20
  78.6 1.5 %collective-permute-start.18 = (bf16[4,80,128]{2,1,0:T(8,128)(2,1)S(1)}, bf16[4,80,128]{2,1,0:T(8,128)(2,1)S(1)}, u32[]{:S(2)}, u32[]{:S(2)}) collective-permute-start(bf16[4,80,128]{2,1,0:T(8,128)(2,1)S(1)} %get-tuple-element.73), channel_id=1, source_target_pairs={{0,4},{1,5},{2,6},{3,7},{4,0},{5,1},{6,2},{7,3},{8,12},{9,13},{10,... | collective-permute-start | bytes 245768 | tf_op jit(solution)/shard_map/ppermute | solution.py:20
  80.1 3.0 %shard_map.76.refs_6_ = bf16[4,4,80,1024]{3,2,1,0:T(8,128)(2,1)S(1)} custom-call(s32[1]{0:T(128)} %bitcast.12.place_ref, bf16[528,1024]{1,0:T(8,128)(2,1)} %collective-permute-done.17.block_ref), custom_call_target="tpu_custom_call" | custom-call | tf_op jit(solution)/shard_map/pallas_call | solution.py:411
  83.1 3.0 %collective-permute-done.18.refs_0_ = bf16[4,80,128]{2,1,0:T(8,128)(2,1)S(1)} collective-permute-done((bf16[4,80,128]{2,1,0:T(8,128)(2,1)S(1)}, bf16[4,80,128]{2,1,0:T(8,128)(2,1)S(1)}, u32[]{:S(2)}, u32[]{:S(2)}) %collective-permute-start.18) | collective-permute-done | bytes 81952 | tf_op jit(solution)/shard_map/ppermute | solution.py:20
  86.7 2.4 %collective-permute-start.20 = (bf16[4,80,128]{2,1,0:T(8,128)(2,1)S(1)}, bf16[4,80,128]{2,1,0:T(8,128)(2,1)S(1)}, u32[]{:S(2)}, u32[]{:S(2)}) collective-permute-start(bf16[4,80,128]{2,1,0:T(8,128)(2,1)S(1)} %collective-permute-done.18.refs_0_), channel_id=1, source_target_pairs={{0,16},{8,24},{16,0},{24,8},{1,17},{9,25},{17,1},{25,9},{2,18},{10... | collective-permute-start | bytes 245768 | tf_op jit(solution)/shard_map/ppermute | solution.py:20
  89.7 3.0 %shard_map.77.refs_7_ = bf16[4,4,80,1024]{3,2,1,0:T(8,128)(2,1)S(1)} custom-call(s32[1]{0:T(128)} %bitcast.12.place_ref, bf16[528,1024]{1,0:T(8,128)(2,1)} %collective-permute-done.22.block_ref), custom_call_target="tpu_custom_call" | custom-call | tf_op jit(solution)/shard_map/pallas_call | solution.py:411
  95.1 1.5 %collective-permute-start.25 = (bf16[4,80,128]{2,1,0:T(8,128)(2,1)S(1)}, bf16[4,80,128]{2,1,0:T(8,128)(2,1)S(1)}, u32[]{:S(2)}, u32[]{:S(2)}) collective-permute-start(bf16[4,80,128]{2,1,0:T(8,128)(2,1)S(1)} %get-tuple-element.64.refs_0_), channel_id=1, source_target_pairs={{0,24},{8,16},{16,8},{24,0},{1,25},{9,17},{17,9},{25,1},{2,26},{10... | collective-permute-start | bytes 245768 | tf_op jit(solution)/shard_map/ppermute | solution.py:20
  98.6 2.3 %collective-permute-done.25.refs_3_ = bf16[4,80,128]{2,1,0:T(8,128)(2,1)S(1)} collective-permute-done((bf16[4,80,128]{2,1,0:T(8,128)(2,1)S(1)}, bf16[4,80,128]{2,1,0:T(8,128)(2,1)S(1)}, u32[]{:S(2)}, u32[]{:S(2)}) %collective-permute-start.25) | collective-permute-done | bytes 81952 | tf_op jit(solution)/shard_map/ppermute | solution.py:20
  103.4 5.0 %collective-permute-done.26 = bf16[2,64,1024]{2,1,0:T(8,128)(2,1)S(1)} collective-permute-done((bf16[2,64,1024]{2,1,0:T(8,128)(2,1)S(1)}, bf16[2,64,1024]{2,1,0:T(8,128)(2,1)S(1)}, u32[]{:S(2)}, u32[]{:S(2)}) %collective-permute-start.26) | collective-permute-done | bytes 262176 | tf_op jit(solution)/shard_map/ppermute | solution.py:20
  (58 shorter events, 22.0 us)
Async XLA Ops:
  0.6 14.5 %collective-permute-start.5 = (bf16[128,1024]{1,0:T(8,128)(2,1)}, bf16[128,1024]{1,0:T(8,128)(2,1)S(1)}, u32[]{:S(2)}, u32[]{:S(2)}) collective-permute-start(bf16[128,1024]{1,0:T(8,128)(2,1)} %bitcast.41), channel_id=1, source_target_pairs={{0,2},{1,3},{2,0},{3,1},{4,6},{5,7},{6,4},{7,5},{8,10},{9,11},{10,... | collective-permute-start | bytes 786440 | tf_op jit(solution)/shard_map/ppermute | solution.py:20
  3.7 21.6 %collective-permute-start.4 = (bf16[128,1024]{1,0:T(8,128)(2,1)}, bf16[128,1024]{1,0:T(8,128)(2,1)S(1)}, u32[]{:S(2)}, u32[]{:S(2)}) collective-permute-start(bf16[128,1024]{1,0:T(8,128)(2,1)} %bitcast.42), channel_id=1, source_target_pairs={{0,4},{1,5},{2,6},{3,7},{4,0},{5,1},{6,2},{7,3},{8,12},{9,13},{10,... | collective-permute-start | bytes 786440 | tf_op jit(solution)/shard_map/ppermute | solution.py:20
  6.3 19.0 %collective-permute-start.3 = (bf16[128,1024]{1,0:T(8,128)(2,1)}, bf16[128,1024]{1,0:T(8,128)(2,1)S(1)}, u32[]{:S(2)}, u32[]{:S(2)}) collective-permute-start(bf16[128,1024]{1,0:T(8,128)(2,1)} %bitcast.43), channel_id=1, source_target_pairs={{0,6},{1,7},{2,4},{3,5},{4,2},{5,3},{6,0},{7,1},{8,14},{9,15},{10,... | collective-permute-start | bytes 786440 | tf_op jit(solution)/shard_map/ppermute | solution.py:20
  6.3 1.2 %copy-start.3 = (bf16[128,4096]{1,0:T(8,128)(2,1)S(1)}, bf16[128,4096]{1,0:T(8,128)(2,1)}, u32[]{:S(2)}) copy-start(bf16[128,4096]{1,0:T(8,128)(2,1)} %cotangent_ref.1) | copy-start | bytes 3145732
  7.5 0.7 copy-start.4
  9.0 17.3 %collective-permute-start = (bf16[144,1024]{1,0:T(8,128)(2,1)S(1)}, bf16[144,1024]{1,0:T(8,128)(2,1)S(1)}, u32[]{:S(2)}, u32[]{:S(2)}) collective-permute-start(bf16[144,1024]{1,0:T(8,128)(2,1)S(1)} %get-tuple-element.35), channel_id=1, source_target_pairs={{0,8},{8,0},{16,24},{24,16},{1,9},{9,1},{17,25},{25,17},{2,10},{10... | collective-permute-start | bytes 884744 | tf_op jit(solution)/shard_map/ppermute | solution.py:20
  10.8 15.6 %collective-permute-start.1 = (bf16[144,1024]{1,0:T(8,128)(2,1)S(1)}, bf16[144,1024]{1,0:T(8,128)(2,1)S(1)}, u32[]{:S(2)}, u32[]{:S(2)}) collective-permute-start(bf16[144,1024]{1,0:T(8,128)(2,1)S(1)} %get-tuple-element.36), channel_id=1, source_target_pairs={{0,16},{8,24},{16,0},{24,8},{1,17},{9,25},{17,1},{25,9},{2,18},{10... | collective-permute-start | bytes 884744 | tf_op jit(solution)/shard_map/ppermute | solution.py:20
  15.1 11.3 %collective-permute-start.2 = (bf16[144,1024]{1,0:T(8,128)(2,1)S(1)}, bf16[144,1024]{1,0:T(8,128)(2,1)S(1)}, u32[]{:S(2)}, u32[]{:S(2)}) collective-permute-start(bf16[144,1024]{1,0:T(8,128)(2,1)S(1)} %get-tuple-element.37), channel_id=1, source_target_pairs={{0,24},{8,16},{16,8},{24,0},{1,25},{9,17},{17,9},{25,1},{2,26},{10... | collective-permute-start | bytes 884744 | tf_op jit(solution)/shard_map/ppermute | solution.py:20
  28.3 2.8 %collective-permute-start.6 = (bf16[528,1024]{1,0:T(8,128)(2,1)S(1)}, bf16[528,1024]{1,0:T(8,128)(2,1)S(1)}, u32[]{:S(2)}, u32[]{:S(2)}) collective-permute-start(bf16[528,1024]{1,0:T(8,128)(2,1)S(1)} %shard_map.69.block_ref), channel_id=1, source_target_pairs={{0,1},{1,0},{2,3},{3,2},{4,5},{5,4},{6,7},{7,6},{8,9},{9,8},{10,11... | collective-permute-start | bytes 3244040 | tf_op jit(solution)/shard_map/ppermute | solution.py:20
  32.8 8.6 %collective-permute-start.9 = (bf16[4,2,80,128]{3,2,1,0:T(8,128)(2,1)S(1)}, bf16[4,2,80,128]{3,2,1,0:T(8,128)(2,1)S(1)}, u32[]{:S(2)}, u32[]{:S(2)}) collective-permute-start(bf16[4,2,80,128]{3,2,1,0:T(8,128)(2,1)S(1)} %get-tuple-element.70), channel_id=1, source_target_pairs={{0,24},{8,16},{16,8},{24,0},{1,25},{9,17},{17,9},{25,1},{2,26},{10... | collective-permute-start | bytes 491528 | tf_op jit(solution)/shard_map/ppermute | solution.py:20
  35.3 8.2 %collective-permute-start.8 = (bf16[4,2,80,128]{3,2,1,0:T(8,128)(2,1)S(1)}, bf16[4,2,80,128]{3,2,1,0:T(8,128)(2,1)S(1)}, u32[]{:S(2)}, u32[]{:S(2)}) collective-permute-start(bf16[4,2,80,128]{3,2,1,0:T(8,128)(2,1)S(1)} %get-tuple-element.71), channel_id=1, source_target_pairs={{0,16},{8,24},{16,0},{24,8},{1,17},{9,25},{17,1},{25,9},{2,18},{10... | collective-permute-start | bytes 491528 | tf_op jit(solution)/shard_map/ppermute | solution.py:20
  35.8 7.8 %collective-permute-start.7 = (bf16[4,2,80,128]{3,2,1,0:T(8,128)(2,1)S(1)}, bf16[4,2,80,128]{3,2,1,0:T(8,128)(2,1)S(1)}, u32[]{:S(2)}, u32[]{:S(2)}) collective-permute-start(bf16[4,2,80,128]{3,2,1,0:T(8,128)(2,1)S(1)} %get-tuple-element.72), channel_id=1, source_target_pairs={{0,8},{8,0},{16,24},{24,16},{1,9},{9,1},{17,25},{25,17},{2,10},{10... | collective-permute-start | bytes 491528 | tf_op jit(solution)/shard_map/ppermute | solution.py:20
  38.1 16.9 %copy-start.2 = (bf16[2,1,640,1536]{3,2,1,0:T(8,128)(2,1)S(1)}, bf16[2,1,640,1536]{3,2,1,0:T(8,128)(2,1)}, u32[]{:S(2)}) copy-start(bf16[2,1,640,1536]{3,2,1,0:T(8,128)(2,1)} %param.8) | copy-start | bytes 11796484
  40.0 1.5 %copy-start = (bf16[4,4,80,1024]{3,2,1,0:T(8,128)(2,1)}, bf16[4,4,80,1024]{3,2,1,0:T(8,128)(2,1)S(1)}, u32[]{:S(2)}) copy-start(bf16[4,4,80,1024]{3,2,1,0:T(8,128)(2,1)S(1)} %shard_map.73.refs_5_) | copy-start | bytes 7864324
  43.7 6.4 %collective-permute-start.12 = (bf16[2,80,128]{2,1,0:T(8,128)(2,1)S(1)}, bf16[2,80,128]{2,1,0:T(8,128)(2,1)S(1)}, u32[]{:S(2)}, u32[]{:S(2)}) collective-permute-start(bf16[2,80,128]{2,1,0:T(8,128)(2,1)S(1)} %get-tuple-element.75), channel_id=1, source_target_pairs={{0,6},{1,7},{2,4},{3,5},{4,2},{5,3},{6,0},{7,1},{8,14},{9,15},{10,... | collective-permute-start | bytes 122888 | tf_op jit(solution)/shard_map/ppermute | solution.py:20
  46.3 6.3 %collective-permute-start.11 = (bf16[2,80,128]{2,1,0:T(8,128)(2,1)S(1)}, bf16[2,80,128]{2,1,0:T(8,128)(2,1)S(1)}, u32[]{:S(2)}, u32[]{:S(2)}) collective-permute-start(bf16[2,80,128]{2,1,0:T(8,128)(2,1)S(1)} %get-tuple-element.76), channel_id=1, source_target_pairs={{0,4},{1,5},{2,6},{3,7},{4,0},{5,1},{6,2},{7,3},{8,12},{9,13},{10,... | collective-permute-start | bytes 122888 | tf_op jit(solution)/shard_map/ppermute | solution.py:20
  50.0 4.0 %collective-permute-start.10 = (bf16[2,80,128]{2,1,0:T(8,128)(2,1)S(1)}, bf16[2,80,128]{2,1,0:T(8,128)(2,1)S(1)}, u32[]{:S(2)}, u32[]{:S(2)}) collective-permute-start(bf16[2,80,128]{2,1,0:T(8,128)(2,1)S(1)} %get-tuple-element.77), channel_id=1, source_target_pairs={{0,2},{1,3},{2,0},{3,1},{4,6},{5,7},{6,4},{7,5},{8,10},{9,11},{10,... | collective-permute-start | bytes 122888 | tf_op jit(solution)/shard_map/ppermute | solution.py:20
  54.0 24.5 %collective-permute-start.17 = (bf16[528,1024]{1,0:T(8,128)(2,1)S(1)}, bf16[528,1024]{1,0:T(8,128)(2,1)}, u32[]{:S(2)}, u32[]{:S(2)}) collective-permute-start(bf16[528,1024]{1,0:T(8,128)(2,1)S(1)} %shard_map.69.block_ref), channel_id=1, source_target_pairs={{0,2},{1,3},{2,0},{3,1},{4,6},{5,7},{6,4},{7,5},{8,10},{9,11},{10,... | collective-permute-start | bytes 3244040 | tf_op jit(solution)/shard_map/ppermute | solution.py:20
  56.4 5.7 %collective-permute-start.15 = (bf16[128,768]{1,0:T(8,128)(2,1)S(1)}, bf16[128,768]{1,0:T(8,128)(2,1)S(1)}, u32[]{:S(2)}, u32[]{:S(2)}) collective-permute-start(bf16[128,768]{1,0:T(8,128)(2,1)S(1)} %convert_element_type.48), channel_id=1, source_target_pairs={{0,16},{8,24},{16,0},{24,8},{1,17},{9,25},{17,1},{25,9},{2,18},{10... | collective-permute-start | bytes 589832 | tf_op jit(solution)/shard_map/ppermute | solution.py:20
  57.9 7.1 %collective-permute-start.13 = (bf16[128,768]{1,0:T(8,128)(2,1)S(1)}, bf16[128,768]{1,0:T(8,128)(2,1)S(1)}, u32[]{:S(2)}, u32[]{:S(2)}) collective-permute-start(bf16[128,768]{1,0:T(8,128)(2,1)S(1)} %convert_element_type.45), channel_id=1, source_target_pairs={{0,8},{8,0},{16,24},{24,16},{1,9},{9,1},{17,25},{25,17},{2,10},{10... | collective-permute-start | bytes 589832 | tf_op jit(solution)/shard_map/ppermute | solution.py:20
  62.2 5.7 %collective-permute-start.16 = (bf16[128,768]{1,0:T(8,128)(2,1)S(1)}, bf16[128,768]{1,0:T(8,128)(2,1)S(1)}, u32[]{:S(2)}, u32[]{:S(2)}) collective-permute-start(bf16[128,768]{1,0:T(8,128)(2,1)S(1)} %get-tuple-element.66), channel_id=1, source_target_pairs={{0,8},{8,0},{16,24},{24,16},{1,9},{9,1},{17,25},{25,17},{2,10},{10... | collective-permute-start | bytes 589832 | tf_op jit(solution)/shard_map/ppermute | solution.py:20
  65.1 5.7 %collective-permute-start.14 = (bf16[128,768]{1,0:T(8,128)(2,1)S(1)}, bf16[128,768]{1,0:T(8,128)(2,1)S(1)}, u32[]{:S(2)}, u32[]{:S(2)}) collective-permute-start(bf16[128,768]{1,0:T(8,128)(2,1)S(1)} %get-tuple-element.68), channel_id=1, source_target_pairs={{0,16},{8,24},{16,0},{24,8},{1,17},{9,25},{17,1},{25,9},{2,18},{10... | collective-permute-start | bytes 589832 | tf_op jit(solution)/shard_map/ppermute | solution.py:20
  78.6 11.2 %collective-permute-start.22 = (bf16[528,1024]{1,0:T(8,128)(2,1)}, bf16[528,1024]{1,0:T(8,128)(2,1)}, u32[]{:S(2)}, u32[]{:S(2)}) collective-permute-start(bf16[528,1024]{1,0:T(8,128)(2,1)} %collective-permute-done.17.block_ref), channel_id=1, source_target_pairs={{0,1},{1,0},{2,3},{3,2},{4,5},{5,4},{6,7},{7,6},{8,9},{9,8},{10,11... | collective-permute-start | bytes 3244040 | tf_op jit(solution)/shard_map/ppermute | solution.py:20
  78.6 7.6 %collective-permute-start.18 = (bf16[4,80,128]{2,1,0:T(8,128)(2,1)S(1)}, bf16[4,80,128]{2,1,0:T(8,128)(2,1)S(1)}, u32[]{:S(2)}, u32[]{:S(2)}) collective-permute-start(bf16[4,80,128]{2,1,0:T(8,128)(2,1)S(1)} %get-tuple-element.73), channel_id=1, source_target_pairs={{0,4},{1,5},{2,6},{3,7},{4,0},{5,1},{6,2},{7,3},{8,12},{9,13},{10,... | collective-permute-start | bytes 245768 | tf_op jit(solution)/shard_map/ppermute | solution.py:20
  83.1 10.4 %copy-start.1 = (bf16[4,4,80,1024]{3,2,1,0:T(8,128)(2,1)S(1)}, bf16[4,4,80,1024]{3,2,1,0:T(8,128)(2,1)}, u32[]{:S(2)}) copy-start(bf16[4,4,80,1024]{3,2,1,0:T(8,128)(2,1)} %copy-done) | copy-start | bytes 7864324
  86.2 6.6 %collective-permute-start.21 = (bf16[4,80,128]{2,1,0:T(8,128)(2,1)S(1)}, bf16[4,80,128]{2,1,0:T(8,128)(2,1)S(1)}, u32[]{:S(2)}, u32[]{:S(2)}) collective-permute-start(bf16[4,80,128]{2,1,0:T(8,128)(2,1)S(1)} %collective-permute-done.18.refs_0_), channel_id=1, source_target_pairs={{0,24},{8,16},{16,8},{24,0},{1,25},{9,17},{17,9},{25,1},{2,26},{10... | collective-permute-start | bytes 245768 | tf_op jit(solution)/shard_map/ppermute | solution.py:20
  86.7 6.2 %collective-permute-start.20 = (bf16[4,80,128]{2,1,0:T(8,128)(2,1)S(1)}, bf16[4,80,128]{2,1,0:T(8,128)(2,1)S(1)}, u32[]{:S(2)}, u32[]{:S(2)}) collective-permute-start(bf16[4,80,128]{2,1,0:T(8,128)(2,1)S(1)} %collective-permute-done.18.refs_0_), channel_id=1, source_target_pairs={{0,16},{8,24},{16,0},{24,8},{1,17},{9,25},{17,1},{25,9},{2,18},{10... | collective-permute-start | bytes 245768 | tf_op jit(solution)/shard_map/ppermute | solution.py:20
  89.1 4.4 %collective-permute-start.19 = (bf16[4,80,128]{2,1,0:T(8,128)(2,1)S(1)}, bf16[4,80,128]{2,1,0:T(8,128)(2,1)S(1)}, u32[]{:S(2)}, u32[]{:S(2)}) collective-permute-start(bf16[4,80,128]{2,1,0:T(8,128)(2,1)S(1)} %collective-permute-done.18.refs_0_), channel_id=1, source_target_pairs={{0,8},{8,0},{16,24},{24,16},{1,9},{9,1},{17,25},{25,17},{2,10},{10... | collective-permute-start | bytes 245768 | tf_op jit(solution)/shard_map/ppermute | solution.py:20
  95.0 13.4 %collective-permute-start.26 = (bf16[2,64,1024]{2,1,0:T(8,128)(2,1)S(1)}, bf16[2,64,1024]{2,1,0:T(8,128)(2,1)S(1)}, u32[]{:S(2)}, u32[]{:S(2)}) collective-permute-start(bf16[2,64,1024]{2,1,0:T(8,128)(2,1)S(1)} %shard_map.78), channel_id=1, source_target_pairs={{0,4},{1,5},{2,6},{3,7},{4,0},{5,1},{6,2},{7,3},{8,12},{9,13},{10,... | collective-permute-start | bytes 786440 | tf_op jit(solution)/shard_map/ppermute | solution.py:20
  95.1 5.8 %collective-permute-start.25 = (bf16[4,80,128]{2,1,0:T(8,128)(2,1)S(1)}, bf16[4,80,128]{2,1,0:T(8,128)(2,1)S(1)}, u32[]{:S(2)}, u32[]{:S(2)}) collective-permute-start(bf16[4,80,128]{2,1,0:T(8,128)(2,1)S(1)} %get-tuple-element.64.refs_0_), channel_id=1, source_target_pairs={{0,24},{8,16},{16,8},{24,0},{1,25},{9,17},{17,9},{25,1},{2,26},{10... | collective-permute-start | bytes 245768 | tf_op jit(solution)/shard_map/ppermute | solution.py:20
  96.6 5.0 %collective-permute-start.24 = (bf16[4,80,128]{2,1,0:T(8,128)(2,1)S(1)}, bf16[4,80,128]{2,1,0:T(8,128)(2,1)S(1)}, u32[]{:S(2)}, u32[]{:S(2)}) collective-permute-start(bf16[4,80,128]{2,1,0:T(8,128)(2,1)S(1)} %get-tuple-element.64.refs_0_), channel_id=1, source_target_pairs={{0,16},{8,24},{16,0},{24,8},{1,17},{9,25},{17,1},{25,9},{2,18},{10... | collective-permute-start | bytes 245768 | tf_op jit(solution)/shard_map/ppermute | solution.py:20
  97.5 4.4 %collective-permute-start.23 = (bf16[4,80,128]{2,1,0:T(8,128)(2,1)S(1)}, bf16[4,80,128]{2,1,0:T(8,128)(2,1)S(1)}, u32[]{:S(2)}, u32[]{:S(2)}) collective-permute-start(bf16[4,80,128]{2,1,0:T(8,128)(2,1)S(1)} %get-tuple-element.64.refs_0_), channel_id=1, source_target_pairs={{0,8},{8,0},{16,24},{24,16},{1,9},{9,1},{17,25},{25,17},{2,10},{10... | collective-permute-start | bytes 245768 | tf_op jit(solution)/shard_map/ppermute | solution.py:20
  (1 other events, 0.7 us)
